TPU v7x, 32 devices: a whole 2x2x4 slice. The times are simulated.
32 devices in a mesh: section: 2 (over core), dp: 4 (over y, x), tensor: 4 (over z).
Axes of the slice: x: 2, y: 2, z: 4, core: 2. Of those that a mesh axis runs over, the one named last changes fastest.
Arguments:
- hidden_in: bfloat16 [8, 1024, 768], P('dp'), may hold values from -6 to 6
- target: bfloat16 [8, 1024, 768], P('dp'), may hold values from -6 to 6
- tissue: int32 [8], P('dp'), may hold values from 0 to 15
- ln1_gain: bfloat16 [2, 768], P('section'), may hold values from 0.5 to 1.5
- ln1_bias: bfloat16 [2, 768], P('section'), may hold values from -1.75 to 1.75
- ln2_gain: bfloat16 [2, 768], P('section'), may hold values from 0.5 to 1.5
- ln2_bias: bfloat16 [2, 768], P('section'), may hold values from -1.75 to 1.75
- qkv_weight: bfloat16 [2, 768, 2304], P('section', None, 'tensor'), may hold values from -0.21875 to 0.21875
- qkv_bias: bfloat16 [2, 2304], P('section', 'tensor'), may hold values from -1.75 to 1.75
- dense_weight: bfloat16 [2, 768, 768], P('section', 'tensor'), may hold values from -1 to 1
- dense_bias: bfloat16 [2, 768], P('section'), may hold values from -1.75 to 1.75
- fc1_weight: bfloat16 [2, 768, 3072], P('section', None, 'tensor'), may hold values from -0.21875 to 0.21875
- fc1_bias: bfloat16 [2, 3072], P('section', 'tensor'), may hold values from -1.75 to 1.75
- fc2_weight: bfloat16 [2, 3072, 768], P('section', 'tensor'), may hold values from -0.21875 to 0.21875
- fc2_bias: bfloat16 [2, 768], P('section'), may hold values from -1.75 to 1.75
Outputs:
- block_out: bfloat16 [2, 8, 1024, 768], P('section', 'dp', None, 'tensor')
- input_grad: float32 [2, 8, 1024, 768], P('section', 'dp', None, 'tensor')
- ln1_gain_grad: float32 [2, 768], P('section')
- ln1_bias_grad: float32 [2, 768], P('section')
- ln2_gain_grad: float32 [2, 768], P('section')
- ln2_bias_grad: float32 [2, 768], P('section')
- qkv_weight_grad: float32 [2, 768, 2304], P('section', None, 'tensor')
- qkv_bias_grad: float32 [2, 2304], P('section', 'tensor')
- dense_weight_grad: float32 [2, 768, 768], P('section', 'tensor')
- dense_bias_grad: float32 [2, 768], P('section')
- fc1_weight_grad: float32 [2, 768, 3072], P('section', None, 'tensor')
- fc1_bias_grad: float32 [2, 3072], P('section', 'tensor')
- fc2_weight_grad: float32 [2, 3072, 768], P('section', 'tensor')
- fc2_bias_grad: float32 [2, 768], P('section')
All inputs are finite; a program needn't handle non-finite values.
Results may differ from a plain program's by a relative error of at most 0.012.
Values may be sent and summed in bfloat16 or wider, within the bound.
A program may use at most 192 MiB of HBM per device.

v0:
```python
import jax
import jax.numpy as jnp
from jax import lax
from jax.sharding import PartitionSpec as P

HEAD = 64
ROT = 16
TISSUES = 16


def shifted(block, axis, distance):
    devices = range(lax.axis_size(axis))
    route = [(i - distance, i) for i in devices if i - distance in devices]
    return lax.ppermute(block, axis, route)


def layer_norm(value, gain, bias):
    center = value - jnp.mean(value, axis=-1, keepdims=True)
    spread = jnp.mean(center * center, axis=-1, keepdims=True)
    return center * lax.rsqrt(spread + 1e-05) * gain + bias


def rotary_tables(seq_len):
    half = ROT // 2
    positions = jnp.arange(seq_len).astype(jnp.float32)
    inverse = jnp.power(10000.0, -2.0 * jnp.arange(half).astype(jnp.float32) / ROT)
    angles = positions[:, None] * inverse[None, :]
    cosines = jnp.concatenate([jnp.cos(angles), jnp.cos(angles)], axis=1)[:, None, :]
    sines = jnp.concatenate([jnp.sin(angles), jnp.sin(angles)], axis=1)[:, None, :]
    return (cosines, sines)


def rotate(heads_in, cosines, sines):
    half = ROT // 2
    turning = heads_in[..., :ROT]
    turned = jnp.concatenate([-turning[..., half:], turning[..., :half]], axis=-1)
    return jnp.concatenate([turning * cosines + turned * sines, heads_in[..., ROT:]], axis=-1)


def rotate_back(grad_in, cosines, sines):
    half = ROT // 2
    turning = grad_in[..., :ROT]
    sine_part = turning * sines
    back_turn = jnp.concatenate([sine_part[..., half:], -sine_part[..., :half]], axis=-1)
    return jnp.concatenate([turning * cosines + back_turn, grad_in[..., ROT:]], axis=-1)


def smooth_gate(value):
    return jax.nn.gelu(value, approximate=False)


def outer_sum(left, right):
    return lax.dot_general(
        left, right, (((0,), (0,)), ((), ())), preferred_element_type=jnp.float32
    )


def against(left, right):
    return lax.dot_general(
        left, right, (((1,), (1,)), ((), ())), preferred_element_type=jnp.float32
    )


def causal_mask(offset, block_rows, seq_len):
    return (offset + jnp.arange(block_rows))[:, None] >= jnp.arange(seq_len)[None, :]


def attend(query_low, key_low, value_low, block_rows):
    seq_len = key_low.shape[0]
    factor = HEAD ** (-0.5)
    contexts = []
    log_parts = []
    for offset in range(0, seq_len, block_rows):
        query_block = query_low[offset : offset + block_rows]
        scores = (
            jnp.einsum("qhd,khd->hqk", query_block, key_low, preferred_element_type=jnp.float32)
            * factor
        )
        scores = jnp.where(causal_mask(offset, block_rows, seq_len)[None], scores, -1e30)
        highest = jnp.max(scores, axis=-1, keepdims=True)
        raised = jnp.exp(scores - highest)
        row_total = jnp.sum(raised, axis=-1, keepdims=True)
        probs_low = (raised / row_total).astype(jnp.bfloat16)
        contexts.append(
            jnp.einsum("hqk,khd->qhd", probs_low, value_low, preferred_element_type=jnp.float32)
        )
        log_parts.append((highest + jnp.log(row_total))[..., 0])
    return (jnp.concatenate(contexts, axis=0), jnp.concatenate(log_parts, axis=1))


def attend_back(query_low, key_low, value_low, log_totals, context_grad, block_rows):
    seq_len = key_low.shape[0]
    factor = HEAD ** (-0.5)
    key_grad = jnp.zeros(key_low.shape, jnp.float32)
    value_grad = jnp.zeros(value_low.shape, jnp.float32)
    query_parts = []
    for offset in range(0, seq_len, block_rows):
        query_block = query_low[offset : offset + block_rows]
        grad_block = context_grad[offset : offset + block_rows]
        scores = (
            jnp.einsum("qhd,khd->hqk", query_block, key_low, preferred_element_type=jnp.float32)
            * factor
        )
        scores = jnp.where(causal_mask(offset, block_rows, seq_len)[None], scores, -1e30)
        probs = jnp.exp(scores - log_totals[:, offset : offset + block_rows, None])
        probs_low = probs.astype(jnp.bfloat16)
        prob_grad = jnp.einsum(
            "qhd,khd->hqk", grad_block, value_low, preferred_element_type=jnp.float32
        )
        row_dot = jnp.sum(probs * prob_grad, axis=-1, keepdims=True)
        score_grad = (probs * (prob_grad - row_dot)).astype(jnp.bfloat16)
        query_parts.append(
            jnp.einsum("hqk,khd->qhd", score_grad, key_low, preferred_element_type=jnp.float32)
            * factor
        )
        key_grad = (
            key_grad
            + jnp.einsum(
                "hqk,qhd->khd", score_grad, query_block, preferred_element_type=jnp.float32
            )
            * factor
        )
        value_grad = value_grad + jnp.einsum(
            "hqk,qhd->khd", probs_low, grad_block, preferred_element_type=jnp.float32
        )
    return (jnp.concatenate(query_parts, axis=0), key_grad, value_grad)


def recompute(block_in, params, tables, block_rows):
    seq_len = block_in.shape[0]
    full_in = block_in.astype(jnp.float32)
    first_low = layer_norm(full_in, params[0], params[1]).astype(jnp.bfloat16)
    second_low = layer_norm(full_in, params[2], params[3]).astype(jnp.bfloat16)
    projected = (
        jnp.dot(first_low, params[4], preferred_element_type=jnp.float32) + params[5]
    ).reshape(seq_len, -1, 3, HEAD)
    cosines, sines = tables
    query_low = rotate(projected[:, :, 0], cosines, sines).astype(jnp.bfloat16)
    key_low = rotate(projected[:, :, 1], cosines, sines).astype(jnp.bfloat16)
    value_low = projected[:, :, 2].astype(jnp.bfloat16)
    context, log_totals = attend(query_low, key_low, value_low, block_rows)
    context_low = context.reshape(seq_len, -1).astype(jnp.bfloat16)
    pre_act = jnp.dot(second_low, params[8], preferred_element_type=jnp.float32) + params[9]
    activated_low = smooth_gate(pre_act).astype(jnp.bfloat16)
    return (
        full_in,
        first_low,
        second_low,
        query_low,
        key_low,
        value_low,
        log_totals,
        context_low,
        pre_act,
        activated_low,
    )


def block_backward(block_in, cotangent, params, tables, block_rows):
    (
        full_in,
        first_low,
        second_low,
        query_low,
        key_low,
        value_low,
        log_totals,
        context_low,
        pre_act,
        activated_low,
    ) = recompute(block_in, params, tables, block_rows)
    seq_len = block_in.shape[0]
    grad_low = cotangent.astype(jnp.bfloat16)
    bias_grad = jnp.sum(grad_low.astype(jnp.float32), axis=0)
    dense_grad = outer_sum(context_low, grad_low)
    context_grad = against(grad_low, params[6]).astype(jnp.bfloat16).reshape(seq_len, -1, HEAD)
    query_grad, key_grad, value_grad = attend_back(
        query_low, key_low, value_low, log_totals, context_grad, block_rows
    )
    cosines, sines = tables
    qkv_grad = jnp.stack(
        [
            rotate_back(query_grad, cosines, sines),
            rotate_back(key_grad, cosines, sines),
            value_grad,
        ],
        axis=2,
    )
    qkv_grad = qkv_grad.reshape(seq_len, -1).astype(jnp.bfloat16)
    qkv_shift_grad = jnp.sum(qkv_grad.astype(jnp.float32), axis=0)
    qkv_mat_grad = outer_sum(first_low, qkv_grad)
    first_back = against(qkv_grad, params[4])
    hidden_grad = against(grad_low, params[10])
    _, gate_back = jax.vjp(smooth_gate, pre_act)
    pre_grad = gate_back(hidden_grad)[0].astype(jnp.bfloat16)
    fc1_mat_grad = outer_sum(second_low, pre_grad)
    fc1_shift_grad = jnp.sum(pre_grad.astype(jnp.float32), axis=0)
    fc2_mat_grad = outer_sum(activated_low, grad_low)
    second_back = against(pre_grad, params[8])
    first_back, second_back = lax.psum((first_back, second_back), "tensor")
    _, norm_one = jax.vjp(layer_norm, full_in, params[0], params[1])
    input_one, gain_one, shift_one = norm_one(first_back)
    _, norm_two = jax.vjp(layer_norm, full_in, params[2], params[3])
    input_two, gain_two, shift_two = norm_two(second_back)
    entry_grad = cotangent + input_one + input_two
    gradients = (
        gain_one,
        shift_one,
        gain_two,
        shift_two,
        qkv_mat_grad,
        qkv_shift_grad,
        dense_grad,
        bias_grad,
        fc1_mat_grad,
        fc1_shift_grad,
        fc2_mat_grad,
        bias_grad,
    )
    return (entry_grad, gradients)


def per_device(
    hidden_in,
    target,
    tissue,
    ln1_gain,
    ln1_bias,
    ln2_gain,
    ln2_bias,
    qkv_weight,
    qkv_bias,
    dense_weight,
    dense_bias,
    fc1_weight,
    fc1_bias,
    fc2_weight,
    fc2_bias,
):
    micro_count, seq_len, model_width = hidden_in.shape
    block_rows = min(512, seq_len)
    section_index = lax.axis_index("section")
    is_first = section_index == 0
    tables = rotary_tables(seq_len)
    params = (
        ln1_gain[0].astype(jnp.float32),
        ln1_bias[0].astype(jnp.float32),
        ln2_gain[0].astype(jnp.float32),
        ln2_bias[0].astype(jnp.float32),
        qkv_weight[0],
        qkv_bias[0].astype(jnp.float32),
        dense_weight[0],
        dense_bias[0].astype(jnp.float32),
        fc1_weight[0],
        fc1_bias[0].astype(jnp.float32),
        fc2_weight[0],
        fc2_bias[0].astype(jnp.float32),
    )
    labels = (tissue[:, None] == jnp.arange(TISSUES)[None, :]).astype(jnp.float32)
    counts = lax.psum(jnp.sum(labels, axis=0), "dp")
    own_count = jnp.sum(labels * counts[None, :], axis=1)
    share = micro_count * lax.axis_size("dp") / TISSUES / own_count

    def forward_turn(received, turn_index):
        own_block = lax.dynamic_index_in_dim(
            hidden_in, jnp.clip(turn_index, 0, micro_count - 1), 0, keepdims=False
        )
        block_in = jnp.where(is_first, own_block, received)
        pieces = recompute(block_in, params, tables, block_rows)
        partial_value = jnp.dot(pieces[7], params[6], preferred_element_type=jnp.float32) + jnp.dot(
            pieces[9], params[10], preferred_element_type=jnp.float32
        )
        summed = lax.psum(partial_value, "tensor")
        result = (pieces[0] + summed + params[7] + params[11]).astype(jnp.bfloat16)
        passed = shifted(result, "section", 1)
        return (passed, (block_in, result))

    turns = jnp.arange(micro_count + 1)
    start_value = jnp.zeros((seq_len, model_width), jnp.bfloat16)
    _, (inputs_all, outputs_all) = lax.scan(forward_turn, start_value, turns)
    kept_in = lax.dynamic_slice_in_dim(inputs_all, section_index, micro_count, 0)
    kept_out = lax.dynamic_slice_in_dim(outputs_all, section_index, micro_count, 0)
    lag = 1 - section_index
    zero_grads = tuple((jnp.zeros(item.shape, jnp.float32) for item in params))

    def backward_turn(carry, turn_index):
        received, totals = carry
        micro_index = turn_index - lag
        is_valid = jnp.logical_and(micro_index >= 0, micro_index < micro_count)
        safe_index = jnp.clip(micro_index, 0, micro_count - 1)
        block_in = lax.dynamic_index_in_dim(kept_in, safe_index, 0, keepdims=False)
        goal = lax.dynamic_index_in_dim(target, safe_index, 0, keepdims=False).astype(jnp.float32)
        weight = lax.dynamic_index_in_dim(share, safe_index, 0, keepdims=False)
        cotangent = jnp.where(is_first, received.astype(jnp.float32), weight * goal)
        entry_grad, gradients = block_backward(block_in, cotangent, params, tables, block_rows)
        passed = shifted(entry_grad.astype(jnp.bfloat16), "section", -1)
        valid_weight = is_valid.astype(jnp.float32)
        gradients = tuple((item * valid_weight for item in gradients))
        totals = tuple((a + b for a, b in zip(totals, gradients)))
        return ((passed, totals), entry_grad)

    (_, totals), entry_all = lax.scan(backward_turn, (start_value, zero_grads), turns)
    totals = lax.psum(
        (
            totals[0],
            totals[1],
            totals[2],
            totals[3],
            totals[4],
            totals[5],
            totals[6],
            totals[7],
            totals[8],
            totals[9],
            totals[10],
            totals[11],
        ),
        "dp",
    )
    kept_grad = lax.dynamic_slice_in_dim(entry_all, lag, micro_count, 0)
    columns = model_width // lax.axis_size("tensor")
    column_start = lax.axis_index("tensor") * columns
    block_out = lax.dynamic_slice_in_dim(kept_out, column_start, columns, 2)[None]
    input_grad = lax.dynamic_slice_in_dim(kept_grad, column_start, columns, 2)[None]
    return (
        block_out,
        input_grad,
        totals[0][None],
        totals[1][None],
        totals[2][None],
        totals[3][None],
        totals[4][None],
        totals[5][None],
        totals[6][None],
        totals[7][None],
        totals[8][None],
        totals[9][None],
        totals[10][None],
        totals[11][None],
    )


def solution(mesh):
    return jax.shard_map(
        per_device,
        mesh=mesh,
        in_specs=(
            P("dp", None, None),
            P("dp", None, None),
            P("dp"),
            P("section", None),
            P("section", None),
            P("section", None),
            P("section", None),
            P("section", None, "tensor"),
            P("section", "tensor"),
            P("section", "tensor", None),
            P("section", None),
            P("section", None, "tensor"),
            P("section", "tensor"),
            P("section", "tensor", None),
            P("section", None),
        ),
        out_specs=(
            P("section", "dp", None, "tensor"),
            P("section", "dp", None, "tensor"),
            P("section", None),
            P("section", None),
            P("section", None),
            P("section", None),
            P("section", None, "tensor"),
            P("section", "tensor"),
            P("section", "tensor", None),
            P("section", None),
            P("section", None, "tensor"),
            P("section", "tensor"),
            P("section", "tensor", None),
            P("section", None),
        ),
        check_vma=False,
    )
```

profile of v0, /device:TPU:0, one launch (start us, length us, event | category | flops | bytes accessed | tf_op | source)
XLA Modules:
  0.0 1640.2 jit_solution(15391513372937711462)
XLA Ops:
  8.9 11.3 psum.112
  27.8 528.7 %while.51 = (s32[]{:T(128)}, bf16[1024,768]{1,0:T(8,128)(2,1)S(1)}, bf16[3,1024,768]{2,1,0:T(8,128)(2,1)}, bf16[3,1024,768]{2,1,0:T(8,128)(2,1)}, pred[]{:T(512)...) while((s32[]{:T(128)}, bf16[1024,768]{1,0:T(8,128)(2,1)S(1)}, ...), condition=%wide.region_8.9_spmd, body=%wide.region_0.8_spmd.sunk | while | flops 4525936128 | bytes 144213776 | solution.py:280
  58.1 12.2 fusion.352
  74.6 120.6 %all-reduce.11.cloned.1.call-done = f32[1024,768]{1,0:T(8,128)} async-done(((f32[1024,768]{1,0:T(8,128)}), f32[1024,768]{1,0:T(8,128)}) %all-reduce.11.cloned.1.call-update) | async-done | bytes 3145744 | tf_op jit(solution)/shard_map/while/body/eval_jaxpr/psum | solution.py:273
  215.3 6.0 fusion.357
  234.4 12.2 fusion.352
  250.9 120.4 %all-reduce.11.cloned.1.call-done = f32[1024,768]{1,0:T(8,128)} async-done(((f32[1024,768]{1,0:T(8,128)}), f32[1024,768]{1,0:T(8,128)}) %all-reduce.11.cloned.1.call-update) | async-done | bytes 3145744 | tf_op jit(solution)/shard_map/while/body/eval_jaxpr/psum | solution.py:273
  410.6 12.2 fusion.352
  427.1 120.4 %all-reduce.11.cloned.1.call-done = f32[1024,768]{1,0:T(8,128)} async-done(((f32[1024,768]{1,0:T(8,128)}), f32[1024,768]{1,0:T(8,128)}) %all-reduce.11.cloned.1.call-update) | async-done | bytes 3145744 | tf_op jit(solution)/shard_map/while/body/eval_jaxpr/psum | solution.py:273
  560.0 906.2 %while.52 = (s32[]{:T(128)}, bf16[1024,768]{1,0:T(8,128)(2,1)}, f32[768]{0:T(1024)S(1)}, f32[768]{0:T(1024)S(1)}, f32[768]{0:T(1024)S(1)}, /*index=5*/f32[768]{0...) while((s32[]{:T(128)}, bf16[1024,768]{1,0:T(8,128)(2,1)}, ...), condition=%wide.region_34.35_spmd.clone, body=%wide.region_12.34_spmd.clone.sunk | while | flops 11983092736 | bytes 526847200 | solution.py:302
  611.0 9.7 convert_reduce_fusion.22
  649.1 206.2 %all-reduce.13.cloned.1.call-done = (f32[1024,768]{1,0:T(8,128)}, f32[1024,768]{1,0:T(8,128)}) async-done(((f32[1024,768]{1,0:T(8,128)}, f32[1024,768]{1,0:T(8,128)}), (f32[1024,768]{1,0:T(8,128)}, f32[1024,768]{1,0:T(8,128)})) %all-reduce.13.cloned.1.call-update) | async-done | bytes 6291472 | tf_op jit(solution)/shard_map/while/body/eval_jaxpr/psum | solution.py:200
  862.9 6.0 bitcast_dynamic-update-slice_fusion.8
  870.2 6.1 select_add_fusion.30
  903.5 9.7 convert_reduce_fusion.22
  943.3 206.2 %all-reduce.13.cloned.1.call-done = (f32[1024,768]{1,0:T(8,128)}, f32[1024,768]{1,0:T(8,128)}) async-done(((f32[1024,768]{1,0:T(8,128)}, f32[1024,768]{1,0:T(8,128)}), (f32[1024,768]{1,0:T(8,128)}, f32[1024,768]{1,0:T(8,128)})) %all-reduce.13.cloned.1.call-update) | async-done | bytes 6291472 | tf_op jit(solution)/shard_map/while/body/eval_jaxpr/psum | solution.py:200
  1157.1 6.0 bitcast_dynamic-update-slice_fusion.8
  1164.4 6.9 select_add_fusion.30
  1198.4 9.7 convert_reduce_fusion.22
  1238.2 206.3 %all-reduce.13.cloned.1.call-done = (f32[1024,768]{1,0:T(8,128)}, f32[1024,768]{1,0:T(8,128)}) async-done(((f32[1024,768]{1,0:T(8,128)}, f32[1024,768]{1,0:T(8,128)}), (f32[1024,768]{1,0:T(8,128)}, f32[1024,768]{1,0:T(8,128)})) %all-reduce.13.cloned.1.call-update) | async-done | bytes 6291472 | tf_op jit(solution)/shard_map/while/body/eval_jaxpr/psum | solution.py:200
  1452.0 6.0 bitcast_dynamic-update-slice_fusion.8
  1459.3 6.9 select_add_fusion.30
  1474.2 17.5 %all-reduce.1 = (f32[1,768]{1,0:T(1,128)}, f32[1,768]{1,0:T(1,128)}, f32[1,768]{1,0:T(1,128)}, f32[1,768]{1,0:T(1,128)}, f32[1,576]{1,0:T(1,128)}, /*index=5*/f3...) all-reduce(f32[1,768]{1,0:T(1,128)S(1)} %broadcast_in_dim.196, ...), channel_id=1, replica_groups=mesh['section'=2,'dp'=4,'tensor'=4] {'dp'}, use_global_device_ids=true, to_apply=%region_35.36 | all-reduce | flops 5952 | bytes 47616 | tf_op jit(solution)/shard_map/psum | solution.py:303
  1491.8 133.4 %all-reduce.9.cloned.1.call-done = (f32[1,768,576]{1,2,0:T(8,128)}, f32[1,192,768]{2,1,0:T(8,128)}, f32[1,768,768]{2,1,0:T(8,128)}, f32[1,768,768]{2,1,0:T(8,128)}) async-done(((f32[1,768,576]{1,2,0:T(8,128)}, f32[1,192,768]{2,1,0:T(8,128)}, f32[1,768,768]{2,1,0:T(8,128)}, f32[1,768,768]{2,1,0:T(8,128)}), (f32[1,768,576]{1,2,0:T(8,128)}, f32[1,192,768]{2,1,0:T(8,128)}, f32[1,768,768]{2,1,0:T(8,128)}, ...) | async-done | bytes 7077904 | tf_op jit(solution)/shard_map/psum | solution.py:303
  (572 shorter events, 340.9 us)
Async XLA Ops:
  27.8 167.4 %all-reduce.11.cloned.1.call-start = ((), (), s32[]{:S(2)}) async-start(), calls=%async_computation.1 | async-start | bytes 6291456 | tf_op jit(solution)/shard_map/while/body/eval_jaxpr/psum | solution.py:273
  199.3 4.9 collective-permute-start
  204.2 167.1 %all-reduce.11.cloned.1.call-start = ((), (), s32[]{:S(2)}) async-start(), calls=%async_computation.1 | async-start | bytes 6291456 | tf_op jit(solution)/shard_map/while/body/eval_jaxpr/psum | solution.py:273
  375.4 4.9 collective-permute-start
  380.3 167.2 %all-reduce.11.cloned.1.call-start = ((), (), s32[]{:S(2)}) async-start(), calls=%async_computation.1 | async-start | bytes 6291456 | tf_op jit(solution)/shard_map/while/body/eval_jaxpr/psum | solution.py:273
  551.6 4.9 collective-permute-start
  584.0 25.3 %copy-start.4 = (bf16[2,1024,768]{2,1,0:T(8,128)(2,1)}, bf16[2,1024,768]{2,1,0:T(8,128)(2,1)S(1)}, u32[]{:S(2)}) copy-start(bf16[2,1024,768]{2,1,0:T(8,128)(2,1)S(1)} %get-tuple-element.1249) | copy-start | bytes 9437188 | tf_op jit(solution)/shard_map/while
  584.0 271.4 %all-reduce.13.cloned.1.call-start = ((), (), s32[]{:S(2)}) async-start(), calls=%async_computation.2 | async-start | bytes 12582912 | tf_op jit(solution)/shard_map/while/body/eval_jaxpr/psum | solution.py:200
  591.1 19.9 %copy-start.6 = (bf16[1024,768]{1,0:T(8,128)(2,1)}, bf16[1024,768]{1,0:T(8,128)(2,1)S(1)}, u32[]{:S(2)}) copy-start(bf16[1024,768]{1,0:T(8,128)(2,1)S(1)} %get-tuple-element.1035) | copy-start | bytes 4718596 | tf_op jit(solution)/shard_map/while
  596.2 27.5 %copy-start = (f32[3,512,1024]{2,1,0:T(8,128)}, f32[3,512,1024]{2,1,0:T(8,128)S(1)}, u32[]{:S(2)}) copy-start(f32[3,512,1024]{2,1,0:T(8,128)S(1)} %get-tuple-element.1049) | copy-start | bytes 18874372 | tf_op jit(solution)/shard_map/while
  604.6 20.3 %copy-start.1 = (f32[3,512,1024]{2,1,0:T(8,128)}, f32[3,512,1024]{2,1,0:T(8,128)S(1)}, u32[]{:S(2)}) copy-start(f32[3,512,1024]{2,1,0:T(8,128)S(1)} %get-tuple-element.1046) | copy-start | bytes 18874372 | tf_op jit(solution)/shard_map/while
  868.9 7.5 collective-permute-start.1
  876.5 25.3 %copy-start.4 = (bf16[2,1024,768]{2,1,0:T(8,128)(2,1)}, bf16[2,1024,768]{2,1,0:T(8,128)(2,1)S(1)}, u32[]{:S(2)}) copy-start(bf16[2,1024,768]{2,1,0:T(8,128)(2,1)S(1)} %get-tuple-element.1249) | copy-start | bytes 9437188 | tf_op jit(solution)/shard_map/while
  876.5 273.1 %all-reduce.13.cloned.1.call-start = ((), (), s32[]{:S(2)}) async-start(), calls=%async_computation.2 | async-start | bytes 12582912 | tf_op jit(solution)/shard_map/while/body/eval_jaxpr/psum | solution.py:200
  883.6 19.9 %copy-start.6 = (bf16[1024,768]{1,0:T(8,128)(2,1)}, bf16[1024,768]{1,0:T(8,128)(2,1)S(1)}, u32[]{:S(2)}) copy-start(bf16[1024,768]{1,0:T(8,128)(2,1)S(1)} %get-tuple-element.1035) | copy-start | bytes 4718596 | tf_op jit(solution)/shard_map/while
  888.7 27.5 %copy-start = (f32[3,512,1024]{2,1,0:T(8,128)}, f32[3,512,1024]{2,1,0:T(8,128)S(1)}, u32[]{:S(2)}) copy-start(f32[3,512,1024]{2,1,0:T(8,128)S(1)} %get-tuple-element.1049) | copy-start | bytes 18874372 | tf_op jit(solution)/shard_map/while
  897.1 20.3 %copy-start.1 = (f32[3,512,1024]{2,1,0:T(8,128)}, f32[3,512,1024]{2,1,0:T(8,128)S(1)}, u32[]{:S(2)}) copy-start(f32[3,512,1024]{2,1,0:T(8,128)S(1)} %get-tuple-element.1046) | copy-start | bytes 18874372 | tf_op jit(solution)/shard_map/while
  1163.1 8.2 collective-permute-start.1
  1171.4 25.3 %copy-start.4 = (bf16[2,1024,768]{2,1,0:T(8,128)(2,1)}, bf16[2,1024,768]{2,1,0:T(8,128)(2,1)S(1)}, u32[]{:S(2)}) copy-start(bf16[2,1024,768]{2,1,0:T(8,128)(2,1)S(1)} %get-tuple-element.1249) | copy-start | bytes 9437188 | tf_op jit(solution)/shard_map/while
  1171.4 273.1 %all-reduce.13.cloned.1.call-start = ((), (), s32[]{:S(2)}) async-start(), calls=%async_computation.2 | async-start | bytes 12582912 | tf_op jit(solution)/shard_map/while/body/eval_jaxpr/psum | solution.py:200
  1183.6 27.5 %copy-start = (f32[3,512,1024]{2,1,0:T(8,128)}, f32[3,512,1024]{2,1,0:T(8,128)S(1)}, u32[]{:S(2)}) copy-start(f32[3,512,1024]{2,1,0:T(8,128)S(1)} %get-tuple-element.1049) | copy-start | bytes 18874372 | tf_op jit(solution)/shard_map/while
  1192.0 20.3 %copy-start.1 = (f32[3,512,1024]{2,1,0:T(8,128)}, f32[3,512,1024]{2,1,0:T(8,128)S(1)}, u32[]{:S(2)}) copy-start(f32[3,512,1024]{2,1,0:T(8,128)S(1)} %get-tuple-element.1046) | copy-start | bytes 18874372 | tf_op jit(solution)/shard_map/while
  1458.0 8.2 collective-permute-start.1
  1466.3 158.9 %all-reduce.9.cloned.1.call-start = ((), (), s32[]{:S(2)}) async-start(), calls=%async_computation | async-start | bytes 14155776 | tf_op jit(solution)/shard_map/psum | solution.py:303
  (97 other events, 396.3 us)
Sparse Core Ops, SparseCore 0:
  74.7 120.4 all-reduce.10
  251.0 120.2 all-reduce.10
  427.2 120.2 all-reduce.10
  632.9 222.3 all-reduce.12
  925.4 224.0 all-reduce.12
  1220.3 224.0 all-reduce.12
Sparse Core Ops, SparseCore 1:
  1471.7 153.4 all-reduce.8
where the time goes:
time: 1660 us; the launch traced here: 1640 us
  waiting for transfers between devices  1120 us (67%)
  matrix products  267 us (16%)
  other arithmetic  109 us (7%)
  local copies, waits for them, and re-layouts  54.4 us (3%)
  loops' own time  30.3 us (2%)
  blocking collectives  28.9 us (2%)
  between operations  16.8 us (1%)
    psum x3, waiting for transfers between devices, block_backward(): first_back, second_back = lax.psum((first_back, second_back), 'tensor')  619 us
    psum x3, waiting for transfers between devices, forward_turn(): summed = lax.psum(partial_value, 'tensor')  361 us
    psum x1, waiting for transfers between devices, per_device(): lax.psum((totals[0], totals[1], totals[2], totals[3], totals[4], totals[5...  133 us
    dot_general x12, matrix products, against(): lax.dot_general(left, right, (((1,), (1,)), ((), ())), preferred_element_...  49.4 us
    dot_general x12, matrix products, attend(): jnp.einsum('hqk,khd->qhd', probs_low, value_low, preferred_element_type=j...  41.2 us
    dot_general x12, matrix products, outer_sum(): lax.dot_general(left, right, (((0,), (0,)), ((), ())), preferred_element_...  40.1 us
    dot_general x3, matrix products, forward_turn(): jnp.dot(pieces[9], params[10], preferred_element_type=jnp.float32)  36.7 us
    sub x6, matrix products, attend(): raised = jnp.exp(scores - highest)  35.9 us
  transfers between devices with their start and end apart: 13, of which 10 were waited for; matrix products, arithmetic and copies ran while one was open for 4% of the time, Pallas kernels for 0%

commit v1 on v0

v1 whole, which is shorter than its diff:
```python
import functools

import jax
import jax.numpy as jnp
import numpy as np
from jax import lax
from jax.experimental import pallas as pl
from jax.experimental.pallas import tpu as pltpu
from jax.sharding import PartitionSpec as P

HEAD = 64
ROT = 16
TISSUES = 16
ROWS = 256
LANES = 128
EPS = 1e-05
MESH = pl.DeviceIdType.MESH
F32 = jnp.float32
BF16 = jnp.bfloat16


def dot_nn(a, b):
    return lax.dot_general(a, b, (((1,), (0,)), ((), ())), preferred_element_type=F32)


def dot_nt(a, b):
    return lax.dot_general(a, b, (((1,), (1,)), ((), ())), preferred_element_type=F32)


def dot_tn(a, b):
    return lax.dot_general(a, b, (((0,), (0,)), ((), ())), preferred_element_type=F32)


def rotary_tables(seq_len):
    half = ROT // 2
    inverse = 10000.0 ** (-2.0 * np.arange(half) / ROT)
    angles = np.arange(seq_len)[:, None] * inverse[None, :]
    cosines = np.ones((seq_len, HEAD))
    left = np.zeros((seq_len, HEAD))
    right = np.zeros((seq_len, HEAD))
    cosines[:, :half] = np.cos(angles)
    cosines[:, half:ROT] = np.cos(angles)
    left[:, :half] = -np.sin(angles)
    right[:, half:ROT] = np.sin(angles)
    tables = np.stack([np.tile(item, (1, LANES // HEAD)) for item in (cosines, left, right)])
    return tables.astype(np.float32)


def pack_columns(weight, lanes):
    lead = weight.shape[:-1]
    heads = weight.shape[-1] // (3 * HEAD)
    split = jnp.moveaxis(weight.reshape(lead + (heads, 3, HEAD)), -2, -3)
    split = split.reshape(lead + (3, heads * HEAD))
    split = jnp.pad(split, [(0, 0)] * (len(lead) + 1) + [(0, lanes - heads * HEAD)])
    return split.reshape(lead + (3 * lanes,))


def unpack_columns(weight, heads):
    lead = weight.shape[:-1]
    split = weight.reshape(lead + (3, -1))[..., : heads * HEAD]
    split = split.reshape(lead + (3, heads, HEAD))
    return jnp.moveaxis(split, -3, -2).reshape(lead + (3 * heads * HEAD,))


def normalise(value):
    center = value - jnp.mean(value, axis=-1, keepdims=True)
    rstd = lax.rsqrt(jnp.mean(center * center, axis=-1, keepdims=True) + EPS)
    return center * rstd, rstd


def train_kernel(
    heads,
    x_in,
    target_in,
    share_in,
    tables,
    wq_in,
    wd_in,
    w1_in,
    w2_in,
    vec_in,
    out_cols,
    grad_cols,
    grads,
    small,
    wq,
    wd,
    w1,
    w2,
    vec,
    chain,
    norm1,
    norm2,
    qkv,
    ctx,
    act,
    gate,
    key_grad,
    value_grad,
    part,
    got,
    met,
    away,
    probs,
    load_sem,
    give_sem,
    take_sem,
    hop_send,
    hop_recv,
    swap_send,
    swap_recv,
):
    section = lax.axis_index("section")
    place = lax.axis_index("tensor")
    chunks, rows, width = part.shape
    lanes = wd.shape[1]
    columns = out_cols.shape[-1]
    inner = jnp.logical_and(place > 0, place < 3)
    outer = jnp.logical_not(inner)
    beside = jnp.where(place == 0, 1, jnp.where(place == 3, 2, jnp.where(place == 1, 0, 3)))
    across = 3 - place

    def at_place(index):
        return {"tensor": index}

    twin = {"section": 1 - section}

    barrier = pltpu.get_barrier_semaphore()
    pl.semaphore_signal(barrier, inc=1, device_id=twin, device_id_type=MESH)
    pl.semaphore_signal(barrier, inc=1, device_id=at_place(beside), device_id_type=MESH)

    @pl.when(inner)
    def _():
        pl.semaphore_signal(barrier, inc=1, device_id=at_place(across), device_id_type=MESH)

    loads = []
    for index, (source, goal) in enumerate(
        ((wq_in, wq), (vec_in, vec), (w1_in, w1), (wd_in, wd), (w2_in, w2))
    ):
        loads.append(pltpu.make_async_copy(source, goal.at[section], load_sem.at[index]))
    input_load = pltpu.make_async_copy(x_in.at[section], chain.at[0], load_sem.at[5])
    target_load = pltpu.make_async_copy(target_in.at[section], chain.at[3], load_sem.at[6])
    input_load.start()
    for item in loads:
        item.start()
    target_load.start()
    pl.semaphore_wait(barrier, jnp.where(inner, 3, 2))
    gifts = []
    for index, (source, goal) in enumerate(
        ((wq_in, wq), (vec_in, vec), (w1_in, w1), (wd_in, wd), (w2_in, w2))
    ):
        gifts.append(
            pltpu.make_async_remote_copy(
                src_ref=source,
                dst_ref=goal.at[section],
                send_sem=give_sem.at[index],
                recv_sem=take_sem.at[index],
                device_id=twin,
                device_id_type=MESH,
            )
        )
    for item in gifts:
        item.start()

    lane = lax.broadcasted_iota(jnp.int32, (1, lanes), 1) // HEAD
    head_masks = [lane == h for h in range(heads)]
    factor = HEAD ** (-0.5)

    def wide(table, start):
        piece = tables[table, start : start + rows, :]
        return jnp.concatenate([piece] * (lanes // LANES), axis=1)

    def turn(value, start):
        ahead = pltpu.roll(value, lanes - ROT // 2, 1)
        behind = pltpu.roll(value, ROT // 2, 1)
        return value * wide(0, start) + ahead * wide(1, start) + behind * wide(2, start)

    def turn_back(value, start):
        ahead = pltpu.roll(value, lanes - ROT // 2, 1)
        behind = pltpu.roll(value, ROT // 2, 1)
        return value * wide(0, start) - ahead * wide(1, start) - behind * wide(2, start)

    def only(mask, value):
        return jnp.where(mask, value, jnp.zeros_like(value))

    def forward_chunk(layer, c):
        start = c * rows
        here = slice(start, start + rows)
        spread, _ = normalise(chain[layer, c].astype(F32))
        first = (spread * vec[layer, 0:1] + vec[layer, 1:2]).astype(BF16)
        second = (spread * vec[layer, 2:3] + vec[layer, 3:4]).astype(BF16)
        projected = dot_nn(first, wq[layer]) + vec[layer, 5:6]
        query = turn(projected[:, :lanes], start).astype(BF16)
        qkv[layer, here, :lanes] = query
        qkv[layer, here, lanes : 2 * lanes] = turn(projected[:, lanes : 2 * lanes], start).astype(
            BF16
        )
        qkv[layer, here, 2 * lanes :] = projected[:, 2 * lanes :].astype(BF16)
        pre = dot_nn(second, w1[layer]) + vec[layer, 6:7]
        below = 0.5 * (1.0 + lax.erf(pre * (0.5**0.5)))
        active = (pre * below).astype(BF16)
        act[layer, here, :] = active
        slope = below + pre * (jnp.exp(-0.5 * pre * pre) * ((2.0 * np.pi) ** -0.5))
        gate[layer, here, :] = slope.astype(BF16)
        diagonal = lax.broadcasted_iota(jnp.int32, (rows, rows), 0) >= lax.broadcasted_iota(
            jnp.int32, (rows, rows), 1
        )
        context = jnp.zeros((rows, lanes), F32)
        for h in range(heads):
            asked = only(head_masks[h], query) * jnp.asarray(factor, BF16)
            near = dot_nt(asked, qkv[layer, here, lanes : 2 * lanes])
            near = jnp.where(diagonal, near, -1e30)
            highest = jnp.max(near, axis=-1, keepdims=True)
            if c > 0:
                far = dot_nt(asked, qkv[layer, :start, lanes : 2 * lanes])
                highest = jnp.maximum(highest, jnp.max(far, axis=-1, keepdims=True))
                far = jnp.exp(far - highest)
            near = jnp.exp(near - highest)
            total = jnp.sum(near, axis=-1, keepdims=True)
            if c > 0:
                total = total + jnp.sum(far, axis=-1, keepdims=True)
            inverse = 1.0 / total
            near = (near * inverse).astype(BF16)
            probs[c][layer, h, :, start:] = near
            mixed = dot_nn(near, qkv[layer, here, 2 * lanes :])
            if c > 0:
                far = (far * inverse).astype(BF16)
                probs[c][layer, h, :, :start] = far
                mixed = mixed + dot_nn(far, qkv[layer, :start, 2 * lanes :])
            context = jnp.where(head_masks[h], mixed, context)
        context = context.astype(BF16)
        ctx[layer, here, :] = context
        part[c] = (dot_nn(context, wd[layer]) + dot_nn(active, w2[layer])).astype(BF16)

    def backward_chunk(layer, c):
        start = c * rows
        stop = start + rows
        here = slice(start, stop)
        first_turn = c == chunks - 1
        slot = chunks - 1 - c
        cotangent = chain[4 - layer, c]
        context_grad = dot_nt(cotangent, wd[layer]).astype(BF16)
        pre_grad = (dot_nt(cotangent, w2[layer]) * gate[layer, here, :].astype(F32)).astype(BF16)
        gate[layer, here, :] = pre_grad
        second_back = dot_nt(pre_grad, w1[layer])
        query = qkv[layer, here, :lanes]
        weighed = context_grad.astype(F32) * ctx[layer, here, :].astype(F32)
        query_grad = jnp.zeros((rows, lanes), F32)
        key_sum = None
        value_sum = None
        for h in range(heads):
            mask = head_masks[h]
            own_grad = only(mask, context_grad)
            asked = only(mask, query) * jnp.asarray(factor, BF16)
            row_dot = jnp.sum(only(mask, weighed), axis=-1, keepdims=True)
            prob = probs[c][layer, h]
            prob_grad = dot_nt(own_grad, qkv[layer, :stop, 2 * lanes :])
            score_grad = (prob.astype(F32) * (prob_grad - row_dot)).astype(BF16)
            query_grad = jnp.where(
                mask, dot_nn(score_grad, qkv[layer, :stop, lanes : 2 * lanes]), query_grad
            )
            key_part = dot_tn(score_grad, asked)
            value_part = dot_tn(prob, own_grad)
            key_sum = key_part if key_sum is None else key_sum + key_part
            value_sum = value_part if value_sum is None else value_sum + value_part
        if first_turn:
            key_grad[:stop] = key_sum
            value_grad[:stop] = value_sum
        else:
            key_grad[:stop] += key_sum
            value_grad[:stop] += value_sum
        qkv[layer, here, :lanes] = turn_back(query_grad * factor, start).astype(BF16)
        qkv[layer, here, lanes : 2 * lanes] = turn_back(key_grad[here], start).astype(BF16)
        qkv[layer, here, 2 * lanes :] = value_grad[here].astype(BF16)
        projected_grad = qkv[layer, here, :]
        first_back = dot_nt(projected_grad, wq[layer])
        spread, rstd = normalise(chain[layer, c].astype(F32))
        norm1[here] = (spread * vec[layer, 0:1] + vec[layer, 1:2]).astype(BF16)
        norm2[here] = (spread * vec[layer, 2:3] + vec[layer, 3:4]).astype(BF16)
        sums = (
            first_back * spread,
            first_back,
            second_back * spread,
            second_back,
            projected_grad.astype(F32),
            cotangent.astype(F32),
            pre_grad.astype(F32),
        )
        for index, item in enumerate(sums):
            line = jnp.sum(item, axis=0, keepdims=True)
            if first_turn:
                small[layer, index : index + 1] = line
            else:
                small[layer, index : index + 1] += line
        if first_turn:
            small[layer, len(sums) :] = jnp.zeros((8 - len(sums), width), F32)
        back = first_back * vec[layer, 0:1] + second_back * vec[layer, 2:3]
        middle = jnp.mean(back, axis=-1, keepdims=True)
        tilt = jnp.mean(back * spread, axis=-1, keepdims=True)
        part[slot] = (rstd * (back - middle - spread * tilt)).astype(BF16)

    def weight_grads(layer):
        cotangent = chain[4 - layer].reshape(chunks * rows, width)
        step = 256
        base = 0
        for left, right in (
            (norm1, qkv.at[layer]),
            (norm2, gate.at[layer]),
            (act.at[layer], None),
            (ctx.at[layer], None),
        ):
            size = left.shape[-1]
            for at in range(0, size, step):
                grads[layer, base + at : base + at + step] = dot_tn(
                    left[:, at : at + step], cotangent if right is None else right[...]
                ).astype(BF16)
            base += size

    def locate(turn_index):
        kind = turn_index // chunks
        slot = lax.rem(turn_index, chunks)
        row = jnp.where(kind < 2, slot, chunks - 1 - slot)
        base = kind + jnp.where(kind < 2, 0, 1)
        return kind, slot, row, base

    def hop(stage, slot, source, goal, target):
        return pltpu.make_async_remote_copy(
            src_ref=source,
            dst_ref=goal,
            send_sem=hop_send.at[stage, slot],
            recv_sem=hop_recv.at[stage, slot],
            device_id=at_place(target),
            device_id_type=MESH,
        )

    def first_hop(slot):
        return hop(0, slot, part.at[slot], got.at[slot], beside)

    def second_hop(slot):
        return hop(1, slot, part.at[slot], met.at[slot], across)

    def third_hop(slot, row, base):
        piece = chain.at[base + 1, row]
        return hop(2, slot, piece, piece, beside)

    def launch(turn_index):
        _, slot, _, _ = locate(turn_index)

        @pl.when(outer)
        def _():
            first_hop(slot).start()

    def meet(turn_index):
        _, slot, _, _ = locate(turn_index)

        @pl.when(inner)
        def _():
            first_hop(slot).wait_recv()
            part[slot] = (part[slot].astype(F32) + got[slot].astype(F32)).astype(BF16)
            second_hop(slot).start()

    def settle(turn_index):
        kind, slot, row, base = locate(turn_index)

        @pl.when(inner)
        def _():
            second_hop(slot).wait_recv()
            keep = jnp.where(kind < 2, 1.0, 0.0)
            shift = vec[jnp.minimum(kind, 1), 4:5] * keep
            total = part[slot].astype(F32) + met[slot].astype(F32)
            chain[base + 1, row] = (chain[base, row].astype(F32) + (total + shift)).astype(BF16)
            third_hop(slot, row, base).start()

    def finish(turn_index):
        _, slot, row, base = locate(turn_index)

        @pl.when(outer)
        def _():
            first_hop(slot).wait_send()
            third_hop(slot, row, base).wait_recv()

        @pl.when(inner)
        def _():
            second_hop(slot).wait_send()
            third_hop(slot, row, base).wait_send()

    def need(index, layer):
        @pl.when(section == layer)
        def _():
            loads[index].wait()

        @pl.when(section != layer)
        def _():
            gifts[index].wait_recv()

    input_load.wait()

    def forward_layer(layer, carry):
        for index in range(len(loads)):
            need(index, layer)
        for c in range(chunks):
            now = layer * chunks + c

            @pl.when(layer > 0)
            def _():
                finish(now - chunks)

            forward_chunk(layer, c)
            launch(now)

            @pl.when(now > 0)
            def _():
                meet(now - 1)

            @pl.when(now > 1)
            def _():
                settle(now - 2)

        return carry

    lax.fori_loop(0, 2, forward_layer, 0)
    target_load.wait()
    share = share_in[0:1, 0:1]
    for c in range(chunks):
        chain[3, c] = (share * chain[3, c].astype(F32)).astype(BF16)

    def backward_layer(turn_index, carry):
        layer = 1 - turn_index
        for at in range(chunks):
            now = (2 + turn_index) * chunks + at
            finish(now - chunks)
            backward_chunk(layer, chunks - 1 - at)
            launch(now)
            meet(now - 1)
            settle(now - 2)
        weight_grads(layer)
        return carry

    lax.fori_loop(0, 2, backward_layer, 0)
    last = 4 * chunks
    meet(last - 1)
    settle(last - 2)
    settle(last - 1)
    for at in range(chunks):
        finish(last - chunks + at)

    pick = (
        lax.broadcasted_iota(jnp.int32, (width, columns), 0)
        == lax.broadcasted_iota(jnp.int32, (width, columns), 1) + place * columns
    ).astype(BF16)

    def narrow(index):
        return dot_nn(chain[index].reshape(chunks * rows, width), pick).astype(BF16)

    away[0] = narrow(2 - section)
    away[1] = narrow(4 + section)
    swaps = []
    for index, goal in enumerate((out_cols, grad_cols)):
        swaps.append(
            pltpu.make_async_remote_copy(
                src_ref=away.at[index],
                dst_ref=goal.at[section],
                send_sem=swap_send.at[index],
                recv_sem=swap_recv.at[index],
                device_id=twin,
                device_id_type=MESH,
            )
        )
    for item in swaps:
        item.start()
    out_cols[section] = narrow(1 + section)
    grad_cols[section] = narrow(5 - section)
    for item in swaps:
        item.wait()
    for item in gifts:
        item.wait_send()


def train(x, target, share, weights, vec, heads):
    wq, wd, w1, w2 = weights
    count, seq_len, width = x.shape
    rows = min(ROWS, seq_len)
    chunks = seq_len // rows
    lanes = wd.shape[0]
    units = w1.shape[1]
    columns = width // lax.axis_size("tensor")
    tables = jnp.asarray(rotary_tables(seq_len))
    total_rows = width + width + units + lanes
    hbm = pl.BlockSpec(memory_space=pl.ANY)
    vmem = pl.BlockSpec(memory_space=pltpu.VMEM)
    return pl.pallas_call(
        functools.partial(spread_refs, heads, chunks),
        out_shape=(
            jax.ShapeDtypeStruct((count, seq_len, columns), BF16),
            jax.ShapeDtypeStruct((count, seq_len, columns), BF16),
            jax.ShapeDtypeStruct((2, total_rows, width), BF16),
            jax.ShapeDtypeStruct((2, 8, width), F32),
        ),
        in_specs=[hbm, hbm, vmem, vmem, hbm, hbm, hbm, hbm, hbm],
        out_specs=(vmem, vmem, vmem, vmem),
        scratch_shapes=[
            pltpu.VMEM((2,) + wq.shape, BF16),
            pltpu.VMEM((2,) + wd.shape, BF16),
            pltpu.VMEM((2,) + w1.shape, BF16),
            pltpu.VMEM((2,) + w2.shape, BF16),
            pltpu.VMEM((2,) + vec.shape, F32),
            pltpu.VMEM((6, chunks, rows, width), BF16),
            pltpu.VMEM((seq_len, width), BF16),
            pltpu.VMEM((seq_len, width), BF16),
            pltpu.VMEM((2, seq_len, 3 * lanes), BF16),
            pltpu.VMEM((2, seq_len, lanes), BF16),
            pltpu.VMEM((2, seq_len, units), BF16),
            pltpu.VMEM((2, seq_len, units), BF16),
            pltpu.VMEM((seq_len, lanes), F32),
            pltpu.VMEM((seq_len, lanes), F32),
            pltpu.VMEM((chunks, rows, width), BF16),
            pltpu.VMEM((chunks, rows, width), BF16),
            pltpu.VMEM((chunks, rows, width), BF16),
            pltpu.VMEM((2, seq_len, columns), BF16),
        ]
        + [pltpu.VMEM((2, heads, rows, (c + 1) * rows), BF16) for c in range(chunks)]
        + [
            pltpu.SemaphoreType.DMA((7,)),
            pltpu.SemaphoreType.DMA((5,)),
            pltpu.SemaphoreType.DMA((5,)),
            pltpu.SemaphoreType.DMA((3, chunks)),
            pltpu.SemaphoreType.DMA((3, chunks)),
            pltpu.SemaphoreType.DMA((2,)),
            pltpu.SemaphoreType.DMA((2,)),
        ],
        compiler_params=pltpu.CompilerParams(
            collective_id=0, has_side_effects=True, vmem_limit_bytes=63 * 2**20
        ),
    )(
        x.reshape(count, chunks, rows, width),
        target.reshape(count, chunks, rows, width),
        share,
        tables,
        wq,
        wd,
        w1,
        w2,
        vec,
    )


def spread_refs(heads, chunks, *refs):
    before = 9 + 4 + 18
    train_kernel(heads, *refs[:before], refs[before : before + chunks], *refs[before + chunks :])


def per_device(
    hidden_in,
    target,
    tissue,
    ln1_gain,
    ln1_bias,
    ln2_gain,
    ln2_bias,
    qkv_weight,
    qkv_bias,
    dense_weight,
    dense_bias,
    fc1_weight,
    fc1_bias,
    fc2_weight,
    fc2_bias,
):
    count, seq_len, width = hidden_in.shape
    section = lax.axis_index("section")
    heads = qkv_weight.shape[-1] // (3 * HEAD)
    lanes = -(-heads * HEAD // LANES) * LANES
    units = fc1_weight.shape[-1]
    labels = (tissue[:, None] == jnp.arange(TISSUES)[None, :]).astype(F32)
    counts = lax.psum(jnp.sum(labels, axis=0), "dp")
    own_count = jnp.sum(labels * counts[None, :], axis=1)
    share = count * lax.axis_size("dp") / TISSUES / own_count
    own_share = lax.dynamic_index_in_dim(share, section, 0, keepdims=False)
    share_tile = jnp.full((8, LANES), own_share, F32)
    weights = (
        pack_columns(qkv_weight[0], lanes),
        jnp.pad(dense_weight[0], [(0, lanes - heads * HEAD), (0, 0)]),
        fc1_weight[0],
        fc2_weight[0],
    )
    vec = jnp.stack(
        [
            ln1_gain[0].astype(F32),
            ln1_bias[0].astype(F32),
            ln2_gain[0].astype(F32),
            ln2_bias[0].astype(F32),
            dense_bias[0].astype(F32) + fc2_bias[0].astype(F32),
            pack_columns(qkv_bias[0], lanes).astype(F32),
            fc1_bias[0].astype(F32),
            jnp.zeros((width,), F32),
        ]
    )
    out_cols, grad_cols, grads, small = train(hidden_in, target, share_tile, weights, vec, heads)
    own = lax.dynamic_index_in_dim(grads, section, 0, keepdims=False)
    other = lax.dynamic_index_in_dim(grads, 1 - section, 0, keepdims=False)
    other = lax.ppermute(other, "section", [(0, 1), (1, 0)])
    total = lax.psum(own + other, "dp").astype(F32)
    small = lax.psum(small, ("section", "dp"))
    small = lax.dynamic_index_in_dim(small, section, 0, keepdims=False)
    norms = lax.psum(small[:4], "tensor")
    valid = heads * HEAD
    return (
        out_cols[None],
        grad_cols.astype(F32)[None],
        norms[0:1],
        norms[1:2],
        norms[2:3],
        norms[3:4],
        unpack_columns(total[:width], heads)[None],
        unpack_columns(small[4], heads)[None],
        total[2 * width + units :][:valid][None],
        small[5:6],
        total[width : 2 * width][None],
        small[6:7],
        total[2 * width : 2 * width + units][None],
        small[5:6],
    )


def solution(mesh):
    return jax.shard_map(
        per_device,
        mesh=mesh,
        in_specs=(
            P("dp", None, None),
            P("dp", None, None),
            P("dp"),
            P("section", None),
            P("section", None),
            P("section", None),
            P("section", None),
            P("section", None, "tensor"),
            P("section", "tensor"),
            P("section", "tensor", None),
            P("section", None),
            P("section", None, "tensor"),
            P("section", "tensor"),
            P("section", "tensor", None),
            P("section", None),
        ),
        out_specs=(
            P("section", "dp", None, "tensor"),
            P("section", "dp", None, "tensor"),
            P("section", None),
            P("section", None),
            P("section", None),
            P("section", None),
            P("section", None, "tensor"),
            P("section", "tensor"),
            P("section", "tensor", None),
            P("section", None),
            P("section", None, "tensor"),
            P("section", "tensor"),
            P("section", "tensor", None),
            P("section", None),
        ),
        check_vma=False,
    )
```

time: 1660 us -> 335 us (0.20); the launches traced: 1640 us -> 334 us
  waiting for transfers between devices: 1120 us -> 56.1 us
  matrix products: 267 us -> 0 us
  Pallas kernels: 0 us -> 173 us
  other arithmetic: 109 us -> 7.48 us
  loops' own time: 30.3 us -> 0 us
  local copies, waits for them, and re-layouts: 54.4 us -> 26.1 us
  blocking collectives: 28.9 us -> 57.1 us
    psum x7 -> x1, waiting for transfers between devices: 1110 us -> 49.4 us  [per_device(): total = lax.psum(own + other, 'dp').astype(F32)]
    dot_general x81 -> x0, matrix products: 231 us -> none  [the longest x12 49.4 us: against(): lax.dot_general(left, right, (((1,), (1,)), ((), ())), preferred_element_...]
    pallas_call x0 -> x1, Pallas kernels: none -> 173 us  [train(): pl.pallas_call(functools.partial(spread_refs, heads, chunks), out_shape=(...]
    reduce_sum x27 -> x0, other arithmetic: 45.6 us -> none  [the longest x6 21.2 us: layer_norm(): return center * lax.rsqrt(spread + 1e-05) * gain + bias]
    dynamic_update_slice x9 -> x0, other arithmetic: 39.2 us -> none  [the longest x6 21.1 us: per_device(): _, (inputs_all, outputs_all) = lax.scan(forward_turn, start_value, turns)]
    sub x6 -> x0, matrix products: 35.9 us -> none  [attend(): raised = jnp.exp(scores - highest)]
    another operation x2 -> x0, loops' own time: 30.3 us -> none  [the longest x1 27.9 us: per_device(): lax.scan(backward_turn, (start_value, zero_grads), turns)]
    psum x1 -> x2, blocking collectives: 17.5 us -> 45.7 us  [the longest x1 27.6 us: per_device(): small = lax.psum(small, ('section', 'dp'))]
  transfers between devices with their start and end apart: 13 -> 2, of which waited for: 10 -> 2; matrix products, arithmetic and copies ran while one was open for 4% -> 2% of each run, Pallas kernels for 0% -> 0%
where the time goes in v1:
time: 335 us; the launch traced here: 334 us
  Pallas kernels  173 us (52%)
  blocking collectives  57.1 us (17%)
  waiting for transfers between devices  56.1 us (17%)
  local copies, waits for them, and re-layouts  26.1 us (8%)
  between operations  14.2 us (4%)
  other arithmetic  7.48 us (2%)
    pallas_call x1, Pallas kernels, train(): pl.pallas_call(functools.partial(spread_refs, heads, chunks), out_shape=(...  173 us
    psum x1, waiting for transfers between devices, per_device(): total = lax.psum(own + other, 'dp').astype(F32)  49.4 us
    psum x1, blocking collectives, per_device(): small = lax.psum(small, ('section', 'dp'))  27.6 us
    psum x1, blocking collectives, per_device(): norms = lax.psum(small[:4], 'tensor')  18.1 us
    psum x1, blocking collectives, per_device(): counts = lax.psum(jnp.sum(labels, axis=0), 'dp')  11.3 us
  transfers between devices with their start and end apart: 2, of which 2 were waited for; matrix products, arithmetic and copies ran while one was open for 2% of the time, Pallas kernels for 0%

profile of v1, /device:TPU:0, one launch (start us, length us, event | category | flops | bytes accessed | tf_op | source)
XLA Modules:
  0.0 334.2 jit_solution(4832873894382473842)
XLA Ops:
  7.2 0.7 convert_reduce_fusion
  8.0 11.3 %psum.28 = f32[16]{0:T(128)S(1)} all-reduce(f32[16]{0:T(128)S(1)} %convert_reduce_fusion), channel_id=1, replica_groups=mesh['section'=2,'dp'=4,'tensor'=4] {'dp'}, use_global_device_ids=true, to_apply=%region_1.0 | all-reduce | flops 16 | bytes 128 | tf_op jit(solution)/shard_map/psum | solution.py:575
  19.3 0.8 select_reduce_fusion
  21.1 1.3 copy.52
  22.4 1.7 pad.13.refs_5_
  24.2 1.5 copy.54.refs_4_
  27.0 1.2 broadcast_in_dim.24.refs_2_
  28.2 173.0 %shard_map.263 = (bf16[2,1024,192]{2,1,0:T(8,128)(2,1)}, bf16[2,1024,192]{2,1,0:T(8,128)(2,1)}, bf16[2,2560,768]{2,1,0:T(8,128)(2,1)}, f32[2,8,768]{2,1,0:T(8,128)}) custom-call(bf16[2,4,256,768]{3,2,1,0:T(8,128)(2,1)} %bitcast.49, bf16[2,4,256,768]{3,2,1,0:T(8,128)(2,1)} %bitcast.50, f32[8,128]{1,0:T(8,128)} %broadcast_in_dim.24.refs_2_, ...), custom_call_target="tpu_custom_call" | custom-call | tf_op jit(solution)/shard_map/pallas_call | solution.py:491
  201.2 2.5 dynamic-slice_bitcast_fusion
  203.9 6.6 %collective-permute-done = bf16[2560,768]{1,0:T(8,128)(2,1)S(1)} collective-permute-done((bf16[2560,768]{1,0:T(8,128)(2,1)S(1)}, bf16[2560,768]{1,0:T(8,128)(2,1)S(1)}, u32[]{:S(2)}, u32[]{:S(2)}) %collective-permute-start) | collective-permute-done | bytes 3932192 | tf_op jit(solution)/shard_map/ppermute | solution.py:601
  210.6 2.3 bitcast_add_fusion
  212.9 1.2 copy-done.3
  214.1 1.2 copy.58
  215.3 27.6 %psum.29 = f32[2,8,768]{2,1,0:T(8,128)S(1)} all-reduce(f32[2,8,768]{2,1,0:T(8,128)S(1)} %copy-done.4), channel_id=1, replica_groups=mesh['section'=2,'dp'=4,'tensor'=4] {'section','dp'}, use_global_device_ids=true, to_apply=%region_3.4 | all-reduce | flops 12288 | bytes 98304 | tf_op jit(solution)/shard_map/psum | solution.py:603
  244.5 1.7 copy.59
  246.1 18.1 %psum.30 = f32[4,768]{1,0:T(4,128)S(1)} all-reduce(f32[4,768]{1,0:T(4,128)S(1)} %dynamic-slice_bitcast_fusion.1), channel_id=1, replica_groups=mesh['section'=2,'dp'=4,'tensor'=4] {'tensor'}, use_global_device_ids=true, to_apply=%region_4.5 | all-reduce | flops 3072 | bytes 24576 | tf_op jit(solution)/shard_map/psum | solution.py:605
  264.9 49.4 %all-reduce.5.cloned.1.call-done = bf16[2560,768]{1,0:T(8,128)(2,1)} async-done(((bf16[2560,768]{1,0:T(8,128)(2,1)}), bf16[2560,768]{1,0:T(8,128)(2,1)}) %all-reduce.5.cloned.1.call-update) | async-done | bytes 3932176 | tf_op jit(solution)/shard_map/psum | solution.py:602
  314.3 2.7 convert_element_type.64
  317.0 0.9 slice_bitcast_fusion.2
  317.9 2.7 slice_bitcast_fusion
  320.6 1.1 copy-done
  321.9 2.0 copy.55
  323.8 1.6 slice.77
  325.4 1.3 copy.56
  (49 shorter events, 5.4 us)
Async XLA Ops:
  7.2 307.1 %all-reduce.5.cloned.1.call-start = ((), (), s32[]{:S(2)}) async-start(), calls=%async_computation | async-start | bytes 7864320 | tf_op jit(solution)/shard_map/psum | solution.py:602
  21.1 5.2 %copy-start.11 = (bf16[1,768]{1,0:T(2,128)(2,1)S(1)}, bf16[1,768]{1,0:T(2,128)(2,1)}, u32[]{:S(2)}) copy-start(bf16[1,768]{1,0:T(2,128)(2,1)} %param.30) | copy-start | bytes 4612
  21.1 5.2 %copy-start.12 = (bf16[1,768]{1,0:T(2,128)(2,1)S(1)}, bf16[1,768]{1,0:T(2,128)(2,1)}, u32[]{:S(2)}) copy-start(bf16[1,768]{1,0:T(2,128)(2,1)} %param.26) | copy-start | bytes 4612
  21.1 5.2 %copy-start.6 = (bf16[1,768]{1,0:T(2,128)(2,1)S(1)}, bf16[1,768]{1,0:T(2,128)(2,1)}, u32[]{:S(2)}) copy-start(bf16[1,768]{1,0:T(2,128)(2,1)} %param.19) | copy-start | bytes 4612
  21.1 5.2 %copy-start.7 = (bf16[1,768]{1,0:T(2,128)(2,1)S(1)}, bf16[1,768]{1,0:T(2,128)(2,1)}, u32[]{:S(2)}) copy-start(bf16[1,768]{1,0:T(2,128)(2,1)} %param.20) | copy-start | bytes 4612
  21.1 5.2 %copy-start.8 = (bf16[1,768]{1,0:T(2,128)(2,1)S(1)}, bf16[1,768]{1,0:T(2,128)(2,1)}, u32[]{:S(2)}) copy-start(bf16[1,768]{1,0:T(2,128)(2,1)} %param.21) | copy-start | bytes 4612
  21.1 5.2 %copy-start.9 = (bf16[1,768]{1,0:T(2,128)(2,1)S(1)}, bf16[1,768]{1,0:T(2,128)(2,1)}, u32[]{:S(2)}) copy-start(bf16[1,768]{1,0:T(2,128)(2,1)} %param.22) | copy-start | bytes 4612
  21.1 5.2 %copy-start.10 = (bf16[1,768]{1,0:T(2,128)(2,1)S(1)}, bf16[1,768]{1,0:T(2,128)(2,1)}, u32[]{:S(2)}) copy-start(bf16[1,768]{1,0:T(2,128)(2,1)} %param.28) | copy-start | bytes 4612
  201.2 9.4 %copy-start.1 = (bf16[2,2560,768]{2,1,0:T(8,128)(2,1)S(1)}, bf16[2,2560,768]{2,1,0:T(8,128)(2,1)}, u32[]{:S(2)}) copy-start(bf16[2,2560,768]{2,1,0:T(8,128)(2,1)} %get-tuple-element.21) | copy-start | bytes 23592964
  203.7 6.8 %collective-permute-start = (bf16[2560,768]{1,0:T(8,128)(2,1)S(1)}, bf16[2560,768]{1,0:T(8,128)(2,1)S(1)}, u32[]{:S(2)}, u32[]{:S(2)}) collective-permute-start(bf16[2560,768]{1,0:T(8,128)(2,1)S(1)} %dynamic-slice_bitcast_fusion), channel_id=1, source_target_pairs={{0,16},{16,0},{1,17},{17,1},{2,18},{18,2},{3,19},{19,3},{4,20},{20... | collective-permute-start | bytes 11796488 | tf_op jit(solution)/shard_map/ppermute | solution.py:601
  212.9 1.2 copy-start.3
  212.9 2.5 copy-start.4
  212.9 31.4 %copy-start.2 = (bf16[2,1024,192]{2,1,0:T(8,128)(2,1)S(1)}, bf16[2,1024,192]{2,1,0:T(8,128)(2,1)}, u32[]{:S(2)}) copy-start(bf16[2,1024,192]{2,1,0:T(8,128)(2,1)} %get-tuple-element.19) | copy-start | bytes 2359300
  243.5 83.2 %copy-start.5 = (f32[1,768]{1,0:T(1,128)}, f32[1,768]{1,0:T(1,128)S(1)}, u32[]{:S(2)}) copy-start(f32[1,768]{1,0:T(1,128)S(1)} %get-tuple-element.114) | copy-start | bytes 9220
  317.9 3.8 %copy-start = (bf16[2560,768]{1,0:T(8,128)(2,1)S(1)}, bf16[2560,768]{1,0:T(8,128)(2,1)}, u32[]{:S(2)}) copy-start(bf16[2560,768]{1,0:T(8,128)(2,1)} %all-reduce.5.cloned.1.call-done) | copy-start | bytes 11796484
Sparse Core Ops, SparseCore 0:
  213.0 101.2 all-reduce.4

commit v2 on v1

v2 whole, which is shorter than its diff:
```python
import functools
import math

import jax
import jax.numpy as jnp
import numpy as np
from jax import lax
from jax.experimental import pallas as pl
from jax.experimental.pallas import tpu as pltpu
from jax.sharding import PartitionSpec as P

HEAD = 64
ROT = 16
TISSUES = 16
ROWS = 256
LANES = 128
EPS = 1e-05
MESH = pl.DeviceIdType.MESH
F32 = jnp.float32
BF16 = jnp.bfloat16


def dot_nn(a, b):
    return lax.dot_general(a, b, (((1,), (0,)), ((), ())), preferred_element_type=F32)


def dot_nt(a, b):
    return lax.dot_general(a, b, (((1,), (1,)), ((), ())), preferred_element_type=F32)


def dot_tn(a, b):
    return lax.dot_general(a, b, (((0,), (0,)), ((), ())), preferred_element_type=F32)


def rotary_tables(seq_len):
    half = ROT // 2
    inverse = 10000.0 ** (-2.0 * np.arange(half) / ROT)
    angles = np.arange(seq_len)[:, None] * inverse[None, :]
    cosines = np.ones((seq_len, HEAD))
    sines = np.zeros((seq_len, HEAD))
    cosines[:, :half] = np.cos(angles)
    cosines[:, half:ROT] = np.cos(angles)
    sines[:, :half] = -np.sin(angles)
    sines[:, half:ROT] = np.sin(angles)
    tables = np.stack([np.tile(item, (1, LANES // HEAD)) for item in (cosines, sines)])
    return tables.astype(np.float32)


def unpack_rows(packed, heads):
    width = packed.shape[-1]
    split = packed.reshape(3, heads, HEAD, width)
    return split.transpose(3, 1, 0, 2).reshape(width, 3 * heads * HEAD)


def unpack_line(line, heads):
    split = line.reshape(3, -1)[:, : heads * HEAD].reshape(3, heads, HEAD)
    return split.transpose(1, 0, 2).reshape(1, 3 * heads * HEAD)


def normalise(value):
    center = value - jnp.mean(value, axis=-1, keepdims=True)
    rstd = lax.rsqrt(jnp.mean(center * center, axis=-1, keepdims=True) + EPS)
    return center * rstd, rstd


def train_kernel(
    heads,
    x_in,
    target_in,
    tissue,
    tables,
    wq_in,
    wd_in,
    w1_in,
    w2_in,
    qkv_bias,
    vec_in,
    out_cols,
    grad_cols,
    grads,
    small,
    wq,
    wd,
    w1,
    w2,
    raw,
    vec,
    chain,
    qkv,
    ctx,
    act,
    gate,
    key_grad,
    value_grad,
    part,
    got,
    met,
    total,
    half_got,
    first_got,
    second_got,
    more_got,
    line_got,
    tally,
    tally_got,
    probs,
    load_sem,
    give_sem,
    take_sem,
    hop_send,
    hop_recv,
    swap_send,
    swap_recv,
    sum_send,
    sum_recv,
    line_send,
    line_recv,
    tally_send,
    tally_recv,
    store_sem,
):
    section = lax.axis_index("section")
    replica = lax.axis_index("dp")
    place = lax.axis_index("tensor")
    copies = lax.axis_size("dp")
    bits = copies.bit_length() - 1
    chunks, rows, width = part.shape
    lanes = wd.shape[1]
    valid = heads * HEAD
    padded = out_cols.shape[-1]
    columns = width // lax.axis_size("tensor")
    inner = jnp.logical_and(place > 0, place < 3)
    outer = jnp.logical_not(inner)
    beside = place + 1 - 2 * lax.rem(place, 2)
    across = 3 - place

    def flipped(bit):
        return replica + (1 << bit) * (1 - 2 * lax.rem(replica // (1 << bit), 2))

    twin = {"section": 1 - section}
    mates = [{"dp": flipped(bit)} for bit in range(bits)]
    near = {"tensor": beside}
    far = {"tensor": across}
    friends = [twin, near, far] + mates

    def send(source, goal, sems, target):
        return pltpu.make_async_remote_copy(
            src_ref=source,
            dst_ref=goal,
            send_sem=sems[0],
            recv_sem=sems[1],
            device_id=target,
            device_id_type=MESH,
        )

    barrier = pltpu.get_barrier_semaphore()
    for friend in friends:
        pl.semaphore_signal(barrier, inc=1, device_id=friend, device_id_type=MESH)

    raw_load = pltpu.make_async_copy(wq_in, raw, load_sem.at[0])
    raw_load.start()
    input_load = pltpu.make_async_copy(x_in.at[section], chain.at[0], load_sem.at[1])
    input_load.start()
    pairs = ((w1_in, w1.at[section]), (wd_in, wd.at[section, :valid]), (w2_in, w2.at[section]))
    loads = [
        pltpu.make_async_copy(source, goal, load_sem.at[2 + index])
        for index, (source, goal) in enumerate(pairs)
    ]
    for item in loads:
        item.start()
    target_load = pltpu.make_async_copy(target_in.at[section], chain.at[3], load_sem.at[5])
    target_load.start()

    column = lax.broadcasted_iota(jnp.int32, (3 * valid, 3 * lanes), 0)
    head_of, rest = column // (3 * HEAD), lax.rem(column, 3 * HEAD)
    goal_of = (rest // HEAD) * lanes + head_of * HEAD + lax.rem(rest, HEAD)
    pack = (goal_of == lax.broadcasted_iota(jnp.int32, goal_of.shape, 1)).astype(BF16)
    for index, item in enumerate(vec_in):
        vec[section, index : index + 1] = item[...].astype(F32)
    vec[section, 4:5] = vec_in[4][...].astype(F32) + vec_in[5][...].astype(F32)
    vec[section, 5:6] = dot_nn(jnp.broadcast_to(qkv_bias[...], (16, 3 * valid)), pack)[0:1]
    vec[section, 7:8] = jnp.zeros((1, width), F32)
    for layer in range(2):
        wd[layer, valid:] = jnp.zeros((lanes - valid, width), BF16)
    raw_load.wait()
    wq[section] = dot_nn(raw[...], pack).astype(BF16)
    pl.semaphore_wait(barrier, len(friends))
    gifts = [
        send(source, goal, (give_sem.at[index], take_sem.at[index]), twin)
        for index, (source, goal) in enumerate(
            ((wq.at[section], wq.at[section]), (vec.at[section], vec.at[section])) + pairs
        )
    ]
    for item in gifts:
        item.start()

    tissue_lane = lax.broadcasted_iota(jnp.int32, (8, LANES), 1)
    marks = [(tissue_lane == tissue[index]).astype(F32) for index in range(tissue.shape[0])]
    tally[...] = functools.reduce(lambda a, b: a + b, marks)

    def tally_step(bit):
        return send(
            tally, tally_got.at[bit], (tally_send.at[bit], tally_recv.at[bit]), mates[bit]
        )

    if bits:
        tally_step(0).start()

    def count_on(bit):
        step = tally_step(bit)
        step.wait()
        tally[...] += tally_got[bit]
        if bit + 1 < bits:
            tally_step(bit + 1).start()

    lane = lax.broadcasted_iota(jnp.int32, (1, lanes), 1) // HEAD
    head_masks = [lane == h for h in range(heads)]
    factor = HEAD ** (-0.5)

    left_half = lax.rem(lax.broadcasted_iota(jnp.int32, (1, lanes), 1), HEAD) < ROT // 2

    def wide(table, start):
        piece = tables[table, start : start + rows, :]
        return jnp.concatenate([piece] * (lanes // LANES), axis=1)

    def turned(value):
        ahead = pltpu.roll(value, lanes - ROT // 2, 1)
        behind = pltpu.roll(value, ROT // 2, 1)
        return jnp.where(left_half, ahead, behind)

    def turn(value, start):
        return value * wide(0, start) + turned(value) * wide(1, start)

    def turn_back(value, start):
        return value * wide(0, start) - turned(value) * wide(1, start)

    def only(mask, value):
        return jnp.where(mask, value, jnp.zeros_like(value))

    def forward_chunk(layer, c):
        start = c * rows
        here = slice(start, start + rows)
        spread, _ = normalise(chain[layer, c].astype(F32))
        first = (spread * vec[layer, 0:1] + vec[layer, 1:2]).astype(BF16)
        second = (spread * vec[layer, 2:3] + vec[layer, 3:4]).astype(BF16)
        projected = dot_nn(first, wq[layer]) + vec[layer, 5:6]
        query = turn(projected[:, :lanes], start).astype(BF16)
        qkv[layer, here, :lanes] = query
        qkv[layer, here, lanes : 2 * lanes] = turn(projected[:, lanes : 2 * lanes], start).astype(
            BF16
        )
        qkv[layer, here, 2 * lanes :] = projected[:, 2 * lanes :].astype(BF16)
        pre = dot_nn(second, w1[layer]) + vec[layer, 6:7]
        below = 0.5 * (1.0 + lax.erf(pre * (0.5**0.5)))
        active = (pre * below).astype(BF16)
        act[layer, here, :] = active
        slope = below + pre * (jnp.exp(-0.5 * pre * pre) * ((2.0 * np.pi) ** -0.5))
        gate[layer, here, :] = slope.astype(BF16)
        diagonal = lax.broadcasted_iota(jnp.int32, (rows, rows), 0) >= lax.broadcasted_iota(
            jnp.int32, (rows, rows), 1
        )
        context = jnp.zeros((rows, lanes), F32)
        for h in range(heads):
            asked = only(head_masks[h], query) * jnp.asarray(factor, BF16)
            near = dot_nt(asked, qkv[layer, here, lanes : 2 * lanes])
            near = jnp.where(diagonal, near, -1e30)
            highest = jnp.max(near, axis=-1, keepdims=True)
            if c > 0:
                far = dot_nt(asked, qkv[layer, :start, lanes : 2 * lanes])
                highest = jnp.maximum(highest, jnp.max(far, axis=-1, keepdims=True))
                far = jnp.exp(far - highest)
            near = jnp.exp(near - highest)
            total = jnp.sum(near, axis=-1, keepdims=True)
            if c > 0:
                total = total + jnp.sum(far, axis=-1, keepdims=True)
            inverse = 1.0 / total
            near = (near * inverse).astype(BF16)
            probs[c][layer, h, :, start:] = near
            mixed = dot_nn(near, qkv[layer, here, 2 * lanes :])
            if c > 0:
                far = (far * inverse).astype(BF16)
                probs[c][layer, h, :, :start] = far
                mixed = mixed + dot_nn(far, qkv[layer, :start, 2 * lanes :])
            context = jnp.where(head_masks[h], mixed, context)
        context = context.astype(BF16)
        ctx[layer, here, :] = context
        part[c] = (dot_nn(context, wd[layer]) + dot_nn(active, w2[layer])).astype(BF16)

    def backward_chunk(layer, c):
        start = c * rows
        stop = start + rows
        here = slice(start, stop)
        first_turn = c == chunks - 1
        slot = chunks - 1 - c
        cotangent = chain[4 - layer, c]
        context_grad = dot_nt(cotangent, wd[layer]).astype(BF16)
        pre_grad = (dot_nt(cotangent, w2[layer]) * gate[layer, here, :].astype(F32)).astype(BF16)
        gate[layer, here, :] = pre_grad
        second_back = dot_nt(pre_grad, w1[layer])
        query = qkv[layer, here, :lanes]
        weighed = context_grad.astype(F32) * ctx[layer, here, :].astype(F32)
        query_grad = jnp.zeros((rows, lanes), F32)
        key_sum = None
        value_sum = None
        for h in range(heads):
            mask = head_masks[h]
            own_grad = only(mask, context_grad)
            asked = only(mask, query) * jnp.asarray(factor, BF16)
            row_dot = jnp.sum(only(mask, weighed), axis=-1, keepdims=True)
            prob = probs[c][layer, h]
            prob_grad = dot_nt(own_grad, qkv[layer, :stop, 2 * lanes :])
            score_grad = (prob.astype(F32) * (prob_grad - row_dot)).astype(BF16)
            query_grad = jnp.where(
                mask, dot_nn(score_grad, qkv[layer, :stop, lanes : 2 * lanes]), query_grad
            )
            key_part = dot_tn(score_grad, asked)
            value_part = dot_tn(prob, own_grad)
            key_sum = key_part if key_sum is None else key_sum + key_part
            value_sum = value_part if value_sum is None else value_sum + value_part
        if first_turn:
            key_grad[:stop] = key_sum
            value_grad[:stop] = value_sum
        else:
            key_grad[:stop] += key_sum
            value_grad[:stop] += value_sum
        qkv[layer, here, :lanes] = turn_back(query_grad * factor, start).astype(BF16)
        qkv[layer, here, lanes : 2 * lanes] = turn_back(key_grad[here], start).astype(BF16)
        qkv[layer, here, 2 * lanes :] = value_grad[here].astype(BF16)
        projected_grad = qkv[layer, here, :]
        first_back = dot_nt(projected_grad, wq[layer])
        spread, rstd = normalise(chain[layer, c].astype(F32))
        first = (spread * vec[layer, 0:1] + vec[layer, 1:2]).astype(BF16)
        second = (spread * vec[layer, 2:3] + vec[layer, 3:4]).astype(BF16)
        sums = (
            first_back * spread,
            first_back,
            second_back * spread,
            second_back,
            projected_grad.astype(F32),
            cotangent.astype(F32),
            pre_grad.astype(F32),
        )
        for index, item in enumerate(sums):
            line = jnp.sum(item, axis=0, keepdims=True)
            if first_turn:
                small[layer, index : index + 1] = line
            else:
                small[layer, index : index + 1] += line
        if first_turn:
            small[layer, len(sums) :] = jnp.zeros((8 - len(sums), width), F32)
        back = first_back * vec[layer, 0:1] + second_back * vec[layer, 2:3]
        middle = jnp.mean(back, axis=-1, keepdims=True)
        tilt = jnp.mean(back * spread, axis=-1, keepdims=True)
        part[slot] = (rstd * (back - middle - spread * tilt)).astype(BF16)
        return here, first_turn, first, second, pre_grad, cotangent

    def add_weight_grads(layer, here, first_turn, first, second, pre_grad, cotangent):
        step = lanes
        base = 0
        sources = (
            (qkv.at[layer, here], first, valid),
            (second, pre_grad, step),
            (act.at[layer, here], cotangent, step),
            (ctx.at[layer, here], cotangent, valid),
        )
        for left, right, kept in sources:
            for at in range(0, left.shape[-1], step):
                piece = dot_tn(left[:, at : at + step], right)[:kept]
                goal = slice(base, base + kept)
                if not first_turn:
                    piece = piece + total[layer, goal].astype(F32)
                total[layer, goal] = piece.astype(BF16)
                base += kept

    all_rows = total.shape[1]
    share_rows = all_rows // 2
    folds = min(bits, 2)

    def spans(group):
        order = (0, 1)[:folds] if group == 0 else (1, 0)[-folds:] if folds else ()
        size = share_rows // 2
        start = section * share_rows + group * size
        steps = []
        for bit in order:
            size = size // 2
            upper = lax.rem(replica // (1 << bit), 2)
            steps.append((bit, start + upper * size, start + (1 - upper) * size, size))
            start = start + upper * size
        return steps, start, size

    groups = [spans(0), spans(1)]
    sum_steps = 2 + 2 * folds + (bits - folds)

    group_rows = share_rows // 2

    def sums_of(layer, start, size):
        return total.at[layer, pl.ds(pl.multiple_of(start, 16), size)]

    def gathered(layer, group, start, size):
        start = start - section * share_rows - group * group_rows
        return (act, gate)[group].at[layer, pl.ds(pl.multiple_of(start, 16), size)]

    def sum_sems(layer, step, group):
        return sum_send.at[layer, step, group], sum_recv.at[layer, step, group]

    def sum_copies(layer, step):
        if step == 0:
            source = sums_of(layer, (1 - section) * share_rows, share_rows)
            return [send(source, half_got.at[layer], sum_sems(layer, 0, 0), twin)]
        copies_now = []
        for group, (steps, start, size) in enumerate(groups):
            sems = sum_sems(layer, step, group)
            if step <= folds:
                bit, _, gone, size = steps[step - 1]
                goal = (first_got, second_got)[step - 1].at[group]
                copies_now.append(send(sums_of(layer, gone, size), goal, sems, mates[bit]))
            elif step <= bits:
                goal = more_got.at[layer, step - 1 - folds, group]
                source = gathered(layer, group, start, size)
                copies_now.append(send(source, goal, sems, mates[step - 1]))
            else:
                bit, start, _, size = steps[bits - step]
                piece = gathered(layer, group, start, size)
                copies_now.append(send(piece, piece, sems, mates[bit]))
        return copies_now

    def last_copies(layer):
        pieces = []
        for group in range(2):
            first_row = section * share_rows + group * group_rows
            piece = gathered(layer, group, first_row, group_rows)
            goal = grads.at[pl.ds(pl.multiple_of(first_row, 16), group_rows)]
            sems = sum_sems(layer, sum_steps - 1, group)
            other_row = (1 - section) * share_rows + group * group_rows
            other = grads.at[pl.ds(pl.multiple_of(other_row, 16), group_rows)]
            pieces.append(
                (
                    send(piece, goal, sems, twin),
                    send(piece, other, sems, twin),
                    pltpu.make_async_copy(piece, goal, store_sem.at[group]),
                )
            )
        return pieces

    def sum_start(layer, step):
        if step < sum_steps - 1:
            for item in sum_copies(layer, step):
                item.start()
            return
        for give, _, keep in last_copies(layer):
            pl.when(section != layer)(give.start)
            pl.when(section == layer)(keep.start)

    def add_rows(goal, base, source):
        size = source.shape[0]
        piece = math.gcd(size, 144)

        def add_piece(index, carry):
            here = pl.ds(pl.multiple_of(index * piece, 16), piece)
            goal[here] = (base[here].astype(F32) + source[here].astype(F32)).astype(BF16)
            return carry

        lax.fori_loop(0, size // piece, add_piece, 0)

    def sum_end(layer, step):
        if step == sum_steps - 1:
            for give, take, keep in last_copies(layer):
                pl.when(section != layer)(give.wait_send)
                pl.when(section == layer)(take.wait_recv)
                pl.when(section == layer)(keep.wait)
            return
        for item in sum_copies(layer, step):
            item.wait()
        if step == 0:
            base = sums_of(layer, section * share_rows, share_rows)
            add_rows(base, base, half_got.at[layer])
            return
        if step > bits:
            return
        for group, (steps, start, size) in enumerate(groups):
            goal = gathered(layer, group, start, size)
            if step < folds:
                base = sums_of(layer, steps[step - 1][1], steps[step - 1][3])
                add_rows(base, base, first_got.at[group])
            elif step == folds:
                add_rows(goal, sums_of(layer, start, size), second_got.at[group])
            else:
                add_rows(goal, goal, more_got.at[layer, step - 1 - folds, group])

    line_friends = [twin] + mates + [near, far]

    def line_copy(step):
        sems = (line_send.at[step], line_recv.at[step])
        return send(small, line_got.at[step], sems, line_friends[step])

    def line_end(step):
        line_copy(step).wait()
        if step <= bits:
            small[...] += line_got[step]
        else:
            small[:, 0:4] += line_got[step, :, 0:4]

    def locate(turn_index):
        kind = turn_index // chunks
        slot = lax.rem(turn_index, chunks)
        row = jnp.where(kind < 2, slot, chunks - 1 - slot)
        base = kind + jnp.where(kind < 2, 0, 1)
        goal = jnp.where(kind == 3, 3, base + 1)
        return kind, slot, row, base, goal

    def hop(stage, slot, source, goal, target):
        return pltpu.make_async_remote_copy(
            src_ref=source,
            dst_ref=goal,
            send_sem=hop_send.at[stage, slot],
            recv_sem=hop_recv.at[stage, slot],
            device_id=target,
            device_id_type=MESH,
        )

    def first_hop(slot):
        return hop(0, slot, part.at[slot], got.at[slot], near)

    def second_hop(slot):
        return hop(1, slot, part.at[slot], met.at[slot], far)

    def third_hop(slot, row, goal):
        piece = chain.at[goal, row]
        return hop(2, slot, piece, piece, near)

    def launch(turn_index):
        _, slot, _, _, _ = locate(turn_index)

        @pl.when(outer)
        def _():
            first_hop(slot).start()

    def meet(turn_index):
        _, slot, _, _, _ = locate(turn_index)

        @pl.when(inner)
        def _():
            first_hop(slot).wait_recv()
            part[slot] = (part[slot].astype(F32) + got[slot].astype(F32)).astype(BF16)
            second_hop(slot).start()

    def settle(turn_index):
        kind, slot, row, base, goal = locate(turn_index)

        @pl.when(inner)
        def _():
            second_hop(slot).wait_recv()
            keep = jnp.where(kind < 2, 1.0, 0.0)
            shift = vec[jnp.minimum(kind, 1), 4:5] * keep
            total = part[slot].astype(F32) + met[slot].astype(F32)
            chain[goal, row] = (chain[base, row].astype(F32) + (total + shift)).astype(BF16)
            third_hop(slot, row, goal).start()

    def finish(turn_index):
        _, slot, row, _, goal = locate(turn_index)

        @pl.when(outer)
        def _():
            first_hop(slot).wait_send()
            third_hop(slot, row, goal).wait_recv()

        @pl.when(inner)
        def _():
            second_hop(slot).wait_send()
            third_hop(slot, row, goal).wait_send()

    def need(index, layer):
        @pl.when(section == layer)
        def _():
            if index > 1:
                loads[index - 2].wait()

        @pl.when(section != layer)
        def _():
            gifts[index].wait_recv()

    input_load.wait()

    def forward_layer(layer, carry):
        for index in range(len(gifts)):
            need(index, layer)
        for c in range(chunks):
            now = layer * chunks + c

            @pl.when(layer > 0)
            def _():
                finish(now - chunks)

            forward_chunk(layer, c)
            launch(now)

            @pl.when(now > 0)
            def _():
                meet(now - 1)

            @pl.when(now > 1)
            def _():
                settle(now - 2)

            for bit in range(bits):
                if bit % chunks == c:
                    pl.when(layer == bit // chunks)(functools.partial(count_on, bit))
        return carry

    lax.fori_loop(0, 2, forward_layer, 0)
    target_load.wait()
    own_mark = jnp.where(section == 0, marks[0], marks[1])[0:1]
    own_count = jnp.sum(own_mark * tally[0:1], axis=-1, keepdims=True)
    share = (tissue.shape[0] * copies / TISSUES) / own_count
    for c in range(chunks):
        chain[3, c] = (share * chain[3, c].astype(F32)).astype(BF16)

    def backward_layer(turn_index, carry):
        layer = 1 - turn_index
        for at in range(chunks):
            now = (2 + turn_index) * chunks + at
            if at == 0:

                @pl.when(layer == 0)
                def _():
                    sum_end(1, 0)
                    sum_start(1, 1)

            finish(now - chunks)

            @pl.when(layer == 0)
            def _():
                sum_end(1, at + 1)
                sum_start(1, at + 2)

            kept = backward_chunk(layer, chunks - 1 - at)
            launch(now)
            add_weight_grads(layer, *kept)
            meet(now - 1)
            settle(now - 2)

        sum_start(layer, 0)
        return carry

    lax.fori_loop(0, 2, backward_layer, 0)
    last = 4 * chunks
    line_copy(0).start()
    meet(last - 1)
    settle(last - 2)
    for step in range(chunks + 1, sum_steps - 1):
        sum_end(1, step)
        sum_start(1, step + 1)
    for step in range(max(sum_steps, len(line_friends))):
        if step < sum_steps:
            sum_end(0, step)
            if step + 1 < sum_steps:
                sum_start(0, step + 1)
        if step < len(line_friends):
            line_end(step)
            if step + 1 < len(line_friends):
                line_copy(step + 1).start()
        if step == 0:
            settle(last - 1)
            sum_end(1, sum_steps - 1)
    for at in range(chunks):
        finish(last - chunks + at)

    own_column = lax.broadcasted_iota(jnp.int32, (width, padded), 1)
    pick = jnp.logical_and(
        lax.broadcasted_iota(jnp.int32, (width, padded), 0) == own_column + place * columns,
        own_column < columns,
    ).astype(BF16)

    def narrow(index, goal):
        def narrow_chunk(c, carry):
            here = pl.ds(pl.multiple_of(c * rows, rows), rows)
            goal[here] = dot_nn(chain[index, c], pick).astype(BF16)
            return carry

        lax.fori_loop(0, chunks, narrow_chunk, 0)

    goals = (out_cols, grad_cols)
    away = [qkv.at[0, :, index * padded : (index + 1) * padded] for index in range(2)]
    home = [qkv.at[1, :, index * padded : (index + 1) * padded] for index in range(2)]
    moves = []
    for index, goal in enumerate(goals):
        narrow((2 - section, 4 - section)[index], away[index])
        sems = (swap_send.at[index], swap_recv.at[index])
        moves.append(send(away[index], goal.at[section], sems, twin))
        moves[-1].start()
        narrow((1 + section, 3 + section)[index], home[index])
        moves.append(
            pltpu.make_async_copy(home[index], goal.at[section], load_sem.at[1 + index])
        )
        moves[-1].start()
    for item in moves:
        item.wait()
    for item in gifts:
        item.wait_send()


def train(x, target, tissue, weights, qkv_bias, vec):
    wq, wd, w1, w2 = weights
    count, seq_len, width = x.shape
    rows = min(ROWS, seq_len)
    chunks = seq_len // rows
    valid = wd.shape[0]
    heads = valid // HEAD
    lanes = -(-valid // LANES) * LANES
    units = w1.shape[1]
    columns = -(-width // lax.axis_size("tensor") // LANES) * LANES
    bits = lax.axis_size("dp").bit_length() - 1
    tables = jnp.asarray(rotary_tables(seq_len))
    total_rows = 3 * valid + width + units + valid
    hbm = pl.BlockSpec(memory_space=pl.ANY)
    vmem = pl.BlockSpec(memory_space=pltpu.VMEM)
    smem = pl.BlockSpec(memory_space=pltpu.SMEM)
    return pl.pallas_call(
        functools.partial(gather_refs, heads, chunks, len(vec)),
        out_shape=(
            jax.ShapeDtypeStruct((count, seq_len, columns), BF16),
            jax.ShapeDtypeStruct((count, seq_len, columns), BF16),
            jax.ShapeDtypeStruct((total_rows, width), BF16),
            jax.ShapeDtypeStruct((2, 8, width), F32),
        ),
        in_specs=[hbm, hbm, smem, vmem, hbm, hbm, hbm, hbm, vmem] + [vmem] * len(vec),
        out_specs=(hbm, hbm, hbm, vmem),
        scratch_shapes=[
            pltpu.VMEM((2, width, 3 * lanes), BF16),
            pltpu.VMEM((2, lanes, width), BF16),
            pltpu.VMEM((2,) + w1.shape, BF16),
            pltpu.VMEM((2,) + w2.shape, BF16),
            pltpu.VMEM(wq.shape, BF16),
            pltpu.VMEM((2, 8, width), F32),
            pltpu.VMEM((5, chunks, rows, width), BF16),
            pltpu.VMEM((2, seq_len, 3 * lanes), BF16),
            pltpu.VMEM((2, seq_len, lanes), BF16),
            pltpu.VMEM((2, seq_len, units), BF16),
            pltpu.VMEM((2, seq_len, units), BF16),
            pltpu.VMEM((seq_len, lanes), F32),
            pltpu.VMEM((seq_len, lanes), F32),
            pltpu.VMEM((chunks, rows, width), BF16),
            pltpu.VMEM((chunks, rows, width), BF16),
            pltpu.VMEM((chunks, rows, width), BF16),
            pltpu.VMEM((2, total_rows, width), BF16),
            pltpu.VMEM((2, total_rows // 2, width), BF16),
            pltpu.VMEM((2, total_rows // 8, width), BF16),
            pltpu.VMEM((2, total_rows // 16, width), BF16),
            pltpu.VMEM((2, max(bits - 2, 1), 2, total_rows // 16 if bits > 2 else 16, width), BF16),
            pltpu.VMEM((3 + bits, 2, 8, width), F32),
            pltpu.VMEM((8, LANES), F32),
            pltpu.VMEM((max(bits, 1), 8, LANES), F32),
        ]
        + [pltpu.VMEM((2, heads, rows, (c + 1) * rows), BF16) for c in range(chunks)]
        + [
            pltpu.SemaphoreType.DMA((6,)),
            pltpu.SemaphoreType.DMA((5,)),
            pltpu.SemaphoreType.DMA((5,)),
            pltpu.SemaphoreType.DMA((3, chunks)),
            pltpu.SemaphoreType.DMA((3, chunks)),
            pltpu.SemaphoreType.DMA((2,)),
            pltpu.SemaphoreType.DMA((2,)),
            pltpu.SemaphoreType.DMA((2, bits + 4, 2)),
            pltpu.SemaphoreType.DMA((2, bits + 4, 2)),
            pltpu.SemaphoreType.DMA((3 + bits,)),
            pltpu.SemaphoreType.DMA((3 + bits,)),
            pltpu.SemaphoreType.DMA((max(bits, 1),)),
            pltpu.SemaphoreType.DMA((max(bits, 1),)),
            pltpu.SemaphoreType.DMA((2,)),
        ],
        compiler_params=pltpu.CompilerParams(
            collective_id=0, has_side_effects=True, vmem_limit_bytes=63 * 2**20
        ),
    )(
        x.reshape(count, chunks, rows, width),
        target.reshape(count, chunks, rows, width),
        tissue,
        tables,
        wq,
        wd,
        w1,
        w2,
        qkv_bias,
        *vec,
    )


def gather_refs(heads, chunks, lines, *refs):
    ends = (9, 9 + lines, 9 + lines + 4 + 24)
    probs = refs[ends[2] : ends[2] + chunks]
    head, vec, body = refs[: ends[0]], refs[ends[0] : ends[1]], refs[ends[1] : ends[2]]
    train_kernel(heads, *head, vec, *body, probs, *refs[ends[2] + chunks :])


def per_device(
    hidden_in,
    target,
    tissue,
    ln1_gain,
    ln1_bias,
    ln2_gain,
    ln2_bias,
    qkv_weight,
    qkv_bias,
    dense_weight,
    dense_bias,
    fc1_weight,
    fc1_bias,
    fc2_weight,
    fc2_bias,
):
    width = hidden_in.shape[-1]
    section = lax.axis_index("section")
    valid = dense_weight.shape[1]
    heads = valid // HEAD
    units = fc1_weight.shape[-1]
    weights = (qkv_weight[0], dense_weight[0], fc1_weight[0], fc2_weight[0])
    vec = (ln1_gain, ln1_bias, ln2_gain, ln2_bias, dense_bias, fc2_bias, fc1_bias)
    out_cols, grad_cols, total, small = train(hidden_in, target, tissue, weights, qkv_bias, vec)
    small = lax.dynamic_index_in_dim(small, section, 0, keepdims=False)
    columns = width // lax.axis_size("tensor")
    total = total.astype(F32)
    ends = np.cumsum([3 * valid, width, units])
    return (
        out_cols[None, ..., :columns],
        grad_cols[None, ..., :columns].astype(F32),
        small[0:1],
        small[1:2],
        small[2:3],
        small[3:4],
        unpack_rows(total[: ends[0]], heads)[None],
        unpack_line(small[4], heads),
        total[ends[2] :][None],
        small[5:6],
        total[ends[0] : ends[1]][None],
        small[6:7],
        total[ends[1] : ends[2]][None],
        small[5:6],
    )


def solution(mesh):
    return jax.shard_map(
        per_device,
        mesh=mesh,
        in_specs=(
            P("dp", None, None),
            P("dp", None, None),
            P("dp"),
            P("section", None),
            P("section", None),
            P("section", None),
            P("section", None),
            P("section", None, "tensor"),
            P("section", "tensor"),
            P("section", "tensor", None),
            P("section", None),
            P("section", None, "tensor"),
            P("section", "tensor"),
            P("section", "tensor", None),
            P("section", None),
        ),
        out_specs=(
            P("section", "dp", None, "tensor"),
            P("section", "dp", None, "tensor"),
            P("section", None),
            P("section", None),
            P("section", None),
            P("section", None),
            P("section", None, "tensor"),
            P("section", "tensor"),
            P("section", "tensor", None),
            P("section", None),
            P("section", None, "tensor"),
            P("section", "tensor"),
            P("section", "tensor", None),
            P("section", None),
        ),
        check_vma=False,
    )
```

time: 335 us -> 224 us (0.67)
  the two profiles are of different devices: /device:TPU:0 before, /device:TPU:9 now
where the time goes in v2:
time: 224 us
  Pallas kernels  206 us (92%)
  local copies, waits for them, and re-layouts  14.8 us (7%)
  other arithmetic  2.31 us (1%)
    pallas_call x1, Pallas kernels, train(): pl.pallas_call(functools.partial(gather_refs, heads, chunks, len(vec)), o...  206 us
    unnamed x8, local copies, waits for them, and re-layouts  6.27 us

profile of v2, /device:TPU:9, one launch (start us, length us, event | category | flops | bytes accessed | tf_op | source)
XLA Modules:
  0.0 223.9 jit_solution(2861843183629987587)
XLA Ops:
  0.6 2.2 copy.30
  2.9 206.2 %shard_map.263 = (bf16[2,1024,256]{2,1,0:T(8,128)(2,1)}, bf16[2,1024,256]{2,1,0:T(8,128)(2,1)}, bf16[2304,768]{1,0:T(8,128)(2,1)}, f32[2,8,768]{2,1,0:T(8,128)}) custom-call(bf16[2,4,256,768]{3,2,1,0:T(8,128)(2,1)} %bitcast.39, bf16[2,4,256,768]{3,2,1,0:T(8,128)(2,1)} %bitcast.40, s32[2]{0:T(128)} %refs_2_.1, f32[2,1024,128]{2,1,0:T(8,128)} %constant.14.clone.refs_3_, ...), custom_call_target="tpu_custom_call" | custom-call | tf_op jit(solution)/shard_map/pallas_call | solution.py:718
  209.1 1.8 bitcast_convert_fusion
  210.8 1.2 copy.33
  212.1 1.7 copy.34
  213.8 1.8 dynamic-slice_bitcast_fusion
  215.5 1.3 slice.82
  216.8 0.0 copy-start
  216.8 1.3 copy.31
  218.2 0.1 reshape.56
  218.3 0.7 reshape.57
  218.9 0.5 copy-done
  219.5 0.5 convert_element_type.11
  220.0 0.9 slice_bitcast_fusion.3
  220.9 0.0 copy-start.1
  220.9 2.5 %slice_bitcast_fusion = (f32[1,768,768]{2,1,0:T(8,128)}, f32[1,768,768]{2,1,0:T(8,128)}) fusion(f32[2304,768]{1,0:T(8,128)S(1)} %convert_element_type.11), kind=kLoop, calls=%fused_computation | loop fusion | bytes 9437184 | tf_op jit(solution)/shard_map/broadcast_in_dim | solution.py:837
  223.4 0.0 copy-done.1
  223.4 0.6 copy.38
  (2 shorter events, 0.0 us)
Async XLA Ops:
  216.8 2.6 %copy-start = (bf16[2304,768]{1,0:T(8,128)(2,1)S(1)}, bf16[2304,768]{1,0:T(8,128)(2,1)}, u32[]{:S(2)}) copy-start(bf16[2304,768]{1,0:T(8,128)(2,1)} %get-tuple-element.21) | copy-start | bytes 10616836
  220.9 2.5 %copy-start.1 = (f32[1,768]{1,0:T(1,128)S(1)}, f32[1,768]{1,0:T(1,128)}, u32[]{:S(2)}) copy-start(f32[1,768]{1,0:T(1,128)} %get-tuple-element.74) | copy-start | bytes 9220

commit v3 on v2

--- a/solution.py
+++ b/solution.py
@@ -13,6 +13,7 @@
 ROT = 16
 TISSUES = 16
 ROWS = 256
+UNIT = 128
 LANES = 128
 EPS = 1e-05
 MESH = pl.DeviceIdType.MESH
@@ -44,17 +45,6 @@
     sines[:, half:ROT] = np.sin(angles)
     tables = np.stack([np.tile(item, (1, LANES // HEAD)) for item in (cosines, sines)])
     return tables.astype(np.float32)
-
-
-def unpack_rows(packed, heads):
-    width = packed.shape[-1]
-    split = packed.reshape(3, heads, HEAD, width)
-    return split.transpose(3, 1, 0, 2).reshape(width, 3 * heads * HEAD)
-
-
-def unpack_line(line, heads):
-    split = line.reshape(3, -1)[:, : heads * HEAD].reshape(3, heads, HEAD)
-    return split.transpose(1, 0, 2).reshape(1, 3 * heads * HEAD)
 
 
 def normalise(value):
@@ -78,12 +68,12 @@
     out_cols,
     grad_cols,
     grads,
+    lines,
     small,
     wq,
     wd,
     w1,
     w2,
-    raw,
     vec,
     chain,
     qkv,
@@ -93,8 +83,11 @@
     key_grad,
     value_grad,
     part,
+    late_part,
     got,
     met,
+    late_got,
+    late_met,
     total,
     half_got,
     first_got,
@@ -118,17 +111,22 @@
     tally_send,
     tally_recv,
     store_sem,
+    free_sem,
 ):
     section = lax.axis_index("section")
     replica = lax.axis_index("dp")
     place = lax.axis_index("tensor")
     copies = lax.axis_size("dp")
     bits = copies.bit_length() - 1
-    chunks, rows, width = part.shape
+    _, chunks, rows, width = chain.shape
+    unit = part.shape[1]
+    halves = rows // unit
+    units = chunks * halves
+    half_width = late_met.shape[-1]
     lanes = wd.shape[1]
     valid = heads * HEAD
-    padded = out_cols.shape[-1]
-    columns = width // lax.axis_size("tensor")
+    columns = out_cols.shape[1]
+    padded = -(-columns // LANES) * LANES
     inner = jnp.logical_and(place > 0, place < 3)
     outer = jnp.logical_not(inner)
     beside = place + 1 - 2 * lax.rem(place, 2)
@@ -157,38 +155,46 @@
     for friend in friends:
         pl.semaphore_signal(barrier, inc=1, device_id=friend, device_id_type=MESH)
 
-    raw_load = pltpu.make_async_copy(wq_in, raw, load_sem.at[0])
-    raw_load.start()
-    input_load = pltpu.make_async_copy(x_in.at[section], chain.at[0], load_sem.at[1])
+    input_load = pltpu.make_async_copy(x_in.at[section], chain.at[0], load_sem.at[0])
     input_load.start()
-    pairs = ((w1_in, w1.at[section]), (wd_in, wd.at[section, :valid]), (w2_in, w2.at[section]))
+    pairs = []
+    for part_index in range(3):
+        for h in range(heads):
+            source = slice((3 * h + part_index) * HEAD, (3 * h + part_index + 1) * HEAD)
+            goal = slice(part_index * lanes + h * HEAD, part_index * lanes + (h + 1) * HEAD)
+            pairs.append((wq_in.at[source], wq.at[section, goal]))
+    pairs += [(w1_in, w1.at[section]), (wd_in, wd.at[section, :valid]), (w2_in, w2.at[section])]
     loads = [
-        pltpu.make_async_copy(source, goal, load_sem.at[2 + index])
+        pltpu.make_async_copy(source, goal, load_sem.at[4 + index])
         for index, (source, goal) in enumerate(pairs)
     ]
     for item in loads:
         item.start()
-    target_load = pltpu.make_async_copy(target_in.at[section], chain.at[3], load_sem.at[5])
+    target_load = pltpu.make_async_copy(target_in.at[section], chain.at[2], load_sem.at[3])
     target_load.start()
 
-    column = lax.broadcasted_iota(jnp.int32, (3 * valid, 3 * lanes), 0)
-    head_of, rest = column // (3 * HEAD), lax.rem(column, 3 * HEAD)
-    goal_of = (rest // HEAD) * lanes + head_of * HEAD + lax.rem(rest, HEAD)
-    pack = (goal_of == lax.broadcasted_iota(jnp.int32, goal_of.shape, 1)).astype(BF16)
     for index, item in enumerate(vec_in):
         vec[section, index : index + 1] = item[...].astype(F32)
     vec[section, 4:5] = vec_in[4][...].astype(F32) + vec_in[5][...].astype(F32)
-    vec[section, 5:6] = dot_nn(jnp.broadcast_to(qkv_bias[...], (16, 3 * valid)), pack)[0:1]
+    line = qkv_bias[...].astype(F32)
+    gap = [jnp.zeros((1, lanes - valid), F32)] if lanes > valid else []
+    packed = []
+    for part_index in range(3):
+        for h in range(heads):
+            packed.append(line[:, (3 * h + part_index) * HEAD : (3 * h + part_index + 1) * HEAD])
+        packed += gap
+    vec[section, 5:6] = jnp.concatenate(packed, axis=1)
     vec[section, 7:8] = jnp.zeros((1, width), F32)
     for layer in range(2):
         wd[layer, valid:] = jnp.zeros((lanes - valid, width), BF16)
-    raw_load.wait()
-    wq[section] = dot_nn(raw[...], pack).astype(BF16)
+        for part_index in range(3):
+            pad = slice(part_index * lanes + valid, (part_index + 1) * lanes)
+            wq[layer, pad] = jnp.zeros((lanes - valid, width), BF16)
     pl.semaphore_wait(barrier, len(friends))
     gifts = [
         send(source, goal, (give_sem.at[index], take_sem.at[index]), twin)
         for index, (source, goal) in enumerate(
-            ((wq.at[section], wq.at[section]), (vec.at[section], vec.at[section])) + pairs
+            [(vec.at[section], vec.at[section])] + pairs
         )
     ]
     for item in gifts:
@@ -237,19 +243,28 @@
     def only(mask, value):
         return jnp.where(mask, value, jnp.zeros_like(value))
 
+    def put(goal, slot, value):
+        for half in range(halves):
+            piece = value[half * unit : (half + 1) * unit]
+            goal[slot * halves + half] = piece.astype(BF16)
+
     def forward_chunk(layer, c):
         start = c * rows
         here = slice(start, start + rows)
+        if c == 0:
+            need(0, 1 + projection, layer)
         spread, _ = normalise(chain[layer, c].astype(F32))
         first = (spread * vec[layer, 0:1] + vec[layer, 1:2]).astype(BF16)
         second = (spread * vec[layer, 2:3] + vec[layer, 3:4]).astype(BF16)
-        projected = dot_nn(first, wq[layer]) + vec[layer, 5:6]
+        projected = dot_nt(first, wq[layer]) + vec[layer, 5:6]
         query = turn(projected[:, :lanes], start).astype(BF16)
         qkv[layer, here, :lanes] = query
         qkv[layer, here, lanes : 2 * lanes] = turn(projected[:, lanes : 2 * lanes], start).astype(
             BF16
         )
         qkv[layer, here, 2 * lanes :] = projected[:, 2 * lanes :].astype(BF16)
+        if c == 0:
+            need(1 + projection, 2 + projection, layer)
         pre = dot_nn(second, w1[layer]) + vec[layer, 6:7]
         below = 0.5 * (1.0 + lax.erf(pre * (0.5**0.5)))
         active = (pre * below).astype(BF16)
@@ -284,7 +299,11 @@
             context = jnp.where(head_masks[h], mixed, context)
         context = context.astype(BF16)
         ctx[layer, here, :] = context
-        part[c] = (dot_nn(context, wd[layer]) + dot_nn(active, w2[layer])).astype(BF16)
+        if c == 0:
+            need(2 + projection, 4 + projection, layer)
+        result = (dot_nn(context, wd[layer]) + dot_nn(active, w2[layer])).astype(BF16)
+        for index, goal in enumerate((part, late_part)):
+            pl.when(layer == index)(functools.partial(put, goal, c, result))
 
     def backward_chunk(layer, c):
         start = c * rows
@@ -292,7 +311,7 @@
         here = slice(start, stop)
         first_turn = c == chunks - 1
         slot = chunks - 1 - c
-        cotangent = chain[4 - layer, c]
+        cotangent = chain[3 - layer, c]
         context_grad = dot_nt(cotangent, wd[layer]).astype(BF16)
         pre_grad = (dot_nt(cotangent, w2[layer]) * gate[layer, here, :].astype(F32)).astype(BF16)
         gate[layer, here, :] = pre_grad
@@ -327,7 +346,7 @@
         qkv[layer, here, lanes : 2 * lanes] = turn_back(key_grad[here], start).astype(BF16)
         qkv[layer, here, 2 * lanes :] = value_grad[here].astype(BF16)
         projected_grad = qkv[layer, here, :]
-        first_back = dot_nt(projected_grad, wq[layer])
+        first_back = dot_nn(projected_grad, wq[layer])
         spread, rstd = normalise(chain[layer, c].astype(F32))
         first = (spread * vec[layer, 0:1] + vec[layer, 1:2]).astype(BF16)
         second = (spread * vec[layer, 2:3] + vec[layer, 3:4]).astype(BF16)
@@ -351,26 +370,31 @@
         back = first_back * vec[layer, 0:1] + second_back * vec[layer, 2:3]
         middle = jnp.mean(back, axis=-1, keepdims=True)
         tilt = jnp.mean(back * spread, axis=-1, keepdims=True)
-        part[slot] = (rstd * (back - middle - spread * tilt)).astype(BF16)
+        put(part, slot, rstd * (back - middle - spread * tilt))
         return here, first_turn, first, second, pre_grad, cotangent
 
     def add_weight_grads(layer, here, first_turn, first, second, pre_grad, cotangent):
         step = lanes
-        base = 0
-        sources = (
-            (qkv.at[layer, here], first, valid),
-            (second, pre_grad, step),
-            (act.at[layer, here], cotangent, step),
-            (ctx.at[layer, here], cotangent, valid),
-        )
-        for left, right, kept in sources:
-            for at in range(0, left.shape[-1], step):
-                piece = dot_tn(left[:, at : at + step], right)[:kept]
-                goal = slice(base, base + kept)
-                if not first_turn:
-                    piece = piece + total[layer, goal].astype(F32)
-                total[layer, goal] = piece.astype(BF16)
-                base += kept
+
+        def add(start, piece):
+            goal = slice(start, start + piece.shape[0])
+            if not first_turn:
+                piece = piece + total[layer, goal].astype(F32)
+            total[layer, goal] = piece.astype(BF16)
+
+        for part_index in range(3):
+            at = part_index * lanes
+            piece = dot_tn(qkv[layer, here, at : at + lanes], first)
+            for h in range(heads):
+                add((3 * h + part_index) * HEAD, piece[h * HEAD : (h + 1) * HEAD])
+        base = 3 * valid
+        for at in range(0, width, step):
+            add(base + at, dot_tn(second[:, at : at + step], pre_grad))
+        base += width
+        for at in range(0, act.shape[-1], step):
+            add(base + at, dot_tn(act[layer, here, at : at + step], cotangent))
+        base += act.shape[-1]
+        add(base, dot_tn(ctx[layer, here], cotangent)[:valid])
 
     all_rows = total.shape[1]
     share_rows = all_rows // 2
@@ -444,6 +468,9 @@
 
     def sum_start(layer, step):
         if step < sum_steps - 1:
+            if isinstance(layer, int) and layer == 0 and 1 <= step <= folds:
+                for group in range(2):
+                    pl.semaphore_wait(free_sem.at[step - 1, group], 1)
             for item in sum_copies(layer, step):
                 item.start()
             return
@@ -486,6 +513,11 @@
                 add_rows(goal, sums_of(layer, start, size), second_got.at[group])
             else:
                 add_rows(goal, goal, more_got.at[layer, step - 1 - folds, group])
+            if layer == 1 and step <= folds:
+                mate = mates[steps[step - 1][0]]
+                pl.semaphore_signal(
+                    free_sem.at[step - 1, group], inc=1, device_id=mate, device_id_type=MESH
+                )
 
     line_friends = [twin] + mates + [near, far]
 
@@ -500,107 +532,162 @@
         else:
             small[:, 0:4] += line_got[step, :, 0:4]
 
-    def locate(turn_index):
-        kind = turn_index // chunks
-        slot = lax.rem(turn_index, chunks)
-        row = jnp.where(kind < 2, slot, chunks - 1 - slot)
-        base = kind + jnp.where(kind < 2, 0, 1)
-        goal = jnp.where(kind == 3, 3, base + 1)
-        return kind, slot, row, base, goal
-
-    def hop(stage, slot, source, goal, target):
-        return pltpu.make_async_remote_copy(
-            src_ref=source,
-            dst_ref=goal,
-            send_sem=hop_send.at[stage, slot],
-            recv_sem=hop_recv.at[stage, slot],
-            device_id=target,
-            device_id_type=MESH,
-        )
-
-    def first_hop(slot):
-        return hop(0, slot, part.at[slot], got.at[slot], near)
-
-    def second_hop(slot):
-        return hop(1, slot, part.at[slot], met.at[slot], far)
-
-    def third_hop(slot, row, goal):
-        piece = chain.at[goal, row]
-        return hop(2, slot, piece, piece, near)
-
-    def launch(turn_index):
-        _, slot, _, _, _ = locate(turn_index)
-
+    low_side = place < 2
+    own_half = pl.multiple_of(jnp.where(low_side, 0, half_width), LANES)
+    other_half = pl.multiple_of(jnp.where(low_side, half_width, 0), LANES)
+    window = place * columns // LANES * LANES
+    window = pl.multiple_of(window, LANES)
+    end_window = pl.multiple_of(jnp.where(low_side, 0, width - padded), LANES)
+
+    sent_width = width - LANES
+    sent_lanes = pl.ds(pl.multiple_of(jnp.where(low_side, LANES, 0), LANES), sent_width)
+
+    def spot(kind, u):
+        chunk = u // halves if kind < 2 else chunks - 1 - u // halves
+        return chunk, slice(u % halves * unit, (u % halves + 1) * unit)
+
+    def buffers(kind, u):
+        if kind == 1:
+            return late_part.at[u], late_got.at[u], late_met.at[u]
+        return part.at[u], got.at[u], met.at[u] if kind != 3 else met.at[u, :, :half_width]
+
+    def hop_sems(kind, stage, u):
+        return hop_send.at[int(kind == 1), stage, u], hop_recv.at[int(kind == 1), stage, u]
+
+    def first_hop(kind, u):
+        own, landing, _ = buffers(kind, u)
+        if kind in (1, 3):
+            own, landing = own.at[:, sent_lanes], landing.at[:, :sent_width]
+        return send(own, landing, hop_sems(kind, 0, u), near)
+
+    def second_hop(kind, u):
+        own, _, landing = buffers(kind, u)
+        if kind in (1, 3):
+            own = own.at[:, pl.ds(other_half, half_width)]
+        return send(own, landing, hop_sems(kind, 1, u), far)
+
+    def third_hop(kind, u):
+        own, _, landing = buffers(kind, u)
+        if kind in (1, 3):
+            own, landing = own.at[:, pl.ds(end_window, padded)], landing.at[:, :padded]
+        else:
+            chunk, here = spot(kind, u)
+            own = landing = chain.at[kind + 1, chunk, here]
+        return send(own, landing, hop_sems(kind, 2, u), near)
+
+    def by_rows(count, work, step=32):
+        def turn_rows(index, carry):
+            work(pl.ds(pl.multiple_of(index * step, step), step))
+            return carry
+
+        lax.fori_loop(0, count // step, turn_rows, 0)
+
+    def launch(kind, c):
         @pl.when(outer)
         def _():
-            first_hop(slot).start()
-
-    def meet(turn_index):
-        _, slot, _, _, _ = locate(turn_index)
-
+            for half in range(halves):
+                first_hop(kind, c * halves + half).start()
+
+    def meet(kind, u):
         @pl.when(inner)
         def _():
-            first_hop(slot).wait_recv()
-            part[slot] = (part[slot].astype(F32) + got[slot].astype(F32)).astype(BF16)
-            second_hop(slot).start()
-
-    def settle(turn_index):
-        kind, slot, row, base, goal = locate(turn_index)
+            first_hop(kind, u).wait_recv()
+            own, landed, _ = buffers(kind, u)
+            if kind in (1, 3):
+                own, landed = own.at[:, sent_lanes], landed.at[:, :sent_width]
+
+            def add(here):
+                own[here] = (own[here].astype(F32) + landed[here].astype(F32)).astype(BF16)
+
+            by_rows(unit, add)
+            second_hop(kind, u).start()
+
+    def settle(kind, u):
+        chunk, here = spot(kind, u)
 
         @pl.when(inner)
         def _():
-            second_hop(slot).wait_recv()
-            keep = jnp.where(kind < 2, 1.0, 0.0)
-            shift = vec[jnp.minimum(kind, 1), 4:5] * keep
-            total = part[slot].astype(F32) + met[slot].astype(F32)
-            chain[goal, row] = (chain[base, row].astype(F32) + (total + shift)).astype(BF16)
-            third_hop(slot, row, goal).start()
-
-    def finish(turn_index):
-        _, slot, row, _, goal = locate(turn_index)
-
+            second_hop(kind, u).wait_recv()
+            own, _, landed = buffers(kind, u)
+            if kind in (1, 3):
+                lanes_here = pl.ds(own_half, half_width)
+                goal = own.at[:, lanes_here]
+                source = goal
+                base = chain.at[kind, chunk, here, lanes_here]
+            else:
+                lanes_here = slice(None)
+                goal = chain.at[kind + 1, chunk, here]
+                source = own
+                base = chain.at[kind, chunk, here]
+
+            def add(at):
+                value = source[at].astype(F32) + landed[at].astype(F32) + base[at].astype(F32)
+                if kind < 2:
+                    value = value + vec[kind, 4:5, lanes_here]
+                goal[at] = value.astype(BF16)
+
+            by_rows(unit, add)
+            if kind > 1:
+                third_hop((0, 2)[kind - 2], u).wait_send()
+            third_hop(kind, u).start()
+
+    def arrive(kind, c):
         @pl.when(outer)
         def _():
-            first_hop(slot).wait_send()
-            third_hop(slot, row, goal).wait_recv()
-
-        @pl.when(inner)
-        def _():
-            second_hop(slot).wait_send()
-            third_hop(slot, row, goal).wait_send()
-
-    def need(index, layer):
+            for half in range(halves):
+                third_hop(kind, c * halves + half).wait_recv()
+
+    def release(kind, c):
+        for half in range(halves):
+            u = c * halves + half
+            pl.when(outer)(first_hop(kind, u).wait_send)
+            pl.when(inner)(second_hop(kind, u).wait_send)
+
+    def let_go(kind):
+        for u in range(units):
+            pl.when(inner)(third_hop(kind, u).wait_send)
+
+    def serve(kind, meets, settles):
+        for index in range(max(len(meets), len(settles))):
+            if index < len(meets):
+                meet(kind, meets[index])
+            if index < len(settles):
+                settle(kind, settles[index])
+
+    projection = 3 * heads
+
+    def need(first, last, layer):
         @pl.when(section == layer)
         def _():
-            if index > 1:
-                loads[index - 2].wait()
+            for index in range(max(first, 1), last):
+                loads[index - 1].wait()
 
         @pl.when(section != layer)
         def _():
-            gifts[index].wait_recv()
+            for index in range(first, last):
+                gifts[index].wait_recv()
 
     input_load.wait()
 
+    forward_turns = (
+        (((), ()), ((), ()), ((0,), ()), ((1, 2, 3), (0, 1, 2))),
+        (((4,), (3,)), ((5, 6), (4, 5)), ((7,), (6, 7)), ((), ())),
+    )
+
     def forward_layer(layer, carry):
-        for index in range(len(gifts)):
-            need(index, layer)
         for c in range(chunks):
-            now = layer * chunks + c
-
-            @pl.when(layer > 0)
-            def _():
-                finish(now - chunks)
-
+            pl.when(layer == 1)(functools.partial(arrive, 0, c))
             forward_chunk(layer, c)
-            launch(now)
-
-            @pl.when(now > 0)
-            def _():
-                meet(now - 1)
-
-            @pl.when(now > 1)
-            def _():
-                settle(now - 2)
+            pl.when(layer == 0)(functools.partial(launch, 0, c))
+            for index in range(2):
+                pl.when(layer == index)(functools.partial(serve, 0, *forward_turns[index][c]))
+
+            if c == 2:
+
+                @pl.when(layer == 1)
+                def _():
+                    launch(1, 0)
+                    launch(1, 1)
 
             for bit in range(bits):
                 if bit % chunks == c:
@@ -612,90 +699,190 @@
     own_mark = jnp.where(section == 0, marks[0], marks[1])[0:1]
     own_count = jnp.sum(own_mark * tally[0:1], axis=-1, keepdims=True)
     share = (tissue.shape[0] * copies / TISSUES) / own_count
-    for c in range(chunks):
-        chain[3, c] = (share * chain[3, c].astype(F32)).astype(BF16)
+    gifts[0].wait_send()
+    vec[0, 7:8] = jnp.broadcast_to(share, (1, width))
+
+    def weigh(c, carry):
+        chain[2, c] = (vec[0, 7:8] * chain[2, c].astype(F32)).astype(BF16)
+        return carry
+
+    lax.fori_loop(0, chunks, weigh, 0)
+
+    backward_turns = (
+        (
+            ((1, (0, 1), ()),),
+            ((1, (2, 3), (0, 1)),),
+            ((1, (), (2, 3)), (2, (0,), ())),
+            ((2, (1, 2), (0, 1)),),
+        ),
+        (
+            ((2, (3, 4), (2, 3)),),
+            ((2, (5, 6), (4, 5)),),
+            ((2, (7,), (6, 7)),),
+            ((3, (0, 1), (0,)),),
+        ),
+    )
+
+    def serve_all(turns):
+        for item in turns:
+            serve(*item)
+
+    early_sums = ((0, None), (None, 1), (None, 2), (3, None))
+
+    def move_sum(step):
+        if step is not None:
+            sum_end(1, step)
+            sum_start(1, step + 1)
 
     def backward_layer(turn_index, carry):
         layer = 1 - turn_index
         for at in range(chunks):
-            now = (2 + turn_index) * chunks + at
-            if at == 0:
+            now = early_sums[at]
+
+            @pl.when(layer == 0)
+            def _():
+                arrive(2, at)
+                release(2, at)
+                move_sum(now[0])
+
+            pl.when(layer == 1)(functools.partial(release, 0, at))
+            kept = backward_chunk(layer, chunks - 1 - at)
+            for index in range(2):
+                pl.when(turn_index == index)(functools.partial(launch, 2 + index, at))
+            add_weight_grads(layer, *kept)
+            if at == chunks - 1:
+                sum_start(layer, 0)
 
                 @pl.when(layer == 0)
                 def _():
-                    sum_end(1, 0)
-                    sum_start(1, 1)
-
-            finish(now - chunks)
+                    launch(1, 2)
+                    launch(1, 3)
 
             @pl.when(layer == 0)
             def _():
-                sum_end(1, at + 1)
-                sum_start(1, at + 2)
-
-            kept = backward_chunk(layer, chunks - 1 - at)
-            launch(now)
-            add_weight_grads(layer, *kept)
-            meet(now - 1)
-            settle(now - 2)
-
-        sum_start(layer, 0)
+                if at == 1:
+                    move_sum(now[1])
+
+            for index in range(2):
+                pl.when(turn_index == index)(
+                    functools.partial(serve_all, backward_turns[index][at])
+                )
+
+            @pl.when(layer == 0)
+            def _():
+                if at == 2:
+                    move_sum(now[1])
+
         return carry
 
     lax.fori_loop(0, 2, backward_layer, 0)
-    last = 4 * chunks
-    line_copy(0).start()
-    meet(last - 1)
-    settle(last - 2)
-    for step in range(chunks + 1, sum_steps - 1):
-        sum_end(1, step)
-        sum_start(1, step + 1)
-    for step in range(max(sum_steps, len(line_friends))):
+
+    shift = lax.rem(place * columns, LANES)
+
+    def staged(index, layer):
+        return probs[-1].at[layer, index, :columns]
+
+    def stage(index, layer, row, value):
+        turned_value = value.astype(F32).T
+        low = turned_value[:columns]
+        high = turned_value[LANES // 2 : LANES // 2 + columns]
+        goal = pl.ds(pl.multiple_of(row, unit), unit)
+        staged(index, layer)[:, goal] = jnp.where(shift == 0, low, high).astype(BF16)
+
+    def stage_whole(index, layer, kind):
+        def stage_unit(u, carry):
+            rows_here = pl.ds(pl.multiple_of(lax.rem(u, halves) * unit, unit), unit)
+            source = chain.at[kind + 1, u // halves, rows_here, pl.ds(window, padded)]
+            stage(index, layer, u * unit, source[...])
+            return carry
+
+        lax.fori_loop(0, units, stage_unit, 0)
+
+    def stage_own(index, layer, kind):
+        for c in range(chunks):
+            arrive(kind, c)
+            release(kind, c)
+        let_go(kind)
+        tile = lax.broadcasted_iota(jnp.int32, (1, padded), 1) // LANES
+        unsent = tile == jnp.where(low_side, 0, padded // LANES - 1)
+        store, landing = (late_part, late_met) if kind == 1 else (part, met)
+
+        def stage_unit(u, carry):
+            chunk = u // halves if kind == 1 else chunks - 1 - u // halves
+            row = chunk * rows + lax.rem(u, halves) * unit
+
+            @pl.when(outer)
+            def _():
+                mine = store[u, :, pl.ds(end_window, padded)]
+                value = landing[u, :, :padded].astype(F32) + only(unsent, mine.astype(F32))
+                stage(index, layer, row, value)
+
+            @pl.when(inner)
+            def _():
+                stage(index, layer, row, store[u, :, pl.ds(window, padded)])
+
+            return carry
+
+        lax.fori_loop(0, units, stage_unit, 0)
+
+    def swap_columns(index, goal):
+        sems = (swap_send.at[index], swap_recv.at[index])
+        return [
+            send(staged(index, 1 - section), goal.at[section], sems, twin),
+            pltpu.make_async_copy(staged(index, section), goal.at[section], load_sem.at[1 + index]),
+        ]
+
+    def sum_next(step):
         if step < sum_steps:
             sum_end(0, step)
             if step + 1 < sum_steps:
                 sum_start(0, step + 1)
+
+    def line_next(step):
         if step < len(line_friends):
             line_end(step)
             if step + 1 < len(line_friends):
                 line_copy(step + 1).start()
-        if step == 0:
-            settle(last - 1)
-            sum_end(1, sum_steps - 1)
-    for at in range(chunks):
-        finish(last - chunks + at)
-
-    own_column = lax.broadcasted_iota(jnp.int32, (width, padded), 1)
-    pick = jnp.logical_and(
-        lax.broadcasted_iota(jnp.int32, (width, padded), 0) == own_column + place * columns,
-        own_column < columns,
-    ).astype(BF16)
-
-    def narrow(index, goal):
-        def narrow_chunk(c, carry):
-            here = pl.ds(pl.multiple_of(c * rows, rows), rows)
-            goal[here] = dot_nn(chain[index, c], pick).astype(BF16)
-            return carry
-
-        lax.fori_loop(0, chunks, narrow_chunk, 0)
-
-    goals = (out_cols, grad_cols)
-    away = [qkv.at[0, :, index * padded : (index + 1) * padded] for index in range(2)]
-    home = [qkv.at[1, :, index * padded : (index + 1) * padded] for index in range(2)]
-    moves = []
-    for index, goal in enumerate(goals):
-        narrow((2 - section, 4 - section)[index], away[index])
-        sems = (swap_send.at[index], swap_recv.at[index])
-        moves.append(send(away[index], goal.at[section], sems, twin))
-        moves[-1].start()
-        narrow((1 + section, 3 + section)[index], home[index])
-        moves.append(
-            pltpu.make_async_copy(home[index], goal.at[section], load_sem.at[1 + index])
-        )
-        moves[-1].start()
+
+    line_copy(0).start()
+    sum_next(0)
+    line_next(0)
+    serve(3, (2, 3), (1, 2))
+    stage_whole(0, 0, 0)
+    stage_whole(1, 1, 2)
+    serve(3, (4, 5), (3, 4))
+    for step in range(chunks, sum_steps - 1):
+        sum_end(1, step)
+        sum_start(1, step + 1)
+    sum_next(1)
+    line_next(1)
+    serve(3, (6, 7), (5, 6))
+    sum_next(2)
+    line_next(2)
+    settle(3, 7)
+    sum_end(1, sum_steps - 1)
+    meet(1, 4)
+    sum_next(3)
+    line_next(3)
+    stage_own(1, 0, 3)
+    moves = swap_columns(1, grad_cols)
     for item in moves:
+        item.start()
+    serve(1, (5, 6, 7), (4, 5, 6))
+    sum_next(4)
+    line_next(4)
+    settle(1, 7)
+    stage_own(0, 1, 1)
+    late_moves = swap_columns(0, out_cols)
+    for item in late_moves:
+        item.start()
+    for step in range(5, max(sum_steps, len(line_friends))):
+        sum_next(step)
+        line_next(step)
+    lines[...] = small[section]
+    for item in moves + late_moves:
         item.wait()
-    for item in gifts:
+    for item in gifts[1:]:
         item.wait_send()
 
 
@@ -704,70 +891,85 @@
     count, seq_len, width = x.shape
     rows = min(ROWS, seq_len)
     chunks = seq_len // rows
+    unit = min(UNIT, rows)
+    pieces = seq_len // unit
     valid = wd.shape[0]
     heads = valid // HEAD
     lanes = -(-valid // LANES) * LANES
     units = w1.shape[1]
-    columns = -(-width // lax.axis_size("tensor") // LANES) * LANES
+    columns = width // lax.axis_size("tensor")
     bits = lax.axis_size("dp").bit_length() - 1
     tables = jnp.asarray(rotary_tables(seq_len))
     total_rows = 3 * valid + width + units + valid
     hbm = pl.BlockSpec(memory_space=pl.ANY)
     vmem = pl.BlockSpec(memory_space=pltpu.VMEM)
     smem = pl.BlockSpec(memory_space=pltpu.SMEM)
+    scratch = [
+        pltpu.VMEM((2, 8, width), F32),
+        pltpu.VMEM((2, 3 * lanes, width), BF16),
+        pltpu.VMEM((2, lanes, width), BF16),
+        pltpu.VMEM((2,) + w1.shape, BF16),
+        pltpu.VMEM((2,) + w2.shape, BF16),
+        pltpu.VMEM((2, 8, width), F32),
+        pltpu.VMEM((4, chunks, rows, width), BF16),
+        pltpu.VMEM((2, seq_len, 3 * lanes), BF16),
+        pltpu.VMEM((2, seq_len, lanes), BF16),
+        pltpu.VMEM((2, seq_len, units), BF16),
+        pltpu.VMEM((2, seq_len, units), BF16),
+        pltpu.VMEM((seq_len, lanes), F32),
+        pltpu.VMEM((seq_len, lanes), F32),
+        pltpu.VMEM((pieces, unit, width), BF16),
+        pltpu.VMEM((pieces, unit, width), BF16),
+        pltpu.VMEM((pieces, unit, width), BF16),
+        pltpu.VMEM((pieces, unit, width), BF16),
+        pltpu.VMEM((pieces, unit, width - LANES), BF16),
+        pltpu.VMEM((pieces, unit, width // 2), BF16),
+        pltpu.VMEM((2, total_rows, width), BF16),
+        pltpu.VMEM((2, total_rows // 2, width), BF16),
+        pltpu.VMEM((2, total_rows // 8, width), BF16),
+        pltpu.VMEM((2, total_rows // 16, width), BF16),
+        pltpu.VMEM((2, max(bits - 2, 1), 2, total_rows // 16 if bits > 2 else 16, width), BF16),
+        pltpu.VMEM((3 + bits, 2, 8, width), F32),
+        pltpu.VMEM((8, LANES), F32),
+        pltpu.VMEM((max(bits, 1), 8, LANES), F32),
+    ]
+    probs = [pltpu.VMEM((2, heads, rows, (c + 1) * rows), BF16) for c in range(chunks)]
+    semaphores = [
+        pltpu.SemaphoreType.DMA((4 + 3 * heads + 3,)),
+        pltpu.SemaphoreType.DMA((4 + 3 * heads,)),
+        pltpu.SemaphoreType.DMA((4 + 3 * heads,)),
+        pltpu.SemaphoreType.DMA((2, 3, pieces)),
+        pltpu.SemaphoreType.DMA((2, 3, pieces)),
+        pltpu.SemaphoreType.DMA((2,)),
+        pltpu.SemaphoreType.DMA((2,)),
+        pltpu.SemaphoreType.DMA((2, bits + 4, 2)),
+        pltpu.SemaphoreType.DMA((2, bits + 4, 2)),
+        pltpu.SemaphoreType.DMA((3 + bits,)),
+        pltpu.SemaphoreType.DMA((3 + bits,)),
+        pltpu.SemaphoreType.DMA((max(bits, 1),)),
+        pltpu.SemaphoreType.DMA((max(bits, 1),)),
+        pltpu.SemaphoreType.DMA((2,)),
+        pltpu.SemaphoreType.REGULAR((2, 2)),
+    ]
+
+    def body(*refs):
+        ends = np.cumsum([9, len(vec), 4 + len(scratch), chunks])
+        head, lines, main, kept = (
+            refs[start:stop] for start, stop in zip([0, *ends[:-1]], ends, strict=True)
+        )
+        train_kernel(heads, *head, lines, *main, kept, *refs[ends[-1] :])
+
     return pl.pallas_call(
-        functools.partial(gather_refs, heads, chunks, len(vec)),
+        body,
         out_shape=(
-            jax.ShapeDtypeStruct((count, seq_len, columns), BF16),
-            jax.ShapeDtypeStruct((count, seq_len, columns), BF16),
+            jax.ShapeDtypeStruct((count, columns, seq_len), BF16),
+            jax.ShapeDtypeStruct((count, columns, seq_len), BF16),
             jax.ShapeDtypeStruct((total_rows, width), BF16),
-            jax.ShapeDtypeStruct((2, 8, width), F32),
+            jax.ShapeDtypeStruct((8, width), F32),
         ),
         in_specs=[hbm, hbm, smem, vmem, hbm, hbm, hbm, hbm, vmem] + [vmem] * len(vec),
         out_specs=(hbm, hbm, hbm, vmem),
-        scratch_shapes=[
-            pltpu.VMEM((2, width, 3 * lanes), BF16),
-            pltpu.VMEM((2, lanes, width), BF16),
-            pltpu.VMEM((2,) + w1.shape, BF16),
-            pltpu.VMEM((2,) + w2.shape, BF16),
-            pltpu.VMEM(wq.shape, BF16),
-            pltpu.VMEM((2, 8, width), F32),
-            pltpu.VMEM((5, chunks, rows, width), BF16),
-            pltpu.VMEM((2, seq_len, 3 * lanes), BF16),
-            pltpu.VMEM((2, seq_len, lanes), BF16),
-            pltpu.VMEM((2, seq_len, units), BF16),
-            pltpu.VMEM((2, seq_len, units), BF16),
-            pltpu.VMEM((seq_len, lanes), F32),
-            pltpu.VMEM((seq_len, lanes), F32),
-            pltpu.VMEM((chunks, rows, width), BF16),
-            pltpu.VMEM((chunks, rows, width), BF16),
-            pltpu.VMEM((chunks, rows, width), BF16),
-            pltpu.VMEM((2, total_rows, width), BF16),
-            pltpu.VMEM((2, total_rows // 2, width), BF16),
-            pltpu.VMEM((2, total_rows // 8, width), BF16),
-            pltpu.VMEM((2, total_rows // 16, width), BF16),
-            pltpu.VMEM((2, max(bits - 2, 1), 2, total_rows // 16 if bits > 2 else 16, width), BF16),
-            pltpu.VMEM((3 + bits, 2, 8, width), F32),
-            pltpu.VMEM((8, LANES), F32),
-            pltpu.VMEM((max(bits, 1), 8, LANES), F32),
-        ]
-        + [pltpu.VMEM((2, heads, rows, (c + 1) * rows), BF16) for c in range(chunks)]
-        + [
-            pltpu.SemaphoreType.DMA((6,)),
-            pltpu.SemaphoreType.DMA((5,)),
-            pltpu.SemaphoreType.DMA((5,)),
-            pltpu.SemaphoreType.DMA((3, chunks)),
-            pltpu.SemaphoreType.DMA((3, chunks)),
-            pltpu.SemaphoreType.DMA((2,)),
-            pltpu.SemaphoreType.DMA((2,)),
-            pltpu.SemaphoreType.DMA((2, bits + 4, 2)),
-            pltpu.SemaphoreType.DMA((2, bits + 4, 2)),
-            pltpu.SemaphoreType.DMA((3 + bits,)),
-            pltpu.SemaphoreType.DMA((3 + bits,)),
-            pltpu.SemaphoreType.DMA((max(bits, 1),)),
-            pltpu.SemaphoreType.DMA((max(bits, 1),)),
-            pltpu.SemaphoreType.DMA((2,)),
-        ],
+        scratch_shapes=scratch + probs + semaphores,
         compiler_params=pltpu.CompilerParams(
             collective_id=0, has_side_effects=True, vmem_limit_bytes=63 * 2**20
         ),
@@ -785,11 +987,59 @@
     )
 
 
-def gather_refs(heads, chunks, lines, *refs):
-    ends = (9, 9 + lines, 9 + lines + 4 + 24)
-    probs = refs[ends[2] : ends[2] + chunks]
-    head, vec, body = refs[: ends[0]], refs[ends[0] : ends[1]], refs[ends[1] : ends[2]]
-    train_kernel(heads, *head, vec, *body, probs, *refs[ends[2] + chunks :])
+def widen_kernel(heads, cols, grad_cols, *refs):
+    sources, lines = refs[:4], refs[4]
+    out_cols, out_grad_cols, *goals = refs[5:]
+    out_cols[...] = cols[...]
+    out_grad_cols[...] = grad_cols[...].astype(F32)
+    for source, goal in zip(sources, goals[:4], strict=True):
+        goal[...] = source[...].astype(F32)
+    for index, goal in zip((0, 1, 2, 3, 5, 6), goals[4:10], strict=True):
+        goal[...] = lines[index : index + 1]
+    line = lines[4:5]
+    lanes = line.shape[1] // 3
+    pieces = []
+    for h in range(heads):
+        for part_index in range(3):
+            start = part_index * lanes + h * HEAD
+            pieces.append(line[:, start : start + HEAD])
+    goals[10][...] = jnp.concatenate(pieces, axis=1)
+
+
+def widen(out_cols, grad_cols, total, lines, heads, units):
+    steps = 4
+    count, columns, seq_len = out_cols.shape
+    width = total.shape[1]
+    sizes = (3 * heads * HEAD, width, units, heads * HEAD)
+    starts = [0, *np.cumsum(sizes[:-1]).tolist()]
+    col_spec = pl.BlockSpec((count, columns // steps, seq_len), lambda i: (0, i, 0))
+
+    def rows_from(start, size):
+        block = size // steps
+        return pl.BlockSpec((block, width), lambda i: (start // block + i, 0))
+
+    def line_spec(lanes):
+        return pl.BlockSpec((1, lanes), lambda i: (0, 0))
+
+    line = jax.ShapeDtypeStruct((1, width), F32)
+    return pl.pallas_call(
+        functools.partial(widen_kernel, heads),
+        grid=(steps,),
+        in_specs=[col_spec, col_spec]
+        + [rows_from(start, size) for start, size in zip(starts, sizes, strict=True)]
+        + [pl.BlockSpec(lines.shape, lambda i: (0, 0))],
+        out_specs=[col_spec, col_spec]
+        + [rows_from(0, size) for size in sizes]
+        + [line_spec(width)] * 6
+        + [line_spec(sizes[0])],
+        out_shape=[
+            jax.ShapeDtypeStruct(out_cols.shape, BF16),
+            jax.ShapeDtypeStruct(out_cols.shape, F32),
+        ]
+        + [jax.ShapeDtypeStruct((size, width), F32) for size in sizes]
+        + [line] * 6
+        + [jax.ShapeDtypeStruct((1, sizes[0]), F32)],
+    )(out_cols, grad_cols, total, total, total, total, lines)
 
 
 def per_device(
@@ -809,33 +1059,30 @@
     fc2_weight,
     fc2_bias,
 ):
-    width = hidden_in.shape[-1]
-    section = lax.axis_index("section")
-    valid = dense_weight.shape[1]
-    heads = valid // HEAD
+    heads = dense_weight.shape[1] // HEAD
     units = fc1_weight.shape[-1]
-    weights = (qkv_weight[0], dense_weight[0], fc1_weight[0], fc2_weight[0])
+    weights = (qkv_weight[0].T, dense_weight[0], fc1_weight[0], fc2_weight[0])
     vec = (ln1_gain, ln1_bias, ln2_gain, ln2_bias, dense_bias, fc2_bias, fc1_bias)
-    out_cols, grad_cols, total, small = train(hidden_in, target, tissue, weights, qkv_bias, vec)
-    small = lax.dynamic_index_in_dim(small, section, 0, keepdims=False)
-    columns = width // lax.axis_size("tensor")
-    total = total.astype(F32)
-    ends = np.cumsum([3 * valid, width, units])
+    out_cols, grad_cols, total, lines = train(hidden_in, target, tissue, weights, qkv_bias, vec)
+    out_cols, grad_cols, qkv_grad, fc1_grad, fc2_grad, dense_grad, *lines = widen(
+        out_cols, grad_cols, total, lines, heads, units
+    )
+    gain1, bias1, gain2, bias2, out_bias, fc1_bias_grad, qkv_bias_grad = lines
     return (
-        out_cols[None, ..., :columns],
-        grad_cols[None, ..., :columns].astype(F32),
-        small[0:1],
-        small[1:2],
-        small[2:3],
-        small[3:4],
-        unpack_rows(total[: ends[0]], heads)[None],
-        unpack_line(small[4], heads),
-        total[ends[2] :][None],
-        small[5:6],
-        total[ends[0] : ends[1]][None],
-        small[6:7],
-        total[ends[1] : ends[2]][None],
-        small[5:6],
+        out_cols.transpose(0, 2, 1)[None],
+        grad_cols.transpose(0, 2, 1)[None],
+        gain1,
+        bias1,
+        gain2,
+        bias2,
+        qkv_grad.T[None],
+        qkv_bias_grad,
+        dense_grad[None],
+        out_bias,
+        fc1_grad[None],
+        fc1_bias_grad,
+        fc2_grad[None],
+        out_bias,
     )
 
 

time: 224 us -> 181 us (0.81)
  the two profiles are of different devices: /device:TPU:9 before, /device:TPU:0 now
where the time goes in v3:
time: 181 us
  Pallas kernels  179 us (99%)
    pallas_call x1, Pallas kernels, train(): pl.pallas_call(body, out_shape=(jax.ShapeDtypeStruct((count, columns, seq...  173 us
    pallas_call x1, Pallas kernels, widen(): pl.pallas_call(functools.partial(widen_kernel, heads), grid=(steps,), in_...  6.54 us

profile of v3, /device:TPU:0, one launch (start us, length us, event | category | flops | bytes accessed | tf_op | source)
XLA Modules:
  0.0 181.1 jit_solution(12283343683302331736)
XLA Ops:
  0.7 172.6 %shard_map.263 = (bf16[2,192,1024]{2,1,0:T(8,128)(2,1)}, bf16[2,192,1024]{2,1,0:T(8,128)(2,1)}, bf16[2304,768]{1,0:T(8,128)(2,1)}, f32[8,768]{1,0:T(8,128)}) custom-call(bf16[2,4,256,768]{3,2,1,0:T(8,128)(2,1)} %bitcast.20, bf16[2,4,256,768]{3,2,1,0:T(8,128)(2,1)} %bitcast.21, s32[2]{0:T(128)} %refs_2_.1, f32[2,1024,128]{2,1,0:T(8,128)} %constant.2.clone.refs_3_, ...), custom_call_target="tpu_custom_call" | custom-call | tf_op jit(solution)/shard_map/pallas_call | solution.py:962
  173.2 6.5 %shard_map.264 = (bf16[2,192,1024]{2,1,0:T(8,128)(2,1)}, f32[2,192,1024]{2,1,0:T(8,128)}, f32[576,768]{1,0:T(8,128)}, f32[768,768]{1,0:T(8,128)}, f32[768,768]{1...) custom-call(bf16[2,192,1024]{2,1,0:T(8,128)(2,1)} %get-tuple-element, ...), custom_call_target="tpu_custom_call" | custom-call | tf_op jit(solution)/shard_map/pallas_call | solution.py:1025
  179.8 1.3 copy.31

commit v4 on v3

--- a/solution.py
+++ b/solution.py
@@ -88,6 +88,9 @@
     met,
     late_got,
     late_met,
+    norm_rows,
+    context_grad,
+    query_back,
     total,
     half_got,
     first_got,
@@ -197,9 +200,11 @@
             [(vec.at[section], vec.at[section])] + pairs
         )
     ]
-    for item in gifts:
+    projection = 3 * heads
+    for item in gifts[: 1 + projection]:
         item.start()
 
+    small[...] = jnp.zeros_like(small)
     tissue_lane = lax.broadcasted_iota(jnp.int32, (8, LANES), 1)
     marks = [(tissue_lane == tissue[index]).astype(F32) for index in range(tissue.shape[0])]
     tally[...] = functools.reduce(lambda a, b: a + b, marks)
@@ -226,7 +231,7 @@
     left_half = lax.rem(lax.broadcasted_iota(jnp.int32, (1, lanes), 1), HEAD) < ROT // 2
 
     def wide(table, start):
-        piece = tables[table, start : start + rows, :]
+        piece = tables[table, pl.ds(start, rows), :]
         return jnp.concatenate([piece] * (lanes // LANES), axis=1)
 
     def turned(value):
@@ -253,6 +258,7 @@
         here = slice(start, start + rows)
         if c == 0:
             need(0, 1 + projection, layer)
+            pl.when(layer == 0)(gifts[1 + projection].start)
         spread, _ = normalise(chain[layer, c].astype(F32))
         first = (spread * vec[layer, 0:1] + vec[layer, 1:2]).astype(BF16)
         second = (spread * vec[layer, 2:3] + vec[layer, 3:4]).astype(BF16)
@@ -264,6 +270,8 @@
         )
         qkv[layer, here, 2 * lanes :] = projected[:, 2 * lanes :].astype(BF16)
         if c == 0:
+            for item in gifts[2 + projection :]:
+                pl.when(layer == 0)(item.start)
             need(1 + projection, 2 + projection, layer)
         pre = dot_nn(second, w1[layer]) + vec[layer, 6:7]
         below = 0.5 * (1.0 + lax.erf(pre * (0.5**0.5)))
@@ -304,26 +312,43 @@
         result = (dot_nn(context, wd[layer]) + dot_nn(active, w2[layer])).astype(BF16)
         for index, goal in enumerate((part, late_part)):
             pl.when(layer == index)(functools.partial(put, goal, c, result))
-
-    def backward_chunk(layer, c):
+        return second
+
+    def feed_back(c, second):
+        here = slice(c * rows, (c + 1) * rows)
+        cotangent = chain[2, c]
+        pre_grad = (dot_nt(cotangent, w2[1]) * gate[1, here, :].astype(F32)).astype(BF16)
+        gate[1, here, :] = pre_grad
+        if c < chunks - 1:
+            norm_rows[...] = second
+            add_forward_grads(1, c, c == 0)
+
+    def rows_of(c):
+        return pl.ds(pl.multiple_of(c * rows, rows), rows)
+
+    def backward_front(layer, c):
+        here = rows_of(c)
+        cotangent = chain[3 - layer, c]
+        context_grad[...] = dot_nt(cotangent, wd[layer]).astype(BF16)
+
+        @pl.when(layer == 0)
+        def _():
+            back = dot_nt(cotangent, w2[0]) * gate[0, here, :].astype(F32)
+            gate[0, here, :] = back.astype(BF16)
+
+    def backward_attention(layer, c):
         start = c * rows
         stop = start + rows
         here = slice(start, stop)
-        first_turn = c == chunks - 1
-        slot = chunks - 1 - c
-        cotangent = chain[3 - layer, c]
-        context_grad = dot_nt(cotangent, wd[layer]).astype(BF16)
-        pre_grad = (dot_nt(cotangent, w2[layer]) * gate[layer, here, :].astype(F32)).astype(BF16)
-        gate[layer, here, :] = pre_grad
-        second_back = dot_nt(pre_grad, w1[layer])
+        own = context_grad[...]
         query = qkv[layer, here, :lanes]
-        weighed = context_grad.astype(F32) * ctx[layer, here, :].astype(F32)
+        weighed = own.astype(F32) * ctx[layer, here, :].astype(F32)
         query_grad = jnp.zeros((rows, lanes), F32)
         key_sum = None
         value_sum = None
         for h in range(heads):
             mask = head_masks[h]
-            own_grad = only(mask, context_grad)
+            own_grad = only(mask, own)
             asked = only(mask, query) * jnp.asarray(factor, BF16)
             row_dot = jnp.sum(only(mask, weighed), axis=-1, keepdims=True)
             prob = probs[c][layer, h]
@@ -336,74 +361,90 @@
             value_part = dot_tn(prob, own_grad)
             key_sum = key_part if key_sum is None else key_sum + key_part
             value_sum = value_part if value_sum is None else value_sum + value_part
-        if first_turn:
+        query_back[...] = query_grad * factor
+        if c == chunks - 1:
             key_grad[:stop] = key_sum
             value_grad[:stop] = value_sum
         else:
             key_grad[:stop] += key_sum
             value_grad[:stop] += value_sum
-        qkv[layer, here, :lanes] = turn_back(query_grad * factor, start).astype(BF16)
+
+    def backward_rest(layer, c):
+        here = rows_of(c)
+        start = pl.multiple_of(c * rows, rows)
+        pre_grad = gate[layer, here]
+        second_back = dot_nt(pre_grad, w1[layer])
+        qkv[layer, here, :lanes] = turn_back(query_back[...], start).astype(BF16)
         qkv[layer, here, lanes : 2 * lanes] = turn_back(key_grad[here], start).astype(BF16)
         qkv[layer, here, 2 * lanes :] = value_grad[here].astype(BF16)
         projected_grad = qkv[layer, here, :]
         first_back = dot_nn(projected_grad, wq[layer])
         spread, rstd = normalise(chain[layer, c].astype(F32))
+        back = first_back * vec[layer, 0:1] + second_back * vec[layer, 2:3]
+        middle = jnp.mean(back, axis=-1, keepdims=True)
+        tilt = jnp.mean(back * spread, axis=-1, keepdims=True)
+        put(part, chunks - 1 - c, rstd * (back - middle - spread * tilt))
         first = (spread * vec[layer, 0:1] + vec[layer, 1:2]).astype(BF16)
-        second = (spread * vec[layer, 2:3] + vec[layer, 3:4]).astype(BF16)
+        norm_rows[...] = (spread * vec[layer, 2:3] + vec[layer, 3:4]).astype(BF16)
         sums = (
             first_back * spread,
             first_back,
             second_back * spread,
             second_back,
             projected_grad.astype(F32),
-            cotangent.astype(F32),
+            chain[3 - layer, c].astype(F32),
             pre_grad.astype(F32),
         )
         for index, item in enumerate(sums):
-            line = jnp.sum(item, axis=0, keepdims=True)
-            if first_turn:
-                small[layer, index : index + 1] = line
-            else:
-                small[layer, index : index + 1] += line
-        if first_turn:
-            small[layer, len(sums) :] = jnp.zeros((8 - len(sums), width), F32)
-        back = first_back * vec[layer, 0:1] + second_back * vec[layer, 2:3]
-        middle = jnp.mean(back, axis=-1, keepdims=True)
-        tilt = jnp.mean(back * spread, axis=-1, keepdims=True)
-        put(part, slot, rstd * (back - middle - spread * tilt))
-        return here, first_turn, first, second, pre_grad, cotangent
-
-    def add_weight_grads(layer, here, first_turn, first, second, pre_grad, cotangent):
-        step = lanes
-
-        def add(start, piece):
-            goal = slice(start, start + piece.shape[0])
-            if not first_turn:
-                piece = piece + total[layer, goal].astype(F32)
-            total[layer, goal] = piece.astype(BF16)
-
+            small[layer, index : index + 1] += jnp.sum(item, axis=0, keepdims=True)
+        return first
+
+    def add_piece_grads(layer, start, piece, first_turn):
+        goal = slice(start, start + piece.shape[0])
+        before = jnp.where(first_turn, 0.0, total[layer, goal].astype(F32))
+        total[layer, goal] = (piece + before).astype(BF16)
+
+    def add_forward_grads(layer, c, first_turn):
+        here = rows_of(c)
+        cotangent = chain.at[3 - layer, c]
+
+        def add_block(index, carry):
+            block = pl.ds(pl.multiple_of(index * lanes, lanes), lanes)
+            goal = pl.ds(pl.multiple_of(width + index * lanes, lanes), lanes)
+            pieces = (
+                (block, dot_tn(norm_rows[:, block], gate[layer, here])),
+                (goal, dot_tn(act[layer, here, block], cotangent[...])),
+            )
+            for at, piece in pieces:
+                before = jnp.where(first_turn, 0.0, total[layer, at].astype(F32))
+                total[layer, at] = (piece + before).astype(BF16)
+            return carry
+
+        lax.fori_loop(0, width // lanes, add_block, 0)
+
+    def add_weight_grads(layer, c, first):
+        base = width + act.shape[-1]
+        here = rows_of(c)
+        first_turn = c == chunks - 1
         for part_index in range(3):
             at = part_index * lanes
             piece = dot_tn(qkv[layer, here, at : at + lanes], first)
             for h in range(heads):
-                add((3 * h + part_index) * HEAD, piece[h * HEAD : (h + 1) * HEAD])
-        base = 3 * valid
-        for at in range(0, width, step):
-            add(base + at, dot_tn(second[:, at : at + step], pre_grad))
-        base += width
-        for at in range(0, act.shape[-1], step):
-            add(base + at, dot_tn(act[layer, here, at : at + step], cotangent))
-        base += act.shape[-1]
-        add(base, dot_tn(ctx[layer, here], cotangent)[:valid])
-
-    all_rows = total.shape[1]
-    share_rows = all_rows // 2
+                row = base + (3 * h + part_index) * HEAD
+                add_piece_grads(layer, row, piece[h * HEAD : (h + 1) * HEAD], first_turn)
+        piece = dot_tn(ctx[layer, here], chain[3 - layer, c])[:valid]
+        add_piece_grads(layer, base + 3 * valid, piece, first_turn)
+
+    cut = width + act.shape[-1]
+    jobs = ((0, cut), (cut, total.shape[1] - cut))
     folds = min(bits, 2)
-
-    def spans(group):
-        order = (0, 1)[:folds] if group == 0 else (1, 0)[-folds:] if folds else ()
-        size = share_rows // 2
-        start = section * share_rows + group * size
+    sum_steps = 2 + 2 * folds + (bits - folds)
+
+    def spans(job, group):
+        order = ((0, 1), (1, 0))[group][:folds]
+        base, size = jobs[job]
+        size = size // 4
+        start = base + section * size * 2 + group * size
         steps = []
         for bit in order:
             size = size // 2
@@ -412,75 +453,81 @@
             start = start + upper * size
         return steps, start, size
 
-    groups = [spans(0), spans(1)]
-    sum_steps = 2 + 2 * folds + (bits - folds)
-
-    group_rows = share_rows // 2
+    groups = [[spans(job, group) for group in range(2)] for job in range(2)]
 
     def sums_of(layer, start, size):
         return total.at[layer, pl.ds(pl.multiple_of(start, 16), size)]
 
-    def gathered(layer, group, start, size):
-        start = start - section * share_rows - group * group_rows
+    def gathered(layer, job, group, start, size):
+        base, job_rows = jobs[job]
+        start = start - base - section * (job_rows // 2) - group * (job_rows // 4) + base // 4
         return (act, gate)[group].at[layer, pl.ds(pl.multiple_of(start, 16), size)]
 
-    def sum_sems(layer, step, group):
-        return sum_send.at[layer, step, group], sum_recv.at[layer, step, group]
-
-    def sum_copies(layer, step):
+    def sum_sems(layer, job, step, group):
+        return sum_send.at[layer, job, step, group], sum_recv.at[layer, job, step, group]
+
+    def landing_of(buffer, job, parts):
+        base, job_rows = jobs[job]
+        return buffer.at[base // parts : (base + job_rows) // parts]
+
+    def sum_copies(layer, job, step):
+        base, job_rows = jobs[job]
         if step == 0:
-            source = sums_of(layer, (1 - section) * share_rows, share_rows)
-            return [send(source, half_got.at[layer], sum_sems(layer, 0, 0), twin)]
+            source = sums_of(layer, base + (1 - section) * (job_rows // 2), job_rows // 2)
+            goal = landing_of(half_got.at[layer], job, 2)
+            return [send(source, goal, sum_sems(layer, job, 0, 0), twin)]
         copies_now = []
-        for group, (steps, start, size) in enumerate(groups):
-            sems = sum_sems(layer, step, group)
+        for group, (steps, start, size) in enumerate(groups[job]):
+            sems = sum_sems(layer, job, step, group)
             if step <= folds:
                 bit, _, gone, size = steps[step - 1]
-                goal = (first_got, second_got)[step - 1].at[group]
+                goal = landing_of((first_got, second_got)[step - 1].at[group], job, 4 << step)
                 copies_now.append(send(sums_of(layer, gone, size), goal, sems, mates[bit]))
             elif step <= bits:
-                goal = more_got.at[layer, step - 1 - folds, group]
-                source = gathered(layer, group, start, size)
+                goal = landing_of(more_got.at[layer, step - 1 - folds, group], job, 16)
+                source = gathered(layer, job, group, start, size)
                 copies_now.append(send(source, goal, sems, mates[step - 1]))
             else:
                 bit, start, _, size = steps[bits - step]
-                piece = gathered(layer, group, start, size)
+                piece = gathered(layer, job, group, start, size)
                 copies_now.append(send(piece, piece, sems, mates[bit]))
         return copies_now
 
-    def last_copies(layer):
+    def last_copies(layer, job):
+        base, job_rows = jobs[job]
+        size = job_rows // 4
         pieces = []
         for group in range(2):
-            first_row = section * share_rows + group * group_rows
-            piece = gathered(layer, group, first_row, group_rows)
-            goal = grads.at[pl.ds(pl.multiple_of(first_row, 16), group_rows)]
-            sems = sum_sems(layer, sum_steps - 1, group)
-            other_row = (1 - section) * share_rows + group * group_rows
-            other = grads.at[pl.ds(pl.multiple_of(other_row, 16), group_rows)]
+            first_row = base + section * (job_rows // 2) + group * size
+            piece = gathered(layer, job, group, first_row, size)
+            goal = grads.at[pl.ds(pl.multiple_of(first_row, 16), size)]
+            sems = sum_sems(layer, job, sum_steps - 1, group)
+            other_row = base + (1 - section) * (job_rows // 2) + group * size
+            other = grads.at[pl.ds(pl.multiple_of(other_row, 16), size)]
             pieces.append(
                 (
                     send(piece, goal, sems, twin),
                     send(piece, other, sems, twin),
-                    pltpu.make_async_copy(piece, goal, store_sem.at[group]),
+                    pltpu.make_async_copy(piece, goal, store_sem.at[job, group]),
                 )
             )
         return pieces
 
-    def sum_start(layer, step):
+    def sum_start(layer, job, step):
         if step < sum_steps - 1:
-            if isinstance(layer, int) and layer == 0 and 1 <= step <= folds:
+            if layer == 0 and 1 <= step <= folds:
                 for group in range(2):
-                    pl.semaphore_wait(free_sem.at[step - 1, group], 1)
-            for item in sum_copies(layer, step):
+                    pl.semaphore_wait(free_sem.at[job, step - 1, group], 1)
+            for item in sum_copies(layer, job, step):
                 item.start()
             return
-        for give, _, keep in last_copies(layer):
+        for give, _, keep in last_copies(layer, job):
             pl.when(section != layer)(give.start)
             pl.when(section == layer)(keep.start)
 
     def add_rows(goal, base, source):
         size = source.shape[0]
-        piece = math.gcd(size, 144)
+        piece = math.gcd(size, 192)
 
         def add_piece(index, carry):
             here = pl.ds(pl.multiple_of(index * piece, 16), piece)
@@ -489,35 +536,50 @@
 
         lax.fori_loop(0, size // piece, add_piece, 0)
 
-    def sum_end(layer, step):
+    def sum_end(layer, job, step):
         if step == sum_steps - 1:
-            for give, take, keep in last_copies(layer):
+            for give, take, keep in last_copies(layer, job):
                 pl.when(section != layer)(give.wait_send)
                 pl.when(section == layer)(take.wait_recv)
                 pl.when(section == layer)(keep.wait)
             return
-        for item in sum_copies(layer, step):
+        for item in sum_copies(layer, job, step):
             item.wait()
         if step == 0:
-            base = sums_of(layer, section * share_rows, share_rows)
-            add_rows(base, base, half_got.at[layer])
+            base, job_rows = jobs[job]
+            kept = sums_of(layer, base + section * (job_rows // 2), job_rows // 2)
+            add_rows(kept, kept, landing_of(half_got.at[layer], job, 2))
             return
         if step > bits:
             return
-        for group, (steps, start, size) in enumerate(groups):
-            goal = gathered(layer, group, start, size)
+        for group, (steps, start, size) in enumerate(groups[job]):
+            goal = gathered(layer, job, group, start, size)
             if step < folds:
                 base = sums_of(layer, steps[step - 1][1], steps[step - 1][3])
-                add_rows(base, base, first_got.at[group])
+                add_rows(base, base, landing_of(first_got.at[group], job, 8))
             elif step == folds:
-                add_rows(goal, sums_of(layer, start, size), second_got.at[group])
+                add_rows(goal, sums_of(layer, start, size), landing_of(second_got.at[group], job, 16))
             else:
-                add_rows(goal, goal, more_got.at[layer, step - 1 - folds, group])
+                landed = landing_of(more_got.at[layer, step - 1 - folds, group], job, 16)
+                add_rows(goal, goal, landed)
             if layer == 1 and step <= folds:
                 mate = mates[steps[step - 1][0]]
                 pl.semaphore_signal(
-                    free_sem.at[step - 1, group], inc=1, device_id=mate, device_id_type=MESH
+                    free_sem.at[job, step - 1, group],
+                    inc=1,
+                    device_id=mate,
+                    device_id_type=MESH,
                 )
+
+    steps_done = {(layer, job): 0 for layer in range(2) for job in range(2)}
+
+    def move_sum(layer, job, step=None):
+        step = steps_done[layer, job] if step is None else step
+        if step < sum_steps:
+            sum_end(layer, job, step)
+            if step + 1 < sum_steps:
+                sum_start(layer, job, step + 1)
+            steps_done[layer, job] = max(steps_done[layer, job], step + 1)
 
     line_friends = [twin] + mates + [near, far]
 
@@ -544,7 +606,7 @@
 
     def spot(kind, u):
         chunk = u // halves if kind < 2 else chunks - 1 - u // halves
-        return chunk, slice(u % halves * unit, (u % halves + 1) * unit)
+        return chunk, pl.ds(pl.multiple_of(lax.rem(u, halves) * unit, unit), unit)
 
     def buffers(kind, u):
         if kind == 1:
@@ -654,8 +716,6 @@
             if index < len(settles):
                 settle(kind, settles[index])
 
-    projection = 3 * heads
-
     def need(first, last, layer):
         @pl.when(section == layer)
         def _():
@@ -669,113 +729,136 @@
 
     input_load.wait()
 
-    forward_turns = (
-        (((), ()), ((), ()), ((0,), ()), ((1, 2, 3), (0, 1, 2))),
-        (((4,), (3,)), ((5, 6), (4, 5)), ((7,), (6, 7)), ((), ())),
+    first_turns = (((), ()), ((), ()), ((0,), ()), ((1, 2), (0, 1)))
+    second_turns = (
+        (((3,), (2,)), ((4,), (3,))),
+        (((5,), (4,)), ((6,), (5,))),
+        (((7,), (6,)), ((), (7,))),
+        (((), ()), ((), ())),
     )
+
+    def weigh(c):
+        chain[2, c] = (vec[0, 7:8] * chain[2, c].astype(F32)).astype(BF16)
+
+    def find_share():
+        own_mark = jnp.where(section == 0, marks[0], marks[1])[0:1]
+        own_count = jnp.sum(own_mark * tally[0:1], axis=-1, keepdims=True)
+        share = (tissue.shape[0] * copies / TISSUES) / own_count
+        gifts[0].wait_send()
+        vec[0, 7:8] = jnp.broadcast_to(share, (1, width))
+        target_load.wait()
 
     def forward_layer(layer, carry):
         for c in range(chunks):
             pl.when(layer == 1)(functools.partial(arrive, 0, c))
-            forward_chunk(layer, c)
-            pl.when(layer == 0)(functools.partial(launch, 0, c))
-            for index in range(2):
-                pl.when(layer == index)(functools.partial(serve, 0, *forward_turns[index][c]))
-
-            if c == 2:
-
-                @pl.when(layer == 1)
-                def _():
-                    launch(1, 0)
-                    launch(1, 1)
-
-            for bit in range(bits):
-                if bit % chunks == c:
-                    pl.when(layer == bit // chunks)(functools.partial(count_on, bit))
-        return carry
-
-    lax.fori_loop(0, 2, forward_layer, 0)
-    target_load.wait()
-    own_mark = jnp.where(section == 0, marks[0], marks[1])[0:1]
-    own_count = jnp.sum(own_mark * tally[0:1], axis=-1, keepdims=True)
-    share = (tissue.shape[0] * copies / TISSUES) / own_count
-    gifts[0].wait_send()
-    vec[0, 7:8] = jnp.broadcast_to(share, (1, width))
-
-    def weigh(c, carry):
-        chain[2, c] = (vec[0, 7:8] * chain[2, c].astype(F32)).astype(BF16)
-        return carry
-
-    lax.fori_loop(0, chunks, weigh, 0)
-
-    backward_turns = (
-        (
-            ((1, (0, 1), ()),),
-            ((1, (2, 3), (0, 1)),),
-            ((1, (), (2, 3)), (2, (0,), ())),
-            ((2, (1, 2), (0, 1)),),
-        ),
-        (
-            ((2, (3, 4), (2, 3)),),
-            ((2, (5, 6), (4, 5)),),
-            ((2, (7,), (6, 7)),),
-            ((3, (0, 1), (0,)),),
-        ),
-    )
-
-    def serve_all(turns):
-        for item in turns:
-            serve(*item)
-
-    early_sums = ((0, None), (None, 1), (None, 2), (3, None))
-
-    def move_sum(step):
-        if step is not None:
-            sum_end(1, step)
-            sum_start(1, step + 1)
-
-    def backward_layer(turn_index, carry):
-        layer = 1 - turn_index
-        for at in range(chunks):
-            now = early_sums[at]
+            second = forward_chunk(layer, c)
 
             @pl.when(layer == 0)
             def _():
-                arrive(2, at)
-                release(2, at)
-                move_sum(now[0])
-
-            pl.when(layer == 1)(functools.partial(release, 0, at))
-            kept = backward_chunk(layer, chunks - 1 - at)
-            for index in range(2):
-                pl.when(turn_index == index)(functools.partial(launch, 2 + index, at))
-            add_weight_grads(layer, *kept)
-            if at == chunks - 1:
-                sum_start(layer, 0)
-
-                @pl.when(layer == 0)
-                def _():
-                    launch(1, 2)
-                    launch(1, 3)
-
-            @pl.when(layer == 0)
+                launch(0, c)
+                serve(0, *first_turns[c])
+                for bit in range(bits):
+                    if min(bit, chunks - 1) == c:
+                        count_on(bit)
+
+            @pl.when(layer == 1)
             def _():
-                if at == 1:
-                    move_sum(now[1])
-
-            for index in range(2):
-                pl.when(turn_index == index)(
-                    functools.partial(serve_all, backward_turns[index][at])
-                )
-
-            @pl.when(layer == 0)
+                serve(0, *second_turns[c][0])
+                if c in (1, 2):
+                    launch(1, c - 1)
+                if c == 0:
+                    find_share()
+                weigh(c)
+                feed_back(c, second)
+                serve(0, *second_turns[c][1])
+
+        return carry
+
+    lax.fori_loop(0, 2, forward_layer, 0)
+
+    meets = {1: (1, 1, 3, 3), 2: (4, 5, 6, 7, 8, 9, 10, 11), 3: (13,)}
+    settles = {1: (3, 3, 4, 4), 2: (6, 7, 8, 9, 10, 11, 12, 12), 3: ()}
+    backward_points = [[] for _ in range(8 * 2)]
+    for kind in (1, 2, 3):
+        order = [(2 * u, meet, kind, u, meets[kind][u]) for u in range(len(meets[kind]))]
+        order += [(2 * u + 3, settle, kind, u, settles[kind][u]) for u in range(len(settles[kind]))]
+        for _, work, kind_now, u, point in sorted(order, key=lambda item: item[0]):
+            backward_points[point].append((work, kind_now, u))
+
+    def serve_point(point):
+        for work, kind, u in backward_points[point]:
+            work(kind, u)
+
+    sum_moves = {
+        3: ((0, 0),),
+        8: ((1, 0),),
+        9: ((0, 2),),
+        10: ((1, 1),),
+        11: ((0, 3),),
+        12: ((1, 2),),
+        13: ((1, 3),),
+    }
+
+    def serve_at(step, point):
+        for index in range(2 * chunks):
+            number = index * 2 + point
+
+            @pl.when(step == index)
             def _():
-                if at == 2:
-                    move_sum(now[1])
-
+                serve_point(number)
+                for job, end in sum_moves.get(number, ()):
+                    move_sum(1, job, end)
+
+    def backward_step(step, carry):
+        turn_index = step // chunks
+        at = lax.rem(step, chunks)
+        layer = 1 - turn_index
+        c = chunks - 1 - at
+        last_step = step == 2 * chunks - 1
+
+        @pl.when(layer == 0)
+        def _():
+            pl.when(at == 0)(functools.partial(move_sum, 1, 0, 1))
+            arrive(2, at)
+            release(2, at)
+
+        pl.when(layer == 1)(functools.partial(release, 0, at))
+        backward_front(layer, c)
+
+        @pl.when(last_step)
+        def _():
+            spread, _ = normalise(chain[0, 0].astype(F32))
+            norm_rows[...] = (spread * vec[0, 2:3] + vec[0, 3:4]).astype(BF16)
+            add_forward_grads(0, 0, False)
+            sum_start(0, 0, 0)
+
+        for index in range(chunks):
+            pl.when(c == index)(functools.partial(backward_attention, layer, index))
+        serve_at(step, 0)
+        first = backward_rest(layer, c)
+        for index in range(2):
+            pl.when(turn_index == index)(functools.partial(launch, 2 + index, at))
+        pl.when(last_step)(functools.partial(move_sum, 0, 0))
+        add_weight_grads(layer, c, first)
+
+        @pl.when(jnp.logical_or(step == 0, jnp.logical_and(layer == 0, c > 0)))
+        def _():
+            add_forward_grads(layer, c, step == chunks)
+
+        @pl.when(step == 0)
+        def _():
+            sum_start(1, 0, 0)
+
+        @pl.when(jnp.logical_and(layer == 0, at > 1))
+        def _():
+            launch(1, at)
+
+        pl.when(step == chunks - 1)(functools.partial(sum_start, 1, 1, 0))
+        pl.when(last_step)(functools.partial(sum_start, 0, 1, 0))
+        serve_at(step, 1)
         return carry
 
-    lax.fori_loop(0, 2, backward_layer, 0)
+    lax.fori_loop(0, 2 * chunks, backward_step, 0)
 
     shift = lax.rem(place * columns, LANES)
 
@@ -832,12 +915,6 @@
             pltpu.make_async_copy(staged(index, section), goal.at[section], load_sem.at[1 + index]),
         ]
 
-    def sum_next(step):
-        if step < sum_steps:
-            sum_end(0, step)
-            if step + 1 < sum_steps:
-                sum_start(0, step + 1)
-
     def line_next(step):
         if step < len(line_friends):
             line_end(step)
@@ -845,40 +922,55 @@
                 line_copy(step + 1).start()
 
     line_copy(0).start()
-    sum_next(0)
+    serve(3, (1, 2), (0,))
+    move_sum(0, 1)
+    settle(3, 1)
     line_next(0)
-    serve(3, (2, 3), (1, 2))
     stage_whole(0, 0, 0)
+    serve(3, (3, 4), (2, 3))
     stage_whole(1, 1, 2)
-    serve(3, (4, 5), (3, 4))
-    for step in range(chunks, sum_steps - 1):
-        sum_end(1, step)
-        sum_start(1, step + 1)
-    sum_next(1)
+    meet(3, 5)
+    move_sum(1, 0)
+    settle(3, 4)
+    meet(1, 4)
+    move_sum(0, 0)
+    settle(3, 5)
+    meet(1, 5)
+    move_sum(0, 1)
     line_next(1)
-    serve(3, (6, 7), (5, 6))
-    sum_next(2)
+    settle(1, 4)
+    meet(3, 6)
+    move_sum(0, 0)
+    settle(1, 5)
+    meet(3, 7)
+    move_sum(0, 1)
     line_next(2)
+    settle(3, 6)
+    meet(1, 6)
+    move_sum(0, 0)
     settle(3, 7)
-    sum_end(1, sum_steps - 1)
-    meet(1, 4)
-    sum_next(3)
+    meet(1, 7)
+    move_sum(0, 1)
     line_next(3)
     stage_own(1, 0, 3)
     moves = swap_columns(1, grad_cols)
     for item in moves:
         item.start()
-    serve(1, (5, 6, 7), (4, 5, 6))
-    sum_next(4)
-    line_next(4)
+    settle(1, 6)
     settle(1, 7)
+    move_sum(1, 1)
+    move_sum(0, 0)
     stage_own(0, 1, 1)
     late_moves = swap_columns(0, out_cols)
     for item in late_moves:
         item.start()
-    for step in range(5, max(sum_steps, len(line_friends))):
-        sum_next(step)
+    move_sum(0, 1)
+    for step in range(4, len(line_friends)):
         line_next(step)
+    for _ in range(sum_steps):
+        for job in range(2):
+            move_sum(0, job)
+            move_sum(1, job)
     lines[...] = small[section]
     for item in moves + late_moves:
         item.wait()
@@ -924,6 +1016,9 @@
         pltpu.VMEM((pieces, unit, width), BF16),
         pltpu.VMEM((pieces, unit, width - LANES), BF16),
         pltpu.VMEM((pieces, unit, width // 2), BF16),
+        pltpu.VMEM((rows, width), BF16),
+        pltpu.VMEM((rows, lanes), BF16),
+        pltpu.VMEM((rows, lanes), F32),
         pltpu.VMEM((2, total_rows, width), BF16),
         pltpu.VMEM((2, total_rows // 2, width), BF16),
         pltpu.VMEM((2, total_rows // 8, width), BF16),
@@ -942,14 +1037,14 @@
         pltpu.SemaphoreType.DMA((2, 3, pieces)),
         pltpu.SemaphoreType.DMA((2,)),
         pltpu.SemaphoreType.DMA((2,)),
-        pltpu.SemaphoreType.DMA((2, bits + 4, 2)),
-        pltpu.SemaphoreType.DMA((2, bits + 4, 2)),
+        pltpu.SemaphoreType.DMA((2, 2, bits + 4, 2)),
+        pltpu.SemaphoreType.DMA((2, 2, bits + 4, 2)),
         pltpu.SemaphoreType.DMA((3 + bits,)),
         pltpu.SemaphoreType.DMA((3 + bits,)),
         pltpu.SemaphoreType.DMA((max(bits, 1),)),
         pltpu.SemaphoreType.DMA((max(bits, 1),)),
-        pltpu.SemaphoreType.DMA((2,)),
-        pltpu.SemaphoreType.REGULAR((2, 2)),
+        pltpu.SemaphoreType.DMA((2, 2)),
+        pltpu.SemaphoreType.REGULAR((2, 2, 2)),
     ]
 
     def body(*refs):
@@ -1007,10 +1102,10 @@
 
 
 def widen(out_cols, grad_cols, total, lines, heads, units):
-    steps = 4
+    steps = 6
     count, columns, seq_len = out_cols.shape
     width = total.shape[1]
-    sizes = (3 * heads * HEAD, width, units, heads * HEAD)
+    sizes = (width, units, 3 * heads * HEAD, heads * HEAD)
     starts = [0, *np.cumsum(sizes[:-1]).tolist()]
     col_spec = pl.BlockSpec((count, columns // steps, seq_len), lambda i: (0, i, 0))
 
@@ -1031,14 +1126,14 @@
         out_specs=[col_spec, col_spec]
         + [rows_from(0, size) for size in sizes]
         + [line_spec(width)] * 6
-        + [line_spec(sizes[0])],
+        + [line_spec(sizes[2])],
         out_shape=[
             jax.ShapeDtypeStruct(out_cols.shape, BF16),
             jax.ShapeDtypeStruct(out_cols.shape, F32),
         ]
         + [jax.ShapeDtypeStruct((size, width), F32) for size in sizes]
         + [line] * 6
-        + [jax.ShapeDtypeStruct((1, sizes[0]), F32)],
+        + [jax.ShapeDtypeStruct((1, sizes[2]), F32)],
     )(out_cols, grad_cols, total, total, total, total, lines)
 
 
@@ -1064,7 +1159,7 @@
     weights = (qkv_weight[0].T, dense_weight[0], fc1_weight[0], fc2_weight[0])
     vec = (ln1_gain, ln1_bias, ln2_gain, ln2_bias, dense_bias, fc2_bias, fc1_bias)
     out_cols, grad_cols, total, lines = train(hidden_in, target, tissue, weights, qkv_bias, vec)
-    out_cols, grad_cols, qkv_grad, fc1_grad, fc2_grad, dense_grad, *lines = widen(
+    out_cols, grad_cols, fc1_grad, fc2_grad, qkv_grad, dense_grad, *lines = widen(
         out_cols, grad_cols, total, lines, heads, units
     )
     gain1, bias1, gain2, bias2, out_bias, fc1_bias_grad, qkv_bias_grad = lines

time: 181 us -> 165 us (0.912)
  Pallas kernels: 179 us -> 162 us
    pallas_call x1, Pallas kernels: 173 us -> 155 us  [train(): pl.pallas_call(body, out_shape=(jax.ShapeDtypeStruct((count, columns, seq...]
where the time goes in v4:
time: 165 us; the launch traced here: 164 us
  Pallas kernels  162 us (98%)
    pallas_call x1, Pallas kernels, train(): pl.pallas_call(body, out_shape=(jax.ShapeDtypeStruct((count, columns, seq...  155 us
    pallas_call x1, Pallas kernels, widen(): pl.pallas_call(functools.partial(widen_kernel, heads), grid=(steps,), in_...  7.23 us

profile of v4, /device:TPU:0, one launch (start us, length us, event | category | flops | bytes accessed | tf_op | source)
XLA Modules:
  0.0 163.7 jit_solution(6049148884477049301)
XLA Ops:
  0.7 154.5 %shard_map.263 = (bf16[2,192,1024]{2,1,0:T(8,128)(2,1)}, bf16[2,192,1024]{2,1,0:T(8,128)(2,1)}, bf16[2304,768]{1,0:T(8,128)(2,1)}, f32[8,768]{1,0:T(8,128)}) custom-call(bf16[2,4,256,768]{3,2,1,0:T(8,128)(2,1)} %bitcast.20, bf16[2,4,256,768]{3,2,1,0:T(8,128)(2,1)} %bitcast.21, s32[2]{0:T(128)} %refs_2_.1, f32[2,1024,128]{2,1,0:T(8,128)} %constant.2.clone.refs_3_, ...), custom_call_target="tpu_custom_call" | custom-call | tf_op jit(solution)/shard_map/pallas_call | solution.py:1057
  155.2 7.2 %shard_map.264 = (bf16[2,192,1024]{2,1,0:T(8,128)(2,1)}, f32[2,192,1024]{2,1,0:T(8,128)}, f32[768,768]{1,0:T(8,128)}, f32[768,768]{1,0:T(8,128)}, f32[576,768]{1...) custom-call(bf16[2,192,1024]{2,1,0:T(8,128)(2,1)} %get-tuple-element, ...), custom_call_target="tpu_custom_call" | custom-call | tf_op jit(solution)/shard_map/pallas_call | solution.py:1120
  162.4 1.3 copy.31

commit v5 on v4

--- a/solution.py
+++ b/solution.py
@@ -201,7 +201,7 @@
         )
     ]
     projection = 3 * heads
-    for item in gifts[: 1 + projection]:
+    for item in gifts[: 2 + projection]:
         item.start()
 
     small[...] = jnp.zeros_like(small)
@@ -258,7 +258,8 @@
         here = slice(start, start + rows)
         if c == 0:
             need(0, 1 + projection, layer)
-            pl.when(layer == 0)(gifts[1 + projection].start)
+            for item in gifts[2 + projection :]:
+                pl.when(layer == 0)(item.start)
         spread, _ = normalise(chain[layer, c].astype(F32))
         first = (spread * vec[layer, 0:1] + vec[layer, 1:2]).astype(BF16)
         second = (spread * vec[layer, 2:3] + vec[layer, 3:4]).astype(BF16)
@@ -270,8 +271,6 @@
         )
         qkv[layer, here, 2 * lanes :] = projected[:, 2 * lanes :].astype(BF16)
         if c == 0:
-            for item in gifts[2 + projection :]:
-                pl.when(layer == 0)(item.start)
             need(1 + projection, 2 + projection, layer)
         pre = dot_nn(second, w1[layer]) + vec[layer, 6:7]
         below = 0.5 * (1.0 + lax.erf(pre * (0.5**0.5)))
@@ -777,7 +776,7 @@
     lax.fori_loop(0, 2, forward_layer, 0)
 
     meets = {1: (1, 1, 3, 3), 2: (4, 5, 6, 7, 8, 9, 10, 11), 3: (13,)}
-    settles = {1: (3, 3, 4, 4), 2: (6, 7, 8, 9, 10, 11, 12, 12), 3: ()}
+    settles = {1: (3, 3, 5, 5), 2: (6, 7, 8, 9, 10, 11, 12, 12), 3: ()}
     backward_points = [[] for _ in range(8 * 2)]
     for kind in (1, 2, 3):
         order = [(2 * u, meet, kind, u, meets[kind][u]) for u in range(len(meets[kind]))]
@@ -790,13 +789,12 @@
             work(kind, u)
 
     sum_moves = {
-        3: ((0, 0),),
+        5: ((0, 0),),
         8: ((1, 0),),
         9: ((0, 2),),
         10: ((1, 1),),
-        11: ((0, 3),),
-        12: ((1, 2),),
-        13: ((1, 3),),
+        11: ((1, 2), (0, 3)),
+        12: ((1, 3),),
     }
 
     def serve_at(step, point):
@@ -922,6 +920,8 @@
                 line_copy(step + 1).start()
 
     line_copy(0).start()
+    for item in gifts[1:]:
+        item.wait_send()
     serve(3, (1, 2), (0,))
     move_sum(0, 1)
     settle(3, 1)
@@ -960,22 +960,22 @@
     settle(1, 7)
     move_sum(1, 1)
     move_sum(0, 0)
+    for step in range(4, len(line_friends)):
+        line_next(step)
+    lines_store = pltpu.make_async_copy(small.at[section], lines, load_sem.at[0])
+    lines_store.start()
+    move_sum(0, 1)
     stage_own(0, 1, 1)
     late_moves = swap_columns(0, out_cols)
     for item in late_moves:
         item.start()
-    move_sum(0, 1)
-    for step in range(4, len(line_friends)):
-        line_next(step)
     for _ in range(sum_steps):
         for job in range(2):
             move_sum(0, job)
             move_sum(1, job)
-    lines[...] = small[section]
     for item in moves + late_moves:
         item.wait()
-    for item in gifts[1:]:
-        item.wait_send()
+    lines_store.wait()
 
 
 def train(x, target, tissue, weights, qkv_bias, vec):
@@ -1063,7 +1063,7 @@
             jax.ShapeDtypeStruct((8, width), F32),
         ),
         in_specs=[hbm, hbm, smem, vmem, hbm, hbm, hbm, hbm, vmem] + [vmem] * len(vec),
-        out_specs=(hbm, hbm, hbm, vmem),
+        out_specs=(hbm, hbm, hbm, hbm),
         scratch_shapes=scratch + probs + semaphores,
         compiler_params=pltpu.CompilerParams(
             collective_id=0, has_side_effects=True, vmem_limit_bytes=63 * 2**20
@@ -1082,59 +1082,117 @@
     )
 
 
-def widen_kernel(heads, cols, grad_cols, *refs):
-    sources, lines = refs[:4], refs[4]
-    out_cols, out_grad_cols, *goals = refs[5:]
-    out_cols[...] = cols[...]
-    out_grad_cols[...] = grad_cols[...].astype(F32)
-    for source, goal in zip(sources, goals[:4], strict=True):
-        goal[...] = source[...].astype(F32)
-    for index, goal in zip((0, 1, 2, 3, 5, 6), goals[4:10], strict=True):
+def widen_kernel(
+    heads,
+    sizes,
+    cols,
+    grad_cols,
+    total,
+    lines,
+    out_cols,
+    out_grad_cols,
+    goal0,
+    goal1,
+    goal2,
+    goal3,
+    gain1,
+    bias1,
+    gain2,
+    bias2,
+    out_bias,
+    out_bias_again,
+    fc1_bias,
+    qkv_bias,
+    cols_kept,
+    cols_low,
+    cols_wide,
+    rows_low,
+    rows_wide,
+    pass_sem,
+    load_sem,
+    store_sem,
+):
+    block = sizes[-1]
+    through = pltpu.make_async_copy(cols, cols_kept, pass_sem.at[0])
+    onward = pltpu.make_async_copy(cols_kept, out_cols, pass_sem.at[1])
+    moves = []
+    for index in range(cols.shape[0]):
+        moves.append(
+            (grad_cols.at[index], cols_low.at[index], cols_wide.at[index], out_grad_cols.at[index])
+        )
+    start = 0
+    for size, goal in zip(sizes, (goal0, goal1, goal2, goal3), strict=True):
+        for at in range(0, size, block):
+            here = slice(start + at, start + at + block)
+            moves.append(
+                (total.at[here], rows_low.at[here], rows_wide.at[here], goal.at[at : at + block])
+            )
+        start += size
+    loads = [
+        pltpu.make_async_copy(source, low, load_sem.at[index])
+        for index, (source, low, _, _) in enumerate(moves)
+    ]
+    stores = [
+        pltpu.make_async_copy(wide, goal, store_sem.at[index])
+        for index, (_, _, wide, goal) in enumerate(moves)
+    ]
+    for item in loads:
+        item.start()
+    through.start()
+    for index, goal in enumerate((gain1, bias1, gain2, bias2)):
         goal[...] = lines[index : index + 1]
+    out_bias[...] = lines[5:6]
+    out_bias_again[...] = lines[5:6]
+    fc1_bias[...] = lines[6:7]
     line = lines[4:5]
     lanes = line.shape[1] // 3
     pieces = []
     for h in range(heads):
         for part_index in range(3):
-            start = part_index * lanes + h * HEAD
-            pieces.append(line[:, start : start + HEAD])
-    goals[10][...] = jnp.concatenate(pieces, axis=1)
+            at = part_index * lanes + h * HEAD
+            pieces.append(line[:, at : at + HEAD])
+    qkv_bias[...] = jnp.concatenate(pieces, axis=1)
+    for load, store, (_, low, wide, _) in zip(loads, stores, moves, strict=True):
+        load.wait()
+        wide[...] = low[...].astype(F32)
+        store.start()
+    through.wait()
+    onward.start()
+    for item in stores:
+        item.wait()
+    onward.wait()
 
 
 def widen(out_cols, grad_cols, total, lines, heads, units):
-    steps = 6
-    count, columns, seq_len = out_cols.shape
     width = total.shape[1]
     sizes = (width, units, 3 * heads * HEAD, heads * HEAD)
-    starts = [0, *np.cumsum(sizes[:-1]).tolist()]
-    col_spec = pl.BlockSpec((count, columns // steps, seq_len), lambda i: (0, i, 0))
-
-    def rows_from(start, size):
-        block = size // steps
-        return pl.BlockSpec((block, width), lambda i: (start // block + i, 0))
-
-    def line_spec(lanes):
-        return pl.BlockSpec((1, lanes), lambda i: (0, 0))
-
+    count = out_cols.shape[0] + sum(sizes) // sizes[-1]
+    hbm = pl.BlockSpec(memory_space=pl.ANY)
+    vmem = pl.BlockSpec(memory_space=pltpu.VMEM)
     line = jax.ShapeDtypeStruct((1, width), F32)
     return pl.pallas_call(
-        functools.partial(widen_kernel, heads),
-        grid=(steps,),
-        in_specs=[col_spec, col_spec]
-        + [rows_from(start, size) for start, size in zip(starts, sizes, strict=True)]
-        + [pl.BlockSpec(lines.shape, lambda i: (0, 0))],
-        out_specs=[col_spec, col_spec]
-        + [rows_from(0, size) for size in sizes]
-        + [line_spec(width)] * 6
-        + [line_spec(sizes[2])],
+        functools.partial(widen_kernel, heads, sizes),
+        in_specs=[hbm, hbm, hbm, vmem],
+        out_specs=[hbm] * 6 + [vmem] * 8,
         out_shape=[
             jax.ShapeDtypeStruct(out_cols.shape, BF16),
             jax.ShapeDtypeStruct(out_cols.shape, F32),
         ]
         + [jax.ShapeDtypeStruct((size, width), F32) for size in sizes]
-        + [line] * 6
+        + [line] * 7
         + [jax.ShapeDtypeStruct((1, sizes[2]), F32)],
-    )(out_cols, grad_cols, total, total, total, total, lines)
+        scratch_shapes=[
+            pltpu.VMEM(out_cols.shape, BF16),
+            pltpu.VMEM(out_cols.shape, BF16),
+            pltpu.VMEM(out_cols.shape, F32),
+            pltpu.VMEM(total.shape, BF16),
+            pltpu.VMEM(total.shape, F32),
+            pltpu.SemaphoreType.DMA((2,)),
+            pltpu.SemaphoreType.DMA((count,)),
+            pltpu.SemaphoreType.DMA((count,)),
+        ],
+        compiler_params=pltpu.CompilerParams(vmem_limit_bytes=60 * 2**20),
+    )(out_cols, grad_cols, total, lines)
 
 
 def per_device(
@@ -1162,7 +1220,7 @@
     out_cols, grad_cols, fc1_grad, fc2_grad, qkv_grad, dense_grad, *lines = widen(
         out_cols, grad_cols, total, lines, heads, units
     )
-    gain1, bias1, gain2, bias2, out_bias, fc1_bias_grad, qkv_bias_grad = lines
+    gain1, bias1, gain2, bias2, dense_bias_grad, fc2_bias_grad, fc1_bias_grad, qkv_bias_grad = lines
     return (
         out_cols.transpose(0, 2, 1)[None],
         grad_cols.transpose(0, 2, 1)[None],
@@ -1173,11 +1231,11 @@
         qkv_grad.T[None],
         qkv_bias_grad,
         dense_grad[None],
-        out_bias,
+        dense_bias_grad,
         fc1_grad[None],
         fc1_bias_grad,
         fc2_grad[None],
-        out_bias,
+        fc2_bias_grad,
     )
 
 

time: 165 us -> 162 us (0.982)
  no operation moved by 1% of the time
where the time goes in v5:
time: 162 us
  Pallas kernels  161 us (99%)
    pallas_call x1, Pallas kernels, train(): pl.pallas_call(body, out_shape=(jax.ShapeDtypeStruct((count, columns, seq...  155 us
    pallas_call x1, Pallas kernels, widen(): pl.pallas_call(functools.partial(widen_kernel, heads, sizes), in_specs=[h...  6.27 us

profile of v5, /device:TPU:0, one launch (start us, length us, event | category | flops | bytes accessed | tf_op | source)
XLA Modules:
  0.0 162.2 jit_solution(17187298613253016846)
XLA Ops:
  0.7 155.1 %shard_map.263 = (bf16[2,192,1024]{2,1,0:T(8,128)(2,1)}, bf16[2,192,1024]{2,1,0:T(8,128)(2,1)}, bf16[2304,768]{1,0:T(8,128)(2,1)}, f32[8,768]{1,0:T(8,128)}) custom-call(bf16[2,4,256,768]{3,2,1,0:T(8,128)(2,1)} %bitcast.20, bf16[2,4,256,768]{3,2,1,0:T(8,128)(2,1)} %bitcast.21, s32[2]{0:T(128)} %refs_2_.1, f32[2,1024,128]{2,1,0:T(8,128)} %constant.2.clone.refs_3_, ...), custom_call_target="tpu_custom_call" | custom-call | tf_op jit(solution)/shard_map/pallas_call | solution.py:1057
  155.8 6.3 %shard_map.264 = (bf16[2,192,1024]{2,1,0:T(8,128)(2,1)}, f32[2,192,1024]{2,1,0:T(8,128)}, f32[768,768]{1,0:T(8,128)}, f32[768,768]{1,0:T(8,128)}, f32[576,768]{1...) custom-call(bf16[2,192,1024]{2,1,0:T(8,128)(2,1)} %get-tuple-element, ...), custom_call_target="tpu_custom_call" | custom-call | tf_op jit(solution)/shard_map/pallas_call | solution.py:1173

commit v6 on v5

--- a/solution.py
+++ b/solution.py
@@ -403,17 +403,18 @@
         before = jnp.where(first_turn, 0.0, total[layer, goal].astype(F32))
         total[layer, goal] = (piece + before).astype(BF16)
 
-    def add_forward_grads(layer, c, first_turn):
+    def add_forward_grads(layer, c, first_turn, parts=("fc1", "fc2")):
         here = rows_of(c)
         cotangent = chain.at[3 - layer, c]
 
         def add_block(index, carry):
             block = pl.ds(pl.multiple_of(index * lanes, lanes), lanes)
             goal = pl.ds(pl.multiple_of(width + index * lanes, lanes), lanes)
-            pieces = (
-                (block, dot_tn(norm_rows[:, block], gate[layer, here])),
-                (goal, dot_tn(act[layer, here, block], cotangent[...])),
-            )
+            pieces = []
+            if "fc1" in parts:
+                pieces.append((block, dot_tn(norm_rows[:, block], gate[layer, here])))
+            if "fc2" in parts:
+                pieces.append((goal, dot_tn(act[layer, here, block], cotangent[...])))
             for at, piece in pieces:
                 before = jnp.where(first_turn, 0.0, total[layer, at].astype(F32))
                 total[layer, at] = (piece + before).astype(BF16)
@@ -435,7 +436,7 @@
         add_piece_grads(layer, base + 3 * valid, piece, first_turn)
 
     cut = width + act.shape[-1]
-    jobs = ((0, cut), (cut, total.shape[1] - cut))
+    jobs = ((width, cut - width), (0, width), (cut, total.shape[1] - cut))
     folds = min(bits, 2)
     sum_steps = 2 + 2 * folds + (bits - folds)
 
@@ -452,7 +453,7 @@
             start = start + upper * size
         return steps, start, size
 
-    groups = [[spans(job, group) for group in range(2)] for job in range(2)]
+    groups = [[spans(job, group) for group in range(2)] for job in range(len(jobs))]
 
     def sums_of(layer, start, size):
         return total.at[layer, pl.ds(pl.multiple_of(start, 16), size)]
@@ -570,7 +571,7 @@
                     device_id_type=MESH,
                 )
 
-    steps_done = {(layer, job): 0 for layer in range(2) for job in range(2)}
+    steps_done = {(layer, job): 0 for layer in range(2) for job in range(len(jobs))}
 
     def move_sum(layer, job, step=None):
         step = steps_done[layer, job] if step is None else step
@@ -643,10 +644,10 @@
 
         lax.fori_loop(0, count // step, turn_rows, 0)
 
-    def launch(kind, c):
+    def launch(kind, c, parts=(0, 1)):
         @pl.when(outer)
         def _():
-            for half in range(halves):
+            for half in parts:
                 first_hop(kind, c * halves + half).start()
 
     def meet(kind, u):
@@ -765,6 +766,8 @@
                 serve(0, *second_turns[c][0])
                 if c in (1, 2):
                     launch(1, c - 1)
+                if c == 2:
+                    launch(1, 2, (0,))
                 if c == 0:
                     find_share()
                 weigh(c)
@@ -775,8 +778,8 @@
 
     lax.fori_loop(0, 2, forward_layer, 0)
 
-    meets = {1: (1, 1, 3, 3), 2: (4, 5, 6, 7, 8, 9, 10, 11), 3: (13,)}
-    settles = {1: (3, 3, 5, 5), 2: (6, 7, 8, 9, 10, 11, 12, 12), 3: ()}
+    meets = {1: (1, 1, 3, 3, 5), 2: (4, 5, 6, 7, 8, 9, 10, 11), 3: (13, 14, 14)}
+    settles = {1: (3, 3, 5, 5, 7), 2: (6, 7, 8, 9, 10, 11, 12, 12), 3: (14,)}
     backward_points = [[] for _ in range(8 * 2)]
     for kind in (1, 2, 3):
         order = [(2 * u, meet, kind, u, meets[kind][u]) for u in range(len(meets[kind]))]
@@ -789,12 +792,13 @@
             work(kind, u)
 
     sum_moves = {
-        5: ((0, 0),),
-        8: ((1, 0),),
-        9: ((0, 2),),
-        10: ((1, 1),),
-        11: ((1, 2), (0, 3)),
-        12: ((1, 3),),
+        5: ((1, 0, 0), (1, 1, 0)),
+        8: ((1, 2, 0),),
+        9: ((1, 0, 2), (1, 1, 2)),
+        10: ((1, 2, 1),),
+        12: ((1, 2, 2), (1, 0, 3), (1, 1, 3)),
+        13: ((1, 2, 3),),
+        14: ((0, 0, 0),),
     }
 
     def serve_at(step, point):
@@ -804,8 +808,8 @@
             @pl.when(step == index)
             def _():
                 serve_point(number)
-                for job, end in sum_moves.get(number, ()):
-                    move_sum(1, job, end)
+                for moved in sum_moves.get(number, ()):
+                    move_sum(*moved)
 
     def backward_step(step, carry):
         turn_index = step // chunks
@@ -816,19 +820,30 @@
 
         @pl.when(layer == 0)
         def _():
-            pl.when(at == 0)(functools.partial(move_sum, 1, 0, 1))
+
+            @pl.when(at == 0)
+            def _():
+                move_sum(1, 0, 1)
+                move_sum(1, 1, 1)
+
             arrive(2, at)
             release(2, at)
 
         pl.when(layer == 1)(functools.partial(release, 0, at))
+
+        @pl.when(last_step)
+        def _():
+            add_forward_grads(0, 0, False, ("fc2",))
+            sum_start(0, 0, 0)
+
         backward_front(layer, c)
 
         @pl.when(last_step)
         def _():
             spread, _ = normalise(chain[0, 0].astype(F32))
             norm_rows[...] = (spread * vec[0, 2:3] + vec[0, 3:4]).astype(BF16)
-            add_forward_grads(0, 0, False)
-            sum_start(0, 0, 0)
+            add_forward_grads(0, 0, False, ("fc1",))
+            sum_start(0, 1, 0)
 
         for index in range(chunks):
             pl.when(c == index)(functools.partial(backward_attention, layer, index))
@@ -836,7 +851,7 @@
         first = backward_rest(layer, c)
         for index in range(2):
             pl.when(turn_index == index)(functools.partial(launch, 2 + index, at))
-        pl.when(last_step)(functools.partial(move_sum, 0, 0))
+        pl.when(last_step)(functools.partial(move_sum, 0, 1))
         add_weight_grads(layer, c, first)
 
         @pl.when(jnp.logical_or(step == 0, jnp.logical_and(layer == 0, c > 0)))
@@ -846,13 +861,15 @@
         @pl.when(step == 0)
         def _():
             sum_start(1, 0, 0)
+            sum_start(1, 1, 0)
 
         @pl.when(jnp.logical_and(layer == 0, at > 1))
         def _():
-            launch(1, at)
-
-        pl.when(step == chunks - 1)(functools.partial(sum_start, 1, 1, 0))
-        pl.when(last_step)(functools.partial(sum_start, 0, 1, 0))
+            pl.when(at == 2)(functools.partial(launch, 1, 2, (1,)))
+            pl.when(at == 3)(functools.partial(launch, 1, 3))
+
+        pl.when(step == chunks - 1)(functools.partial(sum_start, 1, 2, 0))
+        pl.when(last_step)(functools.partial(sum_start, 0, 2, 0))
         serve_at(step, 1)
         return carry
 
@@ -922,55 +939,59 @@
     line_copy(0).start()
     for item in gifts[1:]:
         item.wait_send()
-    serve(3, (1, 2), (0,))
-    move_sum(0, 1)
+    meet(3, 3)
     settle(3, 1)
+    meet(3, 4)
+    move_sum(0, 2)
+    settle(3, 2)
+    meet(3, 5)
+    settle(3, 3)
     line_next(0)
     stage_whole(0, 0, 0)
-    serve(3, (3, 4), (2, 3))
-    stage_whole(1, 1, 2)
-    meet(3, 5)
-    move_sum(1, 0)
+    meet(1, 5)
     settle(3, 4)
-    meet(1, 4)
     move_sum(0, 0)
     settle(3, 5)
-    meet(1, 5)
+    meet(3, 6)
     move_sum(0, 1)
+    stage_whole(1, 1, 2)
+    settle(1, 5)
+    for job in range(2):
+        move_sum(1, job)
+    move_sum(0, 2)
     line_next(1)
-    settle(1, 4)
-    meet(3, 6)
+    meet(3, 7)
+    settle(3, 6)
     move_sum(0, 0)
-    settle(1, 5)
-    meet(3, 7)
+    meet(1, 6)
+    settle(3, 7)
     move_sum(0, 1)
+    move_sum(0, 2)
     line_next(2)
-    settle(3, 6)
-    meet(1, 6)
+    meet(1, 7)
     move_sum(0, 0)
-    settle(3, 7)
-    meet(1, 7)
+    settle(1, 6)
     move_sum(0, 1)
+    settle(1, 7)
+    move_sum(0, 2)
     line_next(3)
+    move_sum(1, 2)
     stage_own(1, 0, 3)
     moves = swap_columns(1, grad_cols)
     for item in moves:
         item.start()
-    settle(1, 6)
-    settle(1, 7)
-    move_sum(1, 1)
+    stage_own(0, 1, 1)
+    late_moves = swap_columns(0, out_cols)
+    for item in late_moves:
+        item.start()
     move_sum(0, 0)
+    move_sum(0, 1)
     for step in range(4, len(line_friends)):
         line_next(step)
     lines_store = pltpu.make_async_copy(small.at[section], lines, load_sem.at[0])
     lines_store.start()
-    move_sum(0, 1)
-    stage_own(0, 1, 1)
-    late_moves = swap_columns(0, out_cols)
-    for item in late_moves:
-        item.start()
     for _ in range(sum_steps):
-        for job in range(2):
+        for job in range(len(jobs)):
             move_sum(0, job)
             move_sum(1, job)
     for item in moves + late_moves:
@@ -1037,14 +1058,14 @@
         pltpu.SemaphoreType.DMA((2, 3, pieces)),
         pltpu.SemaphoreType.DMA((2,)),
         pltpu.SemaphoreType.DMA((2,)),
-        pltpu.SemaphoreType.DMA((2, 2, bits + 4, 2)),
-        pltpu.SemaphoreType.DMA((2, 2, bits + 4, 2)),
+        pltpu.SemaphoreType.DMA((2, 3, bits + 4, 2)),
+        pltpu.SemaphoreType.DMA((2, 3, bits + 4, 2)),
         pltpu.SemaphoreType.DMA((3 + bits,)),
         pltpu.SemaphoreType.DMA((3 + bits,)),
         pltpu.SemaphoreType.DMA((max(bits, 1),)),
         pltpu.SemaphoreType.DMA((max(bits, 1),)),
-        pltpu.SemaphoreType.DMA((2, 2)),
-        pltpu.SemaphoreType.REGULAR((2, 2, 2)),
+        pltpu.SemaphoreType.DMA((3, 2)),
+        pltpu.SemaphoreType.REGULAR((3, 2, 2)),
     ]
 
     def body(*refs):

time: 162 us -> 162 us (level)
  no operation moved by 1% of the time
where the time goes in v6:
time: 162 us; the launch traced here: 161 us
  Pallas kernels  160 us (99%)
    pallas_call x1, Pallas kernels, train(): pl.pallas_call(body, out_shape=(jax.ShapeDtypeStruct((count, columns, seq...  154 us
    pallas_call x1, Pallas kernels, widen(): pl.pallas_call(functools.partial(widen_kernel, heads, sizes), in_specs=[h...  6.27 us

profile of v6, /device:TPU:0, one launch (start us, length us, event | category | flops | bytes accessed | tf_op | source)
XLA Modules:
  0.0 161.0 jit_solution(3235226051611907010)
XLA Ops:
  0.7 153.9 %shard_map.263 = (bf16[2,192,1024]{2,1,0:T(8,128)(2,1)}, bf16[2,192,1024]{2,1,0:T(8,128)(2,1)}, bf16[2304,768]{1,0:T(8,128)(2,1)}, f32[8,768]{1,0:T(8,128)}) custom-call(bf16[2,4,256,768]{3,2,1,0:T(8,128)(2,1)} %bitcast.20, bf16[2,4,256,768]{3,2,1,0:T(8,128)(2,1)} %bitcast.21, s32[2]{0:T(128)} %refs_2_.1, f32[2,1024,128]{2,1,0:T(8,128)} %constant.2.clone.refs_3_, ...), custom_call_target="tpu_custom_call" | custom-call | tf_op jit(solution)/shard_map/pallas_call | solution.py:1078
  154.5 6.3 %shard_map.264 = (bf16[2,192,1024]{2,1,0:T(8,128)(2,1)}, f32[2,192,1024]{2,1,0:T(8,128)}, f32[768,768]{1,0:T(8,128)}, f32[768,768]{1,0:T(8,128)}, f32[576,768]{1...) custom-call(bf16[2,192,1024]{2,1,0:T(8,128)(2,1)} %get-tuple-element, ...), custom_call_target="tpu_custom_call" | custom-call | tf_op jit(solution)/shard_map/pallas_call | solution.py:1194

commit v7 on v6

--- a/solution.py
+++ b/solution.py
@@ -160,12 +160,7 @@
 
     input_load = pltpu.make_async_copy(x_in.at[section], chain.at[0], load_sem.at[0])
     input_load.start()
-    pairs = []
-    for part_index in range(3):
-        for h in range(heads):
-            source = slice((3 * h + part_index) * HEAD, (3 * h + part_index + 1) * HEAD)
-            goal = slice(part_index * lanes + h * HEAD, part_index * lanes + (h + 1) * HEAD)
-            pairs.append((wq_in.at[source], wq.at[section, goal]))
+    pairs = [(wq_in.at[:, index], wq.at[section, index, :heads]) for index in range(3)]
     pairs += [(w1_in, w1.at[section]), (wd_in, wd.at[section, :valid]), (w2_in, w2.at[section])]
     loads = [
         pltpu.make_async_copy(source, goal, load_sem.at[4 + index])
@@ -190,9 +185,7 @@
     vec[section, 7:8] = jnp.zeros((1, width), F32)
     for layer in range(2):
         wd[layer, valid:] = jnp.zeros((lanes - valid, width), BF16)
-        for part_index in range(3):
-            pad = slice(part_index * lanes + valid, (part_index + 1) * lanes)
-            wq[layer, pad] = jnp.zeros((lanes - valid, width), BF16)
+        wq[layer, :, heads:] = jnp.zeros((3, lanes // HEAD - heads, HEAD, width), BF16)
     pl.semaphore_wait(barrier, len(friends))
     gifts = [
         send(source, goal, (give_sem.at[index], take_sem.at[index]), twin)
@@ -200,7 +193,7 @@
             [(vec.at[section], vec.at[section])] + pairs
         )
     ]
-    projection = 3 * heads
+    projection = 3
     for item in gifts[: 2 + projection]:
         item.start()
 
@@ -211,7 +204,7 @@
 
     def tally_step(bit):
         return send(
-            tally, tally_got.at[bit], (tally_send.at[bit], tally_recv.at[bit]), mates[bit]
+            tally, tally_got.at[bit], (tally_send.at[0], tally_recv.at[bit]), mates[bit]
         )
 
     if bits:
@@ -263,7 +256,7 @@
         spread, _ = normalise(chain[layer, c].astype(F32))
         first = (spread * vec[layer, 0:1] + vec[layer, 1:2]).astype(BF16)
         second = (spread * vec[layer, 2:3] + vec[layer, 3:4]).astype(BF16)
-        projected = dot_nt(first, wq[layer]) + vec[layer, 5:6]
+        projected = dot_nt(first, wq[layer].reshape(3 * lanes, width)) + vec[layer, 5:6]
         query = turn(projected[:, :lanes], start).astype(BF16)
         qkv[layer, here, :lanes] = query
         qkv[layer, here, lanes : 2 * lanes] = turn(projected[:, lanes : 2 * lanes], start).astype(
@@ -377,7 +370,7 @@
         qkv[layer, here, lanes : 2 * lanes] = turn_back(key_grad[here], start).astype(BF16)
         qkv[layer, here, 2 * lanes :] = value_grad[here].astype(BF16)
         projected_grad = qkv[layer, here, :]
-        first_back = dot_nn(projected_grad, wq[layer])
+        first_back = dot_nn(projected_grad, wq[layer].reshape(3 * lanes, width))
         spread, rstd = normalise(chain[layer, c].astype(F32))
         back = first_back * vec[layer, 0:1] + second_back * vec[layer, 2:3]
         middle = jnp.mean(back, axis=-1, keepdims=True)
@@ -464,7 +457,7 @@
         return (act, gate)[group].at[layer, pl.ds(pl.multiple_of(start, 16), size)]
 
     def sum_sems(layer, job, step, group):
-        return sum_send.at[layer, job, step, group], sum_recv.at[layer, job, step, group]
+        return sum_send.at[layer, job, group], sum_recv.at[layer, job, step, group]
 
     def landing_of(buffer, job, parts):
         base, job_rows = jobs[job]
@@ -516,8 +509,7 @@
     def sum_start(layer, job, step):
         if step < sum_steps - 1:
             if layer == 0 and 1 <= step <= folds:
-                for group in range(2):
-                    pl.semaphore_wait(free_sem.at[job, step - 1, group], 1)
+                pl.semaphore_wait(free_sem.at[job, step - 1], 2)
             for item in sum_copies(layer, job, step):
                 item.start()
             return
@@ -565,7 +557,7 @@
             if layer == 1 and step <= folds:
                 mate = mates[steps[step - 1][0]]
                 pl.semaphore_signal(
-                    free_sem.at[job, step - 1, group],
+                    free_sem.at[job, step - 1],
                     inc=1,
                     device_id=mate,
                     device_id_type=MESH,
@@ -584,7 +576,7 @@
     line_friends = [twin] + mates + [near, far]
 
     def line_copy(step):
-        sems = (line_send.at[step], line_recv.at[step])
+        sems = (line_send.at[0], line_recv.at[step])
         return send(small, line_got.at[step], sems, line_friends[step])
 
     def line_end(step):
@@ -614,7 +606,8 @@
         return part.at[u], got.at[u], met.at[u] if kind != 3 else met.at[u, :, :half_width]
 
     def hop_sems(kind, stage, u):
-        return hop_send.at[int(kind == 1), stage, u], hop_recv.at[int(kind == 1), stage, u]
+        late = int(kind == 1)
+        return hop_send.at[late, (0, 0, 1)[stage], u], hop_recv.at[late, (0, 1, 0)[stage], u]
 
     def first_hop(kind, u):
         own, landing, _ = buffers(kind, u)
@@ -796,7 +789,8 @@
         8: ((1, 2, 0),),
         9: ((1, 0, 2), (1, 1, 2)),
         10: ((1, 2, 1),),
-        12: ((1, 2, 2), (1, 0, 3), (1, 1, 3)),
+        11: ((1, 2, 2),),
+        12: ((1, 0, 3), (1, 1, 3)),
         13: ((1, 2, 3),),
         14: ((0, 0, 0),),
     }
@@ -947,39 +941,39 @@
     meet(3, 5)
     settle(3, 3)
     line_next(0)
-    stage_whole(0, 0, 0)
+    move_sum(0, 0)
     meet(1, 5)
     settle(3, 4)
-    move_sum(0, 0)
+    move_sum(0, 1)
     settle(3, 5)
     meet(3, 6)
-    move_sum(0, 1)
-    stage_whole(1, 1, 2)
     settle(1, 5)
     for job in range(2):
         move_sum(1, job)
     move_sum(0, 2)
-    line_next(1)
+    stage_whole(0, 0, 0)
     meet(3, 7)
     settle(3, 6)
     move_sum(0, 0)
+    move_sum(0, 1)
+    line_next(1)
     meet(1, 6)
     settle(3, 7)
-    move_sum(0, 1)
     move_sum(0, 2)
-    line_next(2)
+    stage_whole(1, 1, 2)
     meet(1, 7)
     move_sum(0, 0)
     settle(1, 6)
     move_sum(0, 1)
+    line_next(2)
     settle(1, 7)
     move_sum(0, 2)
-    line_next(3)
     move_sum(1, 2)
     stage_own(1, 0, 3)
     moves = swap_columns(1, grad_cols)
     for item in moves:
         item.start()
+    line_next(3)
     stage_own(0, 1, 1)
     late_moves = swap_columns(0, out_cols)
     for item in late_moves:
@@ -1019,7 +1013,7 @@
     smem = pl.BlockSpec(memory_space=pltpu.SMEM)
     scratch = [
         pltpu.VMEM((2, 8, width), F32),
-        pltpu.VMEM((2, 3 * lanes, width), BF16),
+        pltpu.VMEM((2, 3, lanes // HEAD, HEAD, width), BF16),
         pltpu.VMEM((2, lanes, width), BF16),
         pltpu.VMEM((2,) + w1.shape, BF16),
         pltpu.VMEM((2,) + w2.shape, BF16),
@@ -1051,21 +1045,21 @@
     ]
     probs = [pltpu.VMEM((2, heads, rows, (c + 1) * rows), BF16) for c in range(chunks)]
     semaphores = [
-        pltpu.SemaphoreType.DMA((4 + 3 * heads + 3,)),
-        pltpu.SemaphoreType.DMA((4 + 3 * heads,)),
-        pltpu.SemaphoreType.DMA((4 + 3 * heads,)),
-        pltpu.SemaphoreType.DMA((2, 3, pieces)),
-        pltpu.SemaphoreType.DMA((2, 3, pieces)),
+        pltpu.SemaphoreType.DMA((10,)),
+        pltpu.SemaphoreType.DMA((7,)),
+        pltpu.SemaphoreType.DMA((7,)),
+        pltpu.SemaphoreType.DMA((2, 2, pieces)),
+        pltpu.SemaphoreType.DMA((2, 2, pieces)),
         pltpu.SemaphoreType.DMA((2,)),
         pltpu.SemaphoreType.DMA((2,)),
+        pltpu.SemaphoreType.DMA((2, 3, 2)),
         pltpu.SemaphoreType.DMA((2, 3, bits + 4, 2)),
-        pltpu.SemaphoreType.DMA((2, 3, bits + 4, 2)),
+        pltpu.SemaphoreType.DMA((1,)),
         pltpu.SemaphoreType.DMA((3 + bits,)),
-        pltpu.SemaphoreType.DMA((3 + bits,)),
-        pltpu.SemaphoreType.DMA((max(bits, 1),)),
+        pltpu.SemaphoreType.DMA((1,)),
         pltpu.SemaphoreType.DMA((max(bits, 1),)),
         pltpu.SemaphoreType.DMA((3, 2)),
-        pltpu.SemaphoreType.REGULAR((3, 2, 2)),
+        pltpu.SemaphoreType.REGULAR((3, 2)),
     ]
 
     def body(*refs):
@@ -1094,7 +1088,7 @@
         target.reshape(count, chunks, rows, width),
         tissue,
         tables,
-        wq,
+        wq.reshape(heads, 3, HEAD, width),
         wd,
         w1,
         w2,

time: 162 us -> 162 us (level)
  no operation moved by 1% of the time
where the time goes in v7:
time: 162 us; the launch traced here: 161 us
  Pallas kernels  161 us (99%)
    pallas_call x1, Pallas kernels, train(): pl.pallas_call(body, out_shape=(jax.ShapeDtypeStruct((count, columns, seq...  154 us
    pallas_call x1, Pallas kernels, widen(): pl.pallas_call(functools.partial(widen_kernel, heads, sizes), in_specs=[h...  6.27 us

profile of v7, /device:TPU:0, one launch (start us, length us, event | category | flops | bytes accessed | tf_op | source)
XLA Modules:
  0.0 161.4 jit_solution(4017040426032074144)
XLA Ops:
  0.7 154.3 %shard_map.263 = (bf16[2,192,1024]{2,1,0:T(8,128)(2,1)}, bf16[2,192,1024]{2,1,0:T(8,128)(2,1)}, bf16[2304,768]{1,0:T(8,128)(2,1)}, f32[8,768]{1,0:T(8,128)}) custom-call(bf16[2,4,256,768]{3,2,1,0:T(8,128)(2,1)} %bitcast.22, bf16[2,4,256,768]{3,2,1,0:T(8,128)(2,1)} %bitcast.23, s32[2]{0:T(128)} %refs_2_.1, f32[2,1024,128]{2,1,0:T(8,128)} %constant.2.clone.refs_3_, ...), custom_call_target="tpu_custom_call" | custom-call | tf_op jit(solution)/shard_map/pallas_call | solution.py:1072
  154.9 6.3 %shard_map.264 = (bf16[2,192,1024]{2,1,0:T(8,128)(2,1)}, f32[2,192,1024]{2,1,0:T(8,128)}, f32[768,768]{1,0:T(8,128)}, f32[768,768]{1,0:T(8,128)}, f32[576,768]{1...) custom-call(bf16[2,192,1024]{2,1,0:T(8,128)(2,1)} %get-tuple-element, ...), custom_call_target="tpu_custom_call" | custom-call | tf_op jit(solution)/shard_map/pallas_call | solution.py:1188

commit v8 on v7

--- a/solution.py
+++ b/solution.py
@@ -789,8 +789,7 @@
         8: ((1, 2, 0),),
         9: ((1, 0, 2), (1, 1, 2)),
         10: ((1, 2, 1),),
-        11: ((1, 2, 2),),
-        12: ((1, 0, 3), (1, 1, 3)),
+        12: ((1, 2, 2), (1, 0, 3), (1, 1, 3)),
         13: ((1, 2, 3),),
         14: ((0, 0, 0),),
     }
@@ -941,39 +940,39 @@
     meet(3, 5)
     settle(3, 3)
     line_next(0)
-    move_sum(0, 0)
+    stage_whole(0, 0, 0)
     meet(1, 5)
     settle(3, 4)
-    move_sum(0, 1)
+    move_sum(0, 0)
     settle(3, 5)
     meet(3, 6)
+    move_sum(0, 1)
+    stage_whole(1, 1, 2)
     settle(1, 5)
     for job in range(2):
         move_sum(1, job)
     move_sum(0, 2)
-    stage_whole(0, 0, 0)
+    line_next(1)
     meet(3, 7)
     settle(3, 6)
     move_sum(0, 0)
-    move_sum(0, 1)
-    line_next(1)
     meet(1, 6)
     settle(3, 7)
+    move_sum(0, 1)
     move_sum(0, 2)
-    stage_whole(1, 1, 2)
+    line_next(2)
     meet(1, 7)
     move_sum(0, 0)
     settle(1, 6)
     move_sum(0, 1)
-    line_next(2)
     settle(1, 7)
     move_sum(0, 2)
+    line_next(3)
     move_sum(1, 2)
     stage_own(1, 0, 3)
     moves = swap_columns(1, grad_cols)
     for item in moves:
         item.start()
-    line_next(3)
     stage_own(0, 1, 1)
     late_moves = swap_columns(0, out_cols)
     for item in late_moves:

time: 162 us -> 161 us (level)
  no operation moved by 1% of the time
where the time goes in v8:
time: 161 us
  Pallas kernels  160 us (99%)
    pallas_call x1, Pallas kernels, train(): pl.pallas_call(body, out_shape=(jax.ShapeDtypeStruct((count, columns, seq...  153 us
    pallas_call x1, Pallas kernels, widen(): pl.pallas_call(functools.partial(widen_kernel, heads, sizes), in_specs=[h...  6.27 us

profile of v8, /device:TPU:0, one launch (start us, length us, event | category | flops | bytes accessed | tf_op | source)
XLA Modules:
  0.0 160.5 jit_solution(9903069928175608406)
XLA Ops:
  0.7 153.4 %shard_map.263 = (bf16[2,192,1024]{2,1,0:T(8,128)(2,1)}, bf16[2,192,1024]{2,1,0:T(8,128)(2,1)}, bf16[2304,768]{1,0:T(8,128)(2,1)}, f32[8,768]{1,0:T(8,128)}) custom-call(bf16[2,4,256,768]{3,2,1,0:T(8,128)(2,1)} %bitcast.22, bf16[2,4,256,768]{3,2,1,0:T(8,128)(2,1)} %bitcast.23, s32[2]{0:T(128)} %refs_2_.1, f32[2,1024,128]{2,1,0:T(8,128)} %constant.2.clone.refs_3_, ...), custom_call_target="tpu_custom_call" | custom-call | tf_op jit(solution)/shard_map/pallas_call | solution.py:1071
  154.1 6.3 %shard_map.264 = (bf16[2,192,1024]{2,1,0:T(8,128)(2,1)}, f32[2,192,1024]{2,1,0:T(8,128)}, f32[768,768]{1,0:T(8,128)}, f32[768,768]{1,0:T(8,128)}, f32[576,768]{1...) custom-call(bf16[2,192,1024]{2,1,0:T(8,128)(2,1)} %get-tuple-element, ...), custom_call_target="tpu_custom_call" | custom-call | tf_op jit(solution)/shard_map/pallas_call | solution.py:1187

commit v9 on v8

--- a/solution.py
+++ b/solution.py
@@ -457,7 +457,11 @@
         return (act, gate)[group].at[layer, pl.ds(pl.multiple_of(start, 16), size)]
 
     def sum_sems(layer, job, step, group):
-        return sum_send.at[layer, job, group], sum_recv.at[layer, job, step, group]
+        if 1 <= step <= folds:
+            slot = step - 1
+        else:
+            slot = folds + layer + 2 * (step if step == 0 else step - folds)
+        return sum_send.at[layer, job, group], sum_recv.at[job, slot, group]
 
     def landing_of(buffer, job, parts):
         base, job_rows = jobs[job]
@@ -789,7 +793,8 @@
         8: ((1, 2, 0),),
         9: ((1, 0, 2), (1, 1, 2)),
         10: ((1, 2, 1),),
-        12: ((1, 2, 2), (1, 0, 3), (1, 1, 3)),
+        11: ((1, 2, 2),),
+        12: ((1, 0, 3), (1, 1, 3)),
         13: ((1, 2, 3),),
         14: ((0, 0, 0),),
     }
@@ -1052,7 +1057,7 @@
         pltpu.SemaphoreType.DMA((2,)),
         pltpu.SemaphoreType.DMA((2,)),
         pltpu.SemaphoreType.DMA((2, 3, 2)),
-        pltpu.SemaphoreType.DMA((2, 3, bits + 4, 2)),
+        pltpu.SemaphoreType.DMA((3, min(bits, 2) + 2 * (bits + 2), 2)),
         pltpu.SemaphoreType.DMA((1,)),
         pltpu.SemaphoreType.DMA((3 + bits,)),
         pltpu.SemaphoreType.DMA((1,)),

time: 161 us -> 161 us (level)
  no operation moved by 1% of the time
where the time goes in v9:
time: 161 us; the launch traced here: 160 us
  Pallas kernels  159 us (99%)
    pallas_call x1, Pallas kernels, train(): pl.pallas_call(body, out_shape=(jax.ShapeDtypeStruct((count, columns, seq...  153 us
    pallas_call x1, Pallas kernels, widen(): pl.pallas_call(functools.partial(widen_kernel, heads, sizes), in_specs=[h...  6.27 us

profile of v9, /device:TPU:0, one launch (start us, length us, event | category | flops | bytes accessed | tf_op | source)
XLA Modules:
  0.0 160.2 jit_solution(11534720822076690968)
XLA Ops:
  0.7 153.2 %shard_map.263 = (bf16[2,192,1024]{2,1,0:T(8,128)(2,1)}, bf16[2,192,1024]{2,1,0:T(8,128)(2,1)}, bf16[2304,768]{1,0:T(8,128)(2,1)}, f32[8,768]{1,0:T(8,128)}) custom-call(bf16[2,4,256,768]{3,2,1,0:T(8,128)(2,1)} %bitcast.22, bf16[2,4,256,768]{3,2,1,0:T(8,128)(2,1)} %bitcast.23, s32[2]{0:T(128)} %refs_2_.1, f32[2,1024,128]{2,1,0:T(8,128)} %constant.2.clone.refs_3_, ...), custom_call_target="tpu_custom_call" | custom-call | tf_op jit(solution)/shard_map/pallas_call | solution.py:1076
  153.8 6.3 %shard_map.264 = (bf16[2,192,1024]{2,1,0:T(8,128)(2,1)}, f32[2,192,1024]{2,1,0:T(8,128)}, f32[768,768]{1,0:T(8,128)}, f32[768,768]{1,0:T(8,128)}, f32[576,768]{1...) custom-call(bf16[2,192,1024]{2,1,0:T(8,128)(2,1)} %get-tuple-element, ...), custom_call_target="tpu_custom_call" | custom-call | tf_op jit(solution)/shard_map/pallas_call | solution.py:1192
